TPU v7x, 32 devices: a whole 2x2x4 slice. The times are simulated.
32 devices in a mesh: tm: 4 (over x, core), space: 8 (over z, y).
Axes of the slice: x: 2, y: 2, z: 4, core: 2. Of those that a mesh axis runs over, the one named last changes fastest.
Arguments:
- start_states: float32 [4, 128, 1024], P('tm', 'space'), may hold values from -6 to 6
- sigma: float32 [128, 1024], P('space'), may hold values from 0.05 to 5
- labels: int32 [128, 1024], P('space'), may hold values from 0 to 3
- nu_table: float32 [4], replicated, may hold values from 0.3 to 3
- coil: float32 [128, 1024], P('space'), may hold values from -6 to 6
- waveform: float32 [64], P('tm'), may hold values from -4 to 4
Outputs:
- end_states: float32 [4, 128, 1024], P('tm', 'space')
- traces_out: float32 [64, 8192], P('tm', 'space')
All inputs are finite; a program needn't handle non-finite values.
Results may differ from a plain program's by a relative error of at most 0.000026.
Values sent between devices are 32-bit elements; how exact they have to be, the bound alone decides.
No kernel may reach another device: no remote copies, remote signals or barrier semaphores. Data moves between devices by JAX's collectives and lax.ppermute only.
A program may use at most 64 MiB of HBM per device.

v0:
```python
import jax
import jax.numpy as jnp
from jax import lax
from jax.sharding import PartitionSpec as P

JACOBI = 8
SWEEPS = 2


THETA = 0.25


def passed_along(array, axis, by):
    peers = lax.axis_size(axis)
    pairs = [(i, i + by) for i in range(peers) if 0 <= i + by < peers]
    return lax.ppermute(array, axis, pairs)


def from_behind(value, axis, steps):
    count = lax.axis_size(axis)
    pairs = [(source, (source + steps) % count) for source in range(count)]
    return lax.ppermute(value, axis, pairs)


def shifted(field, axis, low, high):
    config = [(0, 0, 0)] * field.ndim
    config[axis % field.ndim] = (low, high, 0)
    return lax.pad(field, jnp.zeros((), field.dtype), config)


def next_column(field):
    return shifted(field, -2, -1, 1)


def prev_column(field):
    return shifted(field, -2, 1, -1)


def next_row(field):
    return shifted(field, -1, -1, 1)


def prev_row(field):
    return shifted(field, -1, 1, -1)


def harmonic(first_nu, second_nu):
    return 2.0 * first_nu * second_nu / (first_nu + second_nu)


def reluctivity(labels, nu_table):
    result = jnp.zeros(labels.shape, jnp.float32)
    for material in range(nu_table.shape[0]):
        result = result + jnp.where(labels == material, nu_table[material], jnp.float32(0.0))
    return result


def coefficients(sigma, nu, first, last):
    kxp = harmonic(nu, next_column(nu))
    kxm = harmonic(nu, prev_column(nu))
    kyp = harmonic(nu, next_row(nu))
    kym = harmonic(nu, prev_row(nu))
    rows = jnp.arange(nu.shape[-1])
    edge_rows = ((rows == 0) | (rows == nu.shape[-1] - 1)).astype(jnp.float32)
    inner = sigma + kxp + kxm + kyp + kym + 2.0 * nu * edge_rows
    left_coef = 2.0 * nu[..., 0, :]
    right_coef = 2.0 * nu[..., -1, :]
    cols = jnp.arange(nu.shape[-2])[:, None]
    at_left = (cols == 0).astype(jnp.float32)
    at_right = (cols == nu.shape[-2] - 1).astype(jnp.float32)
    d_dir = inner + at_left * left_coef[..., None, :] + at_right * right_coef[..., None, :]
    d_neu = (
        inner
        + at_left * (first * left_coef)[..., None, :]
        + at_right * (last * right_coef)[..., None, :]
    )
    return ((sigma, kxp, kxm, kyp, kym), left_coef, right_coef, d_dir, d_neu)


def march(start, couple, diag, coil, waves, left_term, right_term):
    sigma, kxp, kxm, kyp, kym = couple
    cols = jnp.arange(start.shape[-2])[:, None]
    at_left = (cols == 0).astype(jnp.float32)
    at_right = (cols == start.shape[-2] - 1).astype(jnp.float32)

    def advance(previous, inputs):
        wave, left_val, right_val = inputs
        rhs = (
            sigma * previous
            + coil * wave
            + at_left * left_val[..., None, :]
            + at_right * right_val[..., None, :]
        )
        field = previous
        for repeat in range(JACOBI):
            total = (
                rhs
                + kxp * next_column(field)
                + kxm * prev_column(field)
                + kyp * next_row(field)
                + kym * prev_row(field)
            )
            field = total / diag
        return (field, (field[..., 0, :], field[..., -1, :]))

    return lax.scan(advance, start, (waves, left_term, right_term))


def body(start_states, sigma, labels, nu_table, coil, waveform):
    states = start_states[0]
    nu = reluctivity(labels, nu_table)
    place = lax.axis_index("space")
    count = lax.axis_size("space")
    first = (place == 0).astype(jnp.float32)
    last = (place == count - 1).astype(jnp.float32)
    couple, left_coef, right_coef, d_dir, d_neu = coefficients(sigma, nu, first, last)
    zero_waves = jnp.zeros_like(waveform)
    traces = jnp.zeros((waveform.shape[0], states.shape[1]), jnp.float32)
    left_traces = jnp.zeros_like(traces)
    inner_face = 1.0 - last
    ends = states
    for relax_round in range(SWEEPS):
        if relax_round > 0:
            left_traces = passed_along(traces, "space", 1)
        left_term = left_coef * left_traces
        right_term = right_coef * traces
        ends, (firsts, lasts) = march(states, couple, d_dir, coil, waveform, left_term, right_term)
        nb_first, nb_coef = passed_along((firsts, left_coef), "space", -1)
        flux = inner_face * (right_coef * (lasts - traces) + nb_coef * (nb_first - traces))
        flux_left = passed_along(flux, "space", 1)
        unused, (pfirst, plast) = march(
            jnp.zeros_like(states), couple, d_neu, coil, zero_waves, flux_left, flux
        )
        nb_pfirst = passed_along(pfirst, "space", -1)
        traces = traces + THETA * inner_face * (plast + nb_pfirst)
        if relax_round + 1 < SWEEPS:
            states = from_behind(ends, "tm", 1)
    return (ends[None], traces)


def solution(mesh):
    placed = (
        P("tm", "space", None),
        P("space", None),
        P("space", None),
        P(),
        P("space", None),
        P("tm"),
    )
    return jax.shard_map(
        body,
        mesh=mesh,
        in_specs=placed,
        out_specs=(P("tm", "space", None), P("tm", "space")),
        check_vma=False,
    )
```

profile of v0, /device:TPU:8, one launch (start us, length us, event | category | flops | bytes accessed | tf_op | source)
XLA Modules:
  0.0 172.0 jit_solution(11880052353878125775)
XLA Ops:
  2.0 2.6 %select_add_fusion = f32[16,1024]{1,0:T(8,128)S(1)} fusion(s32[16,1024]{1,0:T(8,128)S(1)} %copy-done.3, f32[]{:T(128)} %bitcast.4, f32[]{:T(128)} %bitcast.3, f32[]{:T(128)} %bitcast.2, f32[]{:T(128)} %bitcast.1), kind=kLoop, calls=%fused_computation.469 | loop fusion | flops 180224 | bytes 131088 | tf_op jit(solution)/shard_map/add | solution.py:54
  5.0 0.8 copy-done.1
  5.8 38.7 %while.60 = (s32[]{:T(128)}, f32[16,1024]{1,0:T(8,128)S(1)}, f32[16,1024]{1,0:T(8,128)S(1)}, f32[16,1024]{1,0:T(8,128)S(1)}, f32[16,1024]{1,0:T(8,128)S(1)}, /*i...) while((s32[]{:T(128)}, f32[16,1024]{1,0:T(8,128)S(1)}, ...), condition=%wide.region_1.2_spmd.clone, body=%wide.region_0.1_spmd.clone.sunk | while | flops 1294402 | bytes 4383153 | solution.py:106
  6.4 0.7 fusion.360
  8.8 0.7 fusion.360
  11.2 0.7 fusion.360
  13.7 0.7 fusion.360
  16.1 0.7 fusion.360
  18.5 0.7 fusion.360
  20.9 0.7 fusion.360
  35.5 0.7 fusion.360
  37.9 0.7 fusion.360
  40.3 0.7 fusion.360
  42.7 0.7 fusion.360
  44.5 3.3 %collective-permute-start.2 = (f32[16,1024]{1,0:T(8,128)S(1)}, f32[16,1024]{1,0:T(8,128)S(1)}, u32[]{:S(2)}, u32[]{:S(2)}) collective-permute-start(f32[16,1024]{1,0:T(8,128)S(1)} %get-tuple-element.328), channel_id=1, source_target_pairs={{1,0},{2,1},{3,2},{4,3},{5,4},{6,5},{7,6},{9,8},{10,9},{11,10},{12... | collective-permute-start | bytes 196616 | tf_op jit(solution)/shard_map/ppermute | solution.py:16
  47.8 1.9 %collective-permute-start.1 = (f32[1024]{0:T(1024)S(1)}, f32[1024]{0:T(1024)S(1)}, u32[]{:S(2)}, u32[]{:S(2)}) collective-permute-start(f32[1024]{0:T(1024)S(1)} %bitcast.81), channel_id=1, source_target_pairs={{1,0},{2,1},{3,2},{4,3},{5,4},{6,5},{7,6},{9,8},{10,9},{11,10},{12... | collective-permute-start | bytes 12296 | tf_op jit(solution)/shard_map/ppermute | solution.py:16
  49.8 3.6 %collective-permute-done.1 = f32[1024]{0:T(1024)S(1)} collective-permute-done((f32[1024]{0:T(1024)S(1)}, f32[1024]{0:T(1024)S(1)}, u32[]{:S(2)}, u32[]{:S(2)}) %collective-permute-start.1) | collective-permute-done | bytes 4128 | tf_op jit(solution)/shard_map/ppermute | solution.py:16
  53.4 3.4 %collective-permute-start.3 = (f32[16,1024]{1,0:T(8,128)S(1)}, f32[16,1024]{1,0:T(8,128)S(1)}, u32[]{:S(2)}, u32[]{:S(2)}) collective-permute-start(f32[16,1024]{1,0:T(8,128)S(1)} %add_multiply_fusion.2), channel_id=1, source_target_pairs={{0,1},{1,2},{2,3},{3,4},{4,5},{5,6},{6,7},{8,9},{9,10},{10,11},{11... | collective-permute-start | bytes 196616 | tf_op jit(solution)/shard_map/ppermute | solution.py:16
  56.8 3.6 %collective-permute-done.3 = f32[16,1024]{1,0:T(8,128)S(1)} collective-permute-done((f32[16,1024]{1,0:T(8,128)S(1)}, f32[16,1024]{1,0:T(8,128)S(1)}, u32[]{:S(2)}, u32[]{:S(2)}) %collective-permute-start.3) | collective-permute-done | bytes 65568 | tf_op jit(solution)/shard_map/ppermute | solution.py:16
  60.4 19.5 %while.62 = (s32[]{:T(128)}, f32[16,1024]{1,0:T(8,128)S(1)}, f32[16,1024]{1,0:T(8,128)S(1)}, f32[16,1024]{1,0:T(8,128)S(1)}, f32[16,1024]{1,0:T(8,128)S(1)}, /*i...) while((s32[]{:T(128)}, f32[16,1024]{1,0:T(8,128)S(1)}, ...), condition=%wide.region_3.4_spmd.clone, body=%wide.region_2.3_spmd.clone.sunk | while | flops 1310787 | bytes 4514211 | solution.py:106
  80.0 1.9 %collective-permute-start.4 = (f32[16,1024]{1,0:T(8,128)S(1)}, f32[16,1024]{1,0:T(8,128)S(1)}, u32[]{:S(2)}, u32[]{:S(2)}) collective-permute-start(f32[16,1024]{1,0:T(8,128)S(1)} %get-tuple-element.330), channel_id=1, source_target_pairs={{1,0},{2,1},{3,2},{4,3},{5,4},{6,5},{7,6},{9,8},{10,9},{11,10},{12... | collective-permute-start | bytes 196616 | tf_op jit(solution)/shard_map/ppermute | solution.py:16
  81.9 4.2 %collective-permute-done.4 = f32[16,1024]{1,0:T(8,128)S(1)} collective-permute-done((f32[16,1024]{1,0:T(8,128)S(1)}, f32[16,1024]{1,0:T(8,128)S(1)}, u32[]{:S(2)}, u32[]{:S(2)}) %collective-permute-start.4) | collective-permute-done | bytes 65568 | tf_op jit(solution)/shard_map/ppermute | solution.py:16
  86.1 3.4 %collective-permute-start.5 = (f32[16,1024]{1,0:T(8,128)S(1)}, f32[16,1024]{1,0:T(8,128)S(1)}, u32[]{:S(2)}, u32[]{:S(2)}) collective-permute-start(f32[16,1024]{1,0:T(8,128)S(1)} %get-tuple-element.607), channel_id=1, source_target_pairs={{0,1},{1,2},{2,3},{3,4},{4,5},{5,6},{6,7},{8,9},{9,10},{10,11},{11... | collective-permute-start | bytes 196616 | tf_op jit(solution)/shard_map/ppermute | solution.py:16
  89.6 3.6 %collective-permute-done.5 = f32[16,1024]{1,0:T(8,128)S(1)} collective-permute-done((f32[16,1024]{1,0:T(8,128)S(1)}, f32[16,1024]{1,0:T(8,128)S(1)}, u32[]{:S(2)}, u32[]{:S(2)}) %collective-permute-start.5) | collective-permute-done | bytes 65568 | tf_op jit(solution)/shard_map/ppermute | solution.py:16
  93.3 38.8 %while.61 = (s32[]{:T(128)}, f32[16,1024]{1,0:T(8,128)S(1)}, f32[16,1024]{1,0:T(8,128)S(1)}, f32[16,1024]{1,0:T(8,128)S(1)}, f32[16,1024]{1,0:T(8,128)S(1)}, /*i...) while((s32[]{:T(128)}, f32[16,1024]{1,0:T(8,128)S(1)}, ...), condition=%wide.region_5.6_spmd.clone, body=%wide.region_4.5_spmd.clone.sunk | while | flops 1294402 | bytes 4383153 | solution.py:106
  94.0 0.8 fusion.370
  96.4 0.8 fusion.370
  98.8 0.8 fusion.370
  101.2 0.8 fusion.370
  103.7 0.8 fusion.370
  106.1 0.8 fusion.370
  108.5 0.8 fusion.370
  110.9 0.8 fusion.370
  113.3 0.8 fusion.370
  115.8 0.8 fusion.370
  118.2 0.8 fusion.370
  120.6 0.8 fusion.370
  123.0 0.8 fusion.370
  125.5 0.8 fusion.370
  127.9 0.8 fusion.370
  130.3 0.8 fusion.370
  132.1 3.3 %collective-permute-start.6 = (f32[16,1024]{1,0:T(8,128)S(1)}, f32[16,1024]{1,0:T(8,128)S(1)}, u32[]{:S(2)}, u32[]{:S(2)}) collective-permute-start(f32[16,1024]{1,0:T(8,128)S(1)} %get-tuple-element.333), channel_id=1, source_target_pairs={{1,0},{2,1},{3,2},{4,3},{5,4},{6,5},{7,6},{9,8},{10,9},{11,10},{12... | collective-permute-start | bytes 196616 | tf_op jit(solution)/shard_map/ppermute | solution.py:16
  135.4 2.8 %collective-permute-done.6 = f32[16,1024]{1,0:T(8,128)S(1)} collective-permute-done((f32[16,1024]{1,0:T(8,128)S(1)}, f32[16,1024]{1,0:T(8,128)S(1)}, u32[]{:S(2)}, u32[]{:S(2)}) %collective-permute-start.6) | collective-permute-done | bytes 65568 | tf_op jit(solution)/shard_map/ppermute | solution.py:16
  138.3 4.3 %collective-permute-start.7 = (f32[16,1024]{1,0:T(8,128)S(1)}, f32[16,1024]{1,0:T(8,128)S(1)}, u32[]{:S(2)}, u32[]{:S(2)}) collective-permute-start(f32[16,1024]{1,0:T(8,128)S(1)} %add_multiply_fusion), channel_id=1, source_target_pairs={{0,1},{1,2},{2,3},{3,4},{4,5},{5,6},{6,7},{8,9},{9,10},{10,11},{11... | collective-permute-start | bytes 196616 | tf_op jit(solution)/shard_map/ppermute | solution.py:16
  142.6 2.7 %collective-permute-done.7 = f32[16,1024]{1,0:T(8,128)S(1)} collective-permute-done((f32[16,1024]{1,0:T(8,128)S(1)}, f32[16,1024]{1,0:T(8,128)S(1)}, u32[]{:S(2)}, u32[]{:S(2)}) %collective-permute-start.7) | collective-permute-done | bytes 65568 | tf_op jit(solution)/shard_map/ppermute | solution.py:16
  145.4 19.2 %while.63 = (s32[]{:T(128)}, f32[16,1024]{1,0:T(8,128)S(1)}, f32[16,1024]{1,0:T(8,128)S(1)}, f32[16,1024]{1,0:T(8,128)S(1)}, f32[16,1024]{1,0:T(8,128)S(1)}, /*i...) while((s32[]{:T(128)}, f32[16,1024]{1,0:T(8,128)S(1)}, ...), condition=%wide.region_7.8_spmd.clone, body=%wide.region_6.7_spmd.clone.sunk | while | flops 1310787 | bytes 4514211 | solution.py:106
  164.6 3.3 %collective-permute-start.8 = (f32[16,1024]{1,0:T(8,128)S(1)}, f32[16,1024]{1,0:T(8,128)S(1)}, u32[]{:S(2)}, u32[]{:S(2)}) collective-permute-start(f32[16,1024]{1,0:T(8,128)S(1)} %get-tuple-element.335), channel_id=1, source_target_pairs={{1,0},{2,1},{3,2},{4,3},{5,4},{6,5},{7,6},{9,8},{10,9},{11,10},{12... | collective-permute-start | bytes 196616 | tf_op jit(solution)/shard_map/ppermute | solution.py:16
  167.9 2.8 %collective-permute-done.8 = f32[16,1024]{1,0:T(8,128)S(1)} collective-permute-done((f32[16,1024]{1,0:T(8,128)S(1)}, f32[16,1024]{1,0:T(8,128)S(1)}, u32[]{:S(2)}, u32[]{:S(2)}) %collective-permute-start.8) | collective-permute-done | bytes 65568 | tf_op jit(solution)/shard_map/ppermute | solution.py:16
  (909 shorter events, 92.8 us)
Async XLA Ops:
  0.6 1.4 copy-start.3
  0.7 0.7 copy-start.4
  2.0 2.6 %copy-start = (f32[16,1024]{1,0:T(8,128)S(1)}, f32[16,1024]{1,0:T(8,128)}, u32[]{:S(2)}) copy-start(f32[16,1024]{1,0:T(8,128)} %param.15) | copy-start | bytes 196612
  4.9 0.8 copy-start.1
  4.9 0.9 copy-start.2
  4.9 0.8 copy-start.5
  44.5 8.8 %collective-permute-start.2 = (f32[16,1024]{1,0:T(8,128)S(1)}, f32[16,1024]{1,0:T(8,128)S(1)}, u32[]{:S(2)}, u32[]{:S(2)}) collective-permute-start(f32[16,1024]{1,0:T(8,128)S(1)} %get-tuple-element.328), channel_id=1, source_target_pairs={{1,0},{2,1},{3,2},{4,3},{5,4},{6,5},{7,6},{9,8},{10,9},{11,10},{12... | collective-permute-start | bytes 196616 | tf_op jit(solution)/shard_map/ppermute | solution.py:16
  47.8 5.5 %collective-permute-start.1 = (f32[1024]{0:T(1024)S(1)}, f32[1024]{0:T(1024)S(1)}, u32[]{:S(2)}, u32[]{:S(2)}) collective-permute-start(f32[1024]{0:T(1024)S(1)} %bitcast.81), channel_id=1, source_target_pairs={{1,0},{2,1},{3,2},{4,3},{5,4},{6,5},{7,6},{9,8},{10,9},{11,10},{12... | collective-permute-start | bytes 12296 | tf_op jit(solution)/shard_map/ppermute | solution.py:16
  53.4 7.1 %collective-permute-start.3 = (f32[16,1024]{1,0:T(8,128)S(1)}, f32[16,1024]{1,0:T(8,128)S(1)}, u32[]{:S(2)}, u32[]{:S(2)}) collective-permute-start(f32[16,1024]{1,0:T(8,128)S(1)} %add_multiply_fusion.2), channel_id=1, source_target_pairs={{0,1},{1,2},{2,3},{3,4},{4,5},{5,6},{6,7},{8,9},{9,10},{10,11},{11... | collective-permute-start | bytes 196616 | tf_op jit(solution)/shard_map/ppermute | solution.py:16
  80.0 6.2 %collective-permute-start.4 = (f32[16,1024]{1,0:T(8,128)S(1)}, f32[16,1024]{1,0:T(8,128)S(1)}, u32[]{:S(2)}, u32[]{:S(2)}) collective-permute-start(f32[16,1024]{1,0:T(8,128)S(1)} %get-tuple-element.330), channel_id=1, source_target_pairs={{1,0},{2,1},{3,2},{4,3},{5,4},{6,5},{7,6},{9,8},{10,9},{11,10},{12... | collective-permute-start | bytes 196616 | tf_op jit(solution)/shard_map/ppermute | solution.py:16
  86.1 7.1 %collective-permute-start.5 = (f32[16,1024]{1,0:T(8,128)S(1)}, f32[16,1024]{1,0:T(8,128)S(1)}, u32[]{:S(2)}, u32[]{:S(2)}) collective-permute-start(f32[16,1024]{1,0:T(8,128)S(1)} %get-tuple-element.607), channel_id=1, source_target_pairs={{0,1},{1,2},{2,3},{3,4},{4,5},{5,6},{6,7},{8,9},{9,10},{10,11},{11... | collective-permute-start | bytes 196616 | tf_op jit(solution)/shard_map/ppermute | solution.py:16
  89.6 3.7 %collective-permute-start = (f32[16,1024]{1,0:T(8,128)S(1)}, f32[16,1024]{1,0:T(8,128)S(1)}, u32[]{:S(2)}, u32[]{:S(2)}) collective-permute-start(f32[16,1024]{1,0:T(8,128)S(1)} %get-tuple-element.326), channel_id=1, source_target_pairs={{0,8},{8,16},{16,24},{24,0},{1,9},{9,17},{17,25},{25,1},{2,10},{10... | collective-permute-start | bytes 196616 | tf_op jit(solution)/shard_map/ppermute | solution.py:22
  132.1 6.2 %collective-permute-start.6 = (f32[16,1024]{1,0:T(8,128)S(1)}, f32[16,1024]{1,0:T(8,128)S(1)}, u32[]{:S(2)}, u32[]{:S(2)}) collective-permute-start(f32[16,1024]{1,0:T(8,128)S(1)} %get-tuple-element.333), channel_id=1, source_target_pairs={{1,0},{2,1},{3,2},{4,3},{5,4},{6,5},{7,6},{9,8},{10,9},{11,10},{12... | collective-permute-start | bytes 196616 | tf_op jit(solution)/shard_map/ppermute | solution.py:16
  138.3 7.1 %collective-permute-start.7 = (f32[16,1024]{1,0:T(8,128)S(1)}, f32[16,1024]{1,0:T(8,128)S(1)}, u32[]{:S(2)}, u32[]{:S(2)}) collective-permute-start(f32[16,1024]{1,0:T(8,128)S(1)} %add_multiply_fusion), channel_id=1, source_target_pairs={{0,1},{1,2},{2,3},{3,4},{4,5},{5,6},{6,7},{8,9},{9,10},{10,11},{11... | collective-permute-start | bytes 196616 | tf_op jit(solution)/shard_map/ppermute | solution.py:16
  164.6 6.2 %collective-permute-start.8 = (f32[16,1024]{1,0:T(8,128)S(1)}, f32[16,1024]{1,0:T(8,128)S(1)}, u32[]{:S(2)}, u32[]{:S(2)}) collective-permute-start(f32[16,1024]{1,0:T(8,128)S(1)} %get-tuple-element.335), channel_id=1, source_target_pairs={{1,0},{2,1},{3,2},{4,3},{5,4},{6,5},{7,6},{9,8},{10,9},{11,10},{12... | collective-permute-start | bytes 196616 | tf_op jit(solution)/shard_map/ppermute | solution.py:16
where the time goes:
time: 174 us; the launch traced here: 172 us
  other arithmetic  79 us (45%)
  local copies, waits for them, and re-layouts  37.2 us (21%)
  starting transfers between devices  25 us (14%)
  waiting for transfers between devices  23.5 us (14%)
  loops' own time  6.4 us (4%)
    div x512, other arithmetic, advance(): field = total / diag  74.9 us
    ppermute x8, starting transfers between devices, passed_along(): return lax.ppermute(array, axis, pairs)  25 us
    ppermute x8, waiting for transfers between devices, passed_along(): return lax.ppermute(array, axis, pairs)  23.4 us
    dynamic_slice x96, local copies, waits for them, and re-layouts, march(): return lax.scan(advance, start, (waves, left_term, right_term))  19.8 us
    dynamic_update_slice x128, local copies, waits for them, and re-layouts, march(): return lax.scan(advance, start, (waves, left_term, right_term))  14.1 us
    another operation x4, loops' own time, march(): return lax.scan(advance, start, (waves, left_term, right_term))  6.4 us
  transfers between devices with their start and end apart: 9, of which 8 were waited for; matrix products, arithmetic and copies ran while one was open for 0% of the time, Pallas kernels for 0%

commit v1 on v0

v1 whole, which is shorter than its diff:
```python
import functools

import jax
import jax.numpy as jnp
from jax import lax
from jax.experimental import pallas as pl
from jax.experimental.pallas import tpu as pltpu
from jax.sharding import PartitionSpec as P

JACOBI = 8
SWEEPS = 2
THETA = 0.25

BLOCK = 8
SUB = 8
LANES = 128
DEPTH = 4
LOW = -(DEPTH - 1)
HIGH = BLOCK + DEPTH - 1
ROWS = HIGH - LOW
Q_E, P_O, Q_O, UP_O, DN_O, UP_E, DN_E = range(7)
SIG_E, SIG_O, COIL_E, COIL_O, FACE_E, FACE_O = range(6)
F32 = jnp.float32


def tile_index(axis):
    return lax.broadcasted_iota(jnp.int32, (SUB, LANES), axis)


def next_lane(tile):
    return pltpu.roll(tile, LANES - 1, 1)


def prev_lane(tile):
    return pltpu.roll(tile, 1, 1)


def next_sub(tile):
    return pltpu.roll(tile, SUB - 1, 0)


def prev_sub(tile):
    return pltpu.roll(tile, 1, 0)


def swap_groups(tiles):
    group = tile_index(1) // 16
    for bit in (1, 2, 4):
        new = []
        for j, tile in enumerate(tiles):
            other = tiles[j ^ bit]
            if j & bit:
                new.append(jnp.where((group & bit) != 0, tile, pltpu.roll(other, LANES - 16 * bit, 1)))
            else:
                new.append(jnp.where((group & bit) == 0, tile, pltpu.roll(other, 16 * bit, 1)))
        tiles = new
    return tiles


def to_blocks(tiles):
    lane = tile_index(1)
    order = 8 * (lane % 16) + lane // 16
    return swap_groups([jnp.take_along_axis(tile, order, axis=1) for tile in tiles])


def from_blocks(tiles):
    lane = tile_index(1)
    order = 16 * (lane % 8) + lane // 8
    return [jnp.take_along_axis(tile, order, axis=1) for tile in swap_groups(tiles)]


def load_field(ref, scratch):
    for j in range(BLOCK):
        scratch[16 * j : 16 * j + 16, :] = ref[:, LANES * j : LANES * j + LANES]
    halves = [
        to_blocks([scratch[pl.ds(16 * j + e, SUB, stride=2), :] for j in range(BLOCK)])
        for e in range(2)
    ]
    return halves


def harmonic(first_nu, second_nu):
    return 2.0 * first_nu * second_nu / (first_nu + second_nu)


def spread(tiles):
    rows = {}
    for r in range(LOW, HIGH):
        if r < 0:
            rows[r] = prev_lane(tiles[r + BLOCK])
        elif r >= BLOCK:
            rows[r] = next_lane(tiles[r - BLOCK])
        else:
            rows[r] = tiles[r]
    return rows


def flags():
    place = lax.axis_index("space")
    count = lax.axis_size("space")
    return place % 2 == 0, place > 0, place < count - 1


def plain_kernel(labels_ref, table_ref, sigma_ref, coil_ref, start_ref, nu_out, sigma_out, coil_out, start_out, s0, s1, s2, s3):
    nu = jnp.zeros(labels_ref.shape, F32)
    for material in range(table_ref.shape[0]):
        nu = nu + jnp.where(labels_ref[...] == material, table_ref[material], 0.0)
    for value, scratch, out in ((nu, s0, nu_out), (sigma_ref[...], s1, sigma_out), (coil_ref[...], s2, coil_out), (start_ref[0], s3, start_out)):
        halves = load_field(value, scratch)
        for e in range(2):
            for r in range(BLOCK):
                out[r, e] = halves[e][r]


def unit_up(r):
    return r % BLOCK in (0, 2, 4, 6)


def unit_down(r):
    return r % BLOCK in (2, 4, 6)


def coef_kernel(neumann, nu_ref, sigma_ref, coil_ref, c_out, r_out, scale_out, edge_out):
    _, has_left, has_right = flags()
    sub = tile_index(0)
    lane = tile_index(1)
    nu_e = [nu_ref[r, 0] for r in range(BLOCK)]
    nu_o = [nu_ref[r, 1] for r in range(BLOCK)]
    pair = [harmonic(nu_e[r], nu_o[r]) for r in range(BLOCK)]
    cross_o = [jnp.where(sub == SUB - 1, 0.0, harmonic(nu_o[r], next_sub(nu_e[r]))) for r in range(BLOCK)]
    cross_e = [prev_sub(cross_o[r]) for r in range(BLOCK)]

    def upward(nu):
        ups = [harmonic(nu[r], nu[r + 1]) for r in range(BLOCK - 1)]
        ups.append(jnp.where(lane == LANES - 1, 0.0, harmonic(nu[BLOCK - 1], next_lane(nu[0]))))
        downs = [prev_lane(ups[BLOCK - 1])] + ups[:-1]
        return ups, downs

    up_e, dn_e = upward(nu_e)
    up_o, dn_o = upward(nu_o)
    left_kept = jnp.logical_not(has_left) if neumann else True
    right_kept = jnp.logical_not(has_right) if neumann else True
    inv_e, inv_o, sig_e, sig_o = [], [], [], []
    for r in range(BLOCK):
        d_e = sigma_ref[r, 0] + pair[r] + cross_e[r] + up_e[r] + dn_e[r]
        d_o = sigma_ref[r, 1] + pair[r] + cross_o[r] + up_o[r] + dn_o[r]
        if r in (0, BLOCK - 1):
            on_edge = lane == (0 if r == 0 else LANES - 1)
            d_e = d_e + jnp.where(on_edge, 2.0 * nu_e[r], 0.0)
            d_o = d_o + jnp.where(on_edge, 2.0 * nu_o[r], 0.0)
        d_e = d_e + jnp.where((sub == 0) & left_kept, 2.0 * nu_e[r], 0.0)
        d_o = d_o + jnp.where((sub == SUB - 1) & right_kept, 2.0 * nu_o[r], 0.0)
        inv_e.append(1.0 / d_e)
        inv_o.append(1.0 / d_o)
    scale_e, scale_o = [jnp.ones((SUB, LANES), F32)], []
    for r in range(1, BLOCK):
        if unit_down(r):
            scale_e.append(scale_e[r - 1] * (dn_e[r] * inv_e[r]))
        else:
            scale_e.append(scale_e[r - 1] / (up_e[r - 1] * inv_e[r - 1]))
    for r in range(BLOCK):
        scale_o.append(scale_e[r] / (pair[r] * inv_e[r]))
    rec_e = [inv_e[r] / scale_e[r] for r in range(BLOCK)]
    rec_o = [inv_o[r] / scale_o[r] for r in range(BLOCK)]
    around_e = [prev_lane(scale_e[BLOCK - 1])] + scale_e + [next_lane(scale_e[0])]
    around_o = [prev_lane(scale_o[BLOCK - 1])] + scale_o + [next_lane(scale_o[0])]

    def put(out, slot, tiles, needed=lambda r: True):
        rows = spread(tiles)
        for r in range(LOW, HIGH):
            if needed(r):
                out[r - LOW, slot] = rows[r]

    span = range(BLOCK)
    put(c_out, Q_E, [cross_e[r] * prev_sub(scale_o[r]) * rec_e[r] for r in span])
    put(c_out, P_O, [pair[r] * scale_e[r] * rec_o[r] for r in span])
    put(c_out, Q_O, [cross_o[r] * next_sub(scale_e[r]) * rec_o[r] for r in span])
    put(c_out, UP_O, [up_o[r] * around_o[r + 2] * rec_o[r] for r in span])
    put(c_out, DN_O, [dn_o[r] * around_o[r] * rec_o[r] for r in span])
    put(c_out, UP_E, [up_e[r] * around_e[r + 2] * rec_e[r] for r in span], lambda r: not unit_up(r))
    put(c_out, DN_E, [dn_e[r] * around_e[r] * rec_e[r] for r in span], lambda r: not unit_down(r))
    put(r_out, SIG_E, [sigma_ref[r, 0] * inv_e[r] for r in span])
    put(r_out, SIG_O, [sigma_ref[r, 1] * inv_o[r] for r in span])
    if not neumann:
        put(r_out, COIL_E, [coil_ref[r, 0] * rec_e[r] for r in span])
        put(r_out, COIL_O, [coil_ref[r, 1] * rec_o[r] for r in span])
    put(r_out, FACE_E, [jnp.where((sub == 0) & has_left, rec_e[r], 0.0) for r in span])
    put(r_out, FACE_O, [jnp.where((sub == SUB - 1) & has_right, rec_o[r], 0.0) for r in span])
    for r in range(BLOCK):
        scale_out[r, 0] = scale_e[r]
        scale_out[r, 1] = scale_o[r]
        edge_out[0, r : r + 1] = 2.0 * nu_e[r][0:1]
        edge_out[1, r : r + 1] = 2.0 * nu_o[r][SUB - 1 : SUB]
        edge_out[2, r : r + 1] = scale_e[r][0:1]
        edge_out[3, r : r + 1] = scale_o[r][SUB - 1 : SUB]


def advance(field_e, field_o, rhs, c_ref):
    for turn in range(JACOBI // DEPTH):
        if turn == 0:
            now_e, now_o = field_e, field_o
        else:
            now_e, now_o = haloed(now_e), haloed(now_o)
        for k in range(1, DEPTH + 1):
            new_e, new_o = {}, {}
            for r in range(k - DEPTH, BLOCK + DEPTH - k):
                i = r - LOW
                up = now_e[r + 1] if unit_up(r) else c_ref[i, UP_E] * now_e[r + 1]
                down = now_e[r - 1] if unit_down(r) else c_ref[i, DN_E] * now_e[r - 1]
                new_e[r] = (rhs[r][0] + now_o[r]) + (up + down) + c_ref[i, Q_E] * prev_sub(now_o[r])
                new_o[r] = (
                    (rhs[r][1] + c_ref[i, P_O] * now_e[r])
                    + (c_ref[i, UP_O] * now_o[r + 1] + c_ref[i, DN_O] * now_o[r - 1])
                    + c_ref[i, Q_O] * next_sub(now_e[r])
                )
            now_e, now_o = new_e, new_o
    return now_e, now_o


def haloed(rows):
    out = {r: rows[r] for r in range(BLOCK)}
    for j in range(DEPTH):
        out[j - DEPTH] = prev_lane(rows[BLOCK - DEPTH + j])
        out[BLOCK + j] = next_lane(rows[j])
    return out


def march(start, c_ref, r_ref, wave_ref, left, right, first, last, steps):
    def step(t, carry):
        now_e = haloed(dict(enumerate(carry[:BLOCK])))
        now_o = haloed(dict(enumerate(carry[BLOCK:])))
        rhs = {}
        for r in range(LOW, HIGH):
            i = r - LOW
            b_e = r_ref[i, SIG_E] * now_e[r]
            b_o = r_ref[i, SIG_O] * now_o[r]
            if wave_ref is not None:
                b_e = b_e + r_ref[i, COIL_E] * wave_ref[t]
                b_o = b_o + r_ref[i, COIL_O] * wave_ref[t]
            if left is not None:
                at = pl.ds(t * 3 * BLOCK + BLOCK + r, 1)
                b_e = b_e + r_ref[i, FACE_E] * left[at, :]
                b_o = b_o + r_ref[i, FACE_O] * right[at, :]
            rhs[r] = (b_e, b_o)
        now_e, now_o = advance(now_e, now_o, rhs, c_ref)
        for r in range(BLOCK):
            first[pl.ds(t * BLOCK + r, 1), :] = now_e[r][0:1]
            last[pl.ds(t * BLOCK + r, 1), :] = now_o[r][SUB - 1 : SUB]
        return tuple(now_e[r] for r in range(BLOCK)) + tuple(now_o[r] for r in range(BLOCK))

    return lax.fori_loop(0, steps, step, start)


def put_face(ref, t, tile):
    base = t * 3 * BLOCK
    ref[base : base + BLOCK, :] = prev_lane(tile)
    ref[base + BLOCK : base + 2 * BLOCK, :] = tile
    ref[base + 2 * BLOCK : base + 3 * BLOCK, :] = next_lane(tile)


def at_step(ref, t):
    return ref[t * BLOCK : (t + 1) * BLOCK, :]


def dirichlet_kernel(sweep, steps, *refs):
    if sweep == 0:
        (start_ref, c_ref, r_ref, scale_ref, edge_ref, wave_ref, ends, ev_out, od_out, first, last) = refs
        left = right = None
    else:
        (start_ref, c_ref, r_ref, scale_ref, edge_ref, wave_ref, ev_own, od_own, ev_got, od_got,
         ends, ev_out, od_out, g_left, g_right, first, last, left, right) = refs
    even, _, _ = flags()
    if sweep > 0:
        for t in range(steps):
            ev = THETA * (at_step(ev_own, t) + at_step(ev_got, t))
            od = THETA * (at_step(od_own, t) + at_step(od_got, t))
            at_left = jnp.where(even, od, ev)
            at_right = jnp.where(even, ev, od)
            g_left[t * BLOCK : (t + 1) * BLOCK, :] = at_left
            g_right[t * BLOCK : (t + 1) * BLOCK, :] = at_right
            put_face(left, t, edge_ref[0] * at_left)
            put_face(right, t, edge_ref[1] * at_right)
    start = tuple(start_ref[r, e] / scale_ref[r, e] for e in range(2) for r in range(BLOCK))
    final = march(start, c_ref, r_ref, wave_ref, left, right, first, last, steps)
    for e in range(2):
        for r in range(BLOCK):
            ends[r, e] = final[e * BLOCK + r] * scale_ref[r, e]
    for t in range(steps):
        to_left = edge_ref[2] * at_step(first, t)
        to_right = edge_ref[3] * at_step(last, t)
        if sweep > 0:
            to_left = to_left - at_step(g_left, t)
            to_right = to_right - at_step(g_right, t)
        to_left = edge_ref[0] * to_left
        to_right = edge_ref[1] * to_right
        ev_out[t * BLOCK : (t + 1) * BLOCK, :] = jnp.where(even, to_right, to_left)
        od_out[t * BLOCK : (t + 1) * BLOCK, :] = jnp.where(even, to_left, to_right)


def neumann_kernel(sweep, steps, *refs):
    if sweep + 1 < SWEEPS:
        (c_ref, r_ref, edge_ref, ev_own, od_own, ev_got, od_got, ev_out, od_out, first, last, left, right) = refs
    else:
        (c_ref, r_ref, edge_ref, ev_own, od_own, ev_got, od_got, g_right, mine_out, first_out,
         first, last, left, right, s0, s1) = refs
    even, _, _ = flags()
    for t in range(steps):
        ev = at_step(ev_own, t) + at_step(ev_got, t)
        od = at_step(od_own, t) + at_step(od_got, t)
        put_face(left, t, jnp.where(even, od, ev))
        put_face(right, t, jnp.where(even, ev, od))
    zero = jnp.zeros((SUB, LANES), F32)
    march((zero,) * (2 * BLOCK), c_ref, r_ref, None, left, right, first, last, steps)
    if sweep + 1 < SWEEPS:
        for t in range(steps):
            to_left = edge_ref[2] * at_step(first, t)
            to_right = edge_ref[3] * at_step(last, t)
            ev_out[t * BLOCK : (t + 1) * BLOCK, :] = jnp.where(even, to_right, to_left)
            od_out[t * BLOCK : (t + 1) * BLOCK, :] = jnp.where(even, to_left, to_right)
    else:
        for t in range(steps):
            s0[t * BLOCK : (t + 1) * BLOCK, :] = THETA * (edge_ref[2] * at_step(first, t))
            s1[t * BLOCK : (t + 1) * BLOCK, :] = at_step(g_right, t) + THETA * (edge_ref[3] * at_step(last, t))
        for scratch, out in ((s0, first_out), (s1, mine_out)):
            for half in range(steps // SUB):
                base = half * SUB * BLOCK
                tiles = from_blocks([scratch[pl.ds(base + r, SUB, stride=BLOCK), :] for r in range(BLOCK)])
                for j in range(BLOCK):
                    out[half * SUB : (half + 1) * SUB, j * LANES : (j + 1) * LANES] = tiles[j]


def natural_kernel(ends_ref, out, scratch):
    for e in range(2):
        tiles = from_blocks([ends_ref[r, e] for r in range(BLOCK)])
        for j in range(BLOCK):
            scratch[pl.ds(16 * j + e, SUB, stride=2), :] = tiles[j]
    for j in range(BLOCK):
        out[0, :, LANES * j : LANES * j + LANES] = scratch[16 * j : 16 * j + 16, :]


def join_kernel(mine_ref, got_ref, out):
    _, _, has_right = flags()
    out[...] = jnp.where(has_right, mine_ref[...] + got_ref[...], 0.0)


def call(kernel, name, inputs, outputs, scratch=(), smem=()):
    specs = [
        pl.BlockSpec(memory_space=pltpu.SMEM if i in smem else pltpu.VMEM)
        for i in range(len(inputs))
    ]
    single = not isinstance(outputs, list)
    shapes = [jax.ShapeDtypeStruct(s, F32) for s in ([outputs] if single else outputs)]
    result = pl.pallas_call(
        kernel,
        out_shape=shapes,
        in_specs=specs,
        out_specs=[pl.BlockSpec(memory_space=pltpu.VMEM)] * len(shapes),
        scratch_shapes=[pltpu.VMEM(s, F32) for s in scratch],
        compiler_params=pltpu.CompilerParams(vmem_limit_bytes=6 << 20),
        name=name,
    )(*inputs)
    return result[0] if single else result


def body(start_states, sigma, labels, nu_table, coil, waveform):
    steps = waveform.shape[0]
    columns, rows = sigma.shape
    count = lax.axis_size("space")
    windows = lax.axis_size("tm")
    even_faces = [(i, i ^ 1) for i in range(count)]
    odd_faces = [(i, i + 1 if i % 2 else i - 1) for i in range(1, count - 1)] + [(0, 0), (count - 1, count - 1)]
    field = (BLOCK, 2, SUB, LANES)
    series = (steps * BLOCK, LANES)
    wide = (3 * steps * BLOCK, LANES)
    nu, sig, cur, state = call(
        plain_kernel, "plain", [labels, nu_table, sigma, coil, start_states], [field] * 4, [(128, LANES)] * 4, smem=(1,)
    )
    shapes = [(ROWS, 7, SUB, LANES), (ROWS, 6, SUB, LANES), field, (4, BLOCK, LANES)]
    c_dir, r_dir, scale_dir, edge_dir = call(functools.partial(coef_kernel, False), "coef_dir", [nu, sig, cur], shapes)
    c_neu, r_neu, _, edge_neu = call(functools.partial(coef_kernel, True), "coef_neu", [nu, sig, cur], shapes)

    def swapped(ev, od):
        return lax.ppermute(ev, "space", even_faces), lax.ppermute(od, "space", odd_faces)

    ends, ev, od = call(
        functools.partial(dirichlet_kernel, 0, steps), "dir0",
        [state, c_dir, r_dir, scale_dir, edge_dir, waveform], [field, series, series], [series] * 2, smem=(5,),
    )
    state = lax.ppermute(ends, "tm", [(i, (i + 1) % windows) for i in range(windows)])
    ev_got, od_got = swapped(ev, od)
    ev, od = call(
        functools.partial(neumann_kernel, 0, steps), "neu0",
        [c_neu, r_neu, edge_neu, ev, od, ev_got, od_got], [series] * 2, [series] * 2 + [wide] * 2,
    )
    ev_got, od_got = swapped(ev, od)
    ends, ev, od, _, g_right = call(
        functools.partial(dirichlet_kernel, 1, steps), "dir1",
        [state, c_dir, r_dir, scale_dir, edge_dir, waveform, ev, od, ev_got, od_got],
        [field, series, series, series, series], [series] * 2 + [wide] * 2, smem=(5,),
    )
    ev_got, od_got = swapped(ev, od)
    end_states = call(natural_kernel, "natural", [ends], (1, columns, rows), [(128, LANES)])
    mine, first = call(
        functools.partial(neumann_kernel, 1, steps), "neu1",
        [c_neu, r_neu, edge_neu, ev, od, ev_got, od_got, g_right],
        [(steps, rows)] * 2, [series] * 2 + [wide] * 2 + [series] * 2,
    )
    got = lax.ppermute(first, "space", [(i, i - 1) for i in range(1, count)])
    traces = call(join_kernel, "join", [mine, got], (steps, rows))
    return end_states, traces


def solution(mesh):
    placed = (
        P("tm", "space", None),
        P("space", None),
        P("space", None),
        P(),
        P("space", None),
        P("tm"),
    )
    return jax.shard_map(
        body,
        mesh=mesh,
        in_specs=placed,
        out_specs=(P("tm", "space", None), P("tm", "space")),
        check_vma=False,
    )
```

time: 174 us -> 58.3 us (0.34)
  other arithmetic: 79 us -> 0 us
  local copies, waits for them, and re-layouts: 37.2 us -> 4.66 us
  Pallas kernels: 0 us -> 23.4 us
  starting transfers between devices: 25 us -> 11.4 us
  loops' own time: 6.4 us -> 0 us
  waiting for transfers between devices: 23.5 us -> 17.8 us
    div x512 -> x0, other arithmetic: 74.9 us -> none  [advance(): field = total / diag]
    pallas_call x0 -> x9, Pallas kernels: none -> 23.4 us  [call(): pl.pallas_call(kernel, out_shape=shapes, in_specs=specs, out_specs=[pl.Bl...]
    dynamic_slice x96 -> x0, local copies, waits for them, and re-layouts: 19.8 us -> none  [march(): return lax.scan(advance, start, (waves, left_term, right_term))]
    dynamic_update_slice x128 -> x0, local copies, waits for them, and re-layouts: 14.1 us -> none  [march(): return lax.scan(advance, start, (waves, left_term, right_term))]
    ppermute x9 -> x8, starting transfers between devices: 25 us -> 11.4 us  [the longest x3 5.73 us: swapped(): lax.ppermute(od, 'space', odd_faces)]
    another operation x4 -> x0, loops' own time: 6.4 us -> none  [march(): return lax.scan(advance, start, (waves, left_term, right_term))]
    ppermute x9 -> x8, waiting for transfers between devices: 23.5 us -> 17.8 us  [the longest x3 11.1 us: swapped(): lax.ppermute(od, 'space', odd_faces)]
    add x4 -> x0, other arithmetic: 3.46 us -> none  [the longest x1 2.58 us: reluctivity(): result + jnp.where(labels == material, nu_table[material], jnp.float32(0.0))]
  transfers between devices with their start and end apart: 9 -> 8, of which waited for: 8 -> 6; matrix products, arithmetic and copies ran while one was open for 0% -> 0% of each run, Pallas kernels for 0% -> 11%
where the time goes in v1:
time: 58.3 us; the launch traced here: 57.9 us
  Pallas kernels  23.4 us (40%)
  waiting for transfers between devices  17.8 us (31%)
  starting transfers between devices  11.4 us (20%)
  local copies, waits for them, and re-layouts  4.66 us (8%)
  between operations  0.73 us (1%)
    pallas_call x9, Pallas kernels, call(): pl.pallas_call(kernel, out_shape=shapes, in_specs=specs, out_specs=[pl.Bl...  23.4 us
    ppermute x3, waiting for transfers between devices, swapped(): lax.ppermute(od, 'space', odd_faces)  11.1 us
    ppermute x3, starting transfers between devices, swapped(): lax.ppermute(od, 'space', odd_faces)  5.73 us
    unnamed x12, local copies, waits for them, and re-layouts  4.66 us
    ppermute x3, starting transfers between devices, swapped(): lax.ppermute(ev, 'space', even_faces)  3.68 us
    ppermute x3, waiting for transfers between devices, swapped(): lax.ppermute(ev, 'space', even_faces)  3.37 us
    ppermute x1, waiting for transfers between devices, body(): got = lax.ppermute(first, 'space', [(i, i - 1) for i in range(1, count)])  3.3 us
    ppermute x1, starting transfers between devices, body(): got = lax.ppermute(first, 'space', [(i, i - 1) for i in range(1, count)])  1.92 us
  transfers between devices with their start and end apart: 8, of which 6 were waited for; matrix products, arithmetic and copies ran while one was open for 0% of the time, Pallas kernels for 11%

profile of v1, /device:TPU:8, one launch (start us, length us, event | category | flops | bytes accessed | tf_op | source)
XLA Modules:
  0.0 57.9 jit_solution(8885778941158887731)
XLA Ops:
  0.6 0.0 copy-start
  0.6 0.8 %copy-done = s32[16,1024]{1,0:T(8,128)S(1)} copy-done((s32[16,1024]{1,0:T(8,128)S(1)}, s32[16,1024]{1,0:T(8,128)}, u32[]{:S(2)}) %copy-start) | copy-done | bytes 65560
  1.5 0.0 copy-start.1
  1.5 0.8 %copy-done.1 = f32[16,1024]{1,0:T(8,128)S(1)} copy-done((f32[16,1024]{1,0:T(8,128)S(1)}, f32[16,1024]{1,0:T(8,128)}, u32[]{:S(2)}) %copy-start.1) | copy-done | bytes 65560
  2.3 0.0 copy-start.2
  2.3 0.8 %copy-done.2 = f32[16,1024]{1,0:T(8,128)S(1)} copy-done((f32[16,1024]{1,0:T(8,128)S(1)}, f32[16,1024]{1,0:T(8,128)}, u32[]{:S(2)}) %copy-start.2) | copy-done | bytes 65560
  3.2 0.0 copy-start.3
  3.2 0.8 %copy-done.3 = f32[1,16,1024]{2,1,0:T(8,128)S(1)} copy-done((f32[1,16,1024]{2,1,0:T(8,128)S(1)}, f32[1,16,1024]{2,1,0:T(8,128)}, u32[]{:S(2)}) %copy-start.3) | copy-done | bytes 65560
  4.0 0.0 copy-start.5
  4.0 0.7 %copy-done.5 = f32[4]{0:T(128)S(1)} copy-done((f32[4]{0:T(128)S(1)}, f32[4]{0:T(128)}, u32[]{:S(2)}) %copy-start.5) | copy-done | bytes 40
  4.6 1.1 %plain.1 = (f32[8,2,8,128]{3,2,1,0:T(8,128)S(1)}, f32[8,2,8,128]{3,2,1,0:T(8,128)S(1)}, f32[8,2,8,128]{3,2,1,0:T(8,128)S(1)}, f32[8,2,8,128]{3,2,1,0:T(8,128)S(1)}) custom-call(s32[16,1024]{1,0:T(8,128)S(1)} %copy-done, f32[4]{0:T(128)S(1)} %copy-done.5, f32[16,1024]{1,0:T(8,128)S(1)} %copy-done.1, f32[16,1024]{1,0:T(8,128)S(1)} %copy-done.2, ...), custom_call_target="tpu_custom_call" | custom-call | tf_op jit(solution)/shard_map/plain/pallas_call | solution.py:353
  5.7 0.3 coef_dir.1
  6.0 0.0 copy-start.4
  6.0 0.7 %copy-done.4 = f32[16]{0:T(128)S(1)} copy-done((f32[16]{0:T(128)S(1)}, f32[16]{0:T(128)}, u32[]{:S(2)}) %copy-start.4) | copy-done | bytes 88
  6.7 4.8 %dir0.1 = (f32[8,2,8,128]{3,2,1,0:T(8,128)S(1)}, f32[128,128]{1,0:T(8,128)S(1)}, f32[128,128]{1,0:T(8,128)S(1)}) custom-call(f32[8,2,8,128]{3,2,1,0:T(8,128)S(1)} %get-tuple-element.24.refs_0_, f32[14,7,8,128]{3,2,1,0:T(8,128)S(1)} %get-tuple-element.28.refs_1_, f32[14,6,8,128]{3,2,1,0:T(8,128)S(1)} %get-tuple-element.29.refs_2_, ...), custom_call_target="tpu_custom_call" | custom-call | tf_op jit(solution)/shard_map/dir0/pallas_call | solution.py:353
  11.5 1.6 %collective-permute-start.1 = (f32[128,128]{1,0:T(8,128)S(1)}, f32[128,128]{1,0:T(8,128)S(1)}, u32[]{:S(2)}, u32[]{:S(2)}) collective-permute-start(f32[128,128]{1,0:T(8,128)S(1)} %get-tuple-element.36.refs_3_), channel_id=1, source_target_pairs={{0,1},{1,0},{2,3},{3,2},{4,5},{5,4},{6,7},{7,6},{8,9},{9,8},{10,11... | collective-permute-start | bytes 196616 | tf_op jit(solution)/shard_map/ppermute | solution.py:383
  13.1 1.9 %collective-permute-start.2 = (f32[128,128]{1,0:T(8,128)S(1)}, f32[128,128]{1,0:T(8,128)S(1)}, u32[]{:S(2)}, u32[]{:S(2)}) collective-permute-start(f32[128,128]{1,0:T(8,128)S(1)} %get-tuple-element.37.refs_4_), channel_id=1, source_target_pairs={{1,2},{2,1},{3,4},{4,3},{5,6},{6,5},{0,0},{7,7},{9,10},{10,9},{11,... | collective-permute-start | bytes 196616 | tf_op jit(solution)/shard_map/ppermute | solution.py:383
  15.0 0.1 collective-permute-start
  15.1 0.8 %coef_neu.1 = (f32[14,7,8,128]{3,2,1,0:T(8,128)S(1)}, f32[14,6,8,128]{3,2,1,0:T(8,128)S(1)}, f32[8,2,8,128]{3,2,1,0:T(8,128)}, f32[4,8,128]{2,1,0:T(8,128)S(1)}) custom-call(f32[8,2,8,128]{3,2,1,0:T(8,128)S(1)} %get-tuple-element.25.nu_ref, f32[8,2,8,128]{3,2,1,0:T(8,128)S(1)} %get-tuple-element.26.sigma_ref, f32[8,2,8,128]{3,2,1,0:T(8,128)S(1)} %get-tuple-element.27.coil_ref), custom_call_target="tpu_custom_call" | custom-call | tf_op jit(solution)/shard_map/coef_neu/pallas_call | solution.py:353
  15.9 0.0 collective-permute-done.1.refs_5_
  15.9 4.2 %collective-permute-done.2.refs_6_ = f32[128,128]{1,0:T(8,128)S(1)} collective-permute-done((f32[128,128]{1,0:T(8,128)S(1)}, f32[128,128]{1,0:T(8,128)S(1)}, u32[]{:S(2)}, u32[]{:S(2)}) %collective-permute-start.2) | collective-permute-done | bytes 65568 | tf_op jit(solution)/shard_map/ppermute | solution.py:383
  20.2 4.4 %neu0.1 = (f32[128,128]{1,0:T(8,128)S(1)}, f32[128,128]{1,0:T(8,128)S(1)}) custom-call(f32[14,7,8,128]{3,2,1,0:T(8,128)S(1)} %get-tuple-element.33.refs_0_, f32[14,6,8,128]{3,2,1,0:T(8,128)S(1)} %get-tuple-element.34.refs_1_, f32[4,8,128]{2,1,0:T(8,128)S(1)} %get-tuple-element.35.refs_2_, f32[128,128]{1,0:T(8,128)S(1)} %get-tuple-element.36.refs_3_, ...), custom_call_target="tpu_custom_call" | custom-call | tf_op jit(solution)/shard_map/neu0/pallas_call | solution.py:353
  24.6 0.6 collective-permute-start.3
  25.1 1.9 %collective-permute-start.4 = (f32[128,128]{1,0:T(8,128)S(1)}, f32[128,128]{1,0:T(8,128)S(1)}, u32[]{:S(2)}, u32[]{:S(2)}) collective-permute-start(f32[128,128]{1,0:T(8,128)S(1)} %get-tuple-element.39.refs_7_), channel_id=1, source_target_pairs={{1,2},{2,1},{3,4},{4,3},{5,6},{6,5},{0,0},{7,7},{9,10},{10,9},{11,... | collective-permute-start | bytes 196616 | tf_op jit(solution)/shard_map/ppermute | solution.py:383
  27.1 0.0 collective-permute-done.refs_0_
  27.1 1.8 %collective-permute-done.3.refs_8_ = f32[128,128]{1,0:T(8,128)S(1)} collective-permute-done((f32[128,128]{1,0:T(8,128)S(1)}, f32[128,128]{1,0:T(8,128)S(1)}, u32[]{:S(2)}, u32[]{:S(2)}) %collective-permute-start.3) | collective-permute-done | bytes 65568 | tf_op jit(solution)/shard_map/ppermute | solution.py:383
  28.9 3.3 %collective-permute-done.4.refs_9_ = f32[128,128]{1,0:T(8,128)S(1)} collective-permute-done((f32[128,128]{1,0:T(8,128)S(1)}, f32[128,128]{1,0:T(8,128)S(1)}, u32[]{:S(2)}, u32[]{:S(2)}) %collective-permute-start.4) | collective-permute-done | bytes 65568 | tf_op jit(solution)/shard_map/ppermute | solution.py:383
  32.2 5.7 %dir1.1 = (f32[8,2,8,128]{3,2,1,0:T(8,128)S(1)}, f32[128,128]{1,0:T(8,128)S(1)}, f32[128,128]{1,0:T(8,128)S(1)}, f32[128,128]{1,0:T(8,128)}, f32[128,128]{1,0:T(8,128)S(1)}) custom-call(f32[8,2,8,128]{3,2,1,0:T(8,128)S(1)} %collective-permute-done.refs_0_, f32[14,7,8,128]{3,2,1,0:T(8,128)S(1)} %get-tuple-element.28.refs_1_, ...), custom_call_target="tpu_custom_call" | custom-call | tf_op jit(solution)/shard_map/dir1/pallas_call | solution.py:353
  37.9 1.5 %collective-permute-start.5 = (f32[128,128]{1,0:T(8,128)S(1)}, f32[128,128]{1,0:T(8,128)S(1)}, u32[]{:S(2)}, u32[]{:S(2)}) collective-permute-start(f32[128,128]{1,0:T(8,128)S(1)} %get-tuple-element.41.refs_3_), channel_id=1, source_target_pairs={{0,1},{1,0},{2,3},{3,2},{4,5},{5,4},{6,7},{7,6},{8,9},{9,8},{10,11... | collective-permute-start | bytes 196616 | tf_op jit(solution)/shard_map/ppermute | solution.py:383
  39.4 1.9 %collective-permute-start.6 = (f32[128,128]{1,0:T(8,128)S(1)}, f32[128,128]{1,0:T(8,128)S(1)}, u32[]{:S(2)}, u32[]{:S(2)}) collective-permute-start(f32[128,128]{1,0:T(8,128)S(1)} %get-tuple-element.42.refs_4_), channel_id=1, source_target_pairs={{1,2},{2,1},{3,4},{4,3},{5,6},{6,5},{0,0},{7,7},{9,10},{10,9},{11,... | collective-permute-start | bytes 196616 | tf_op jit(solution)/shard_map/ppermute | solution.py:383
  41.3 1.5 %collective-permute-done.5.refs_5_ = f32[128,128]{1,0:T(8,128)S(1)} collective-permute-done((f32[128,128]{1,0:T(8,128)S(1)}, f32[128,128]{1,0:T(8,128)S(1)}, u32[]{:S(2)}, u32[]{:S(2)}) %collective-permute-start.5) | collective-permute-done | bytes 65568 | tf_op jit(solution)/shard_map/ppermute | solution.py:383
  42.8 3.6 %collective-permute-done.6.refs_6_ = f32[128,128]{1,0:T(8,128)S(1)} collective-permute-done((f32[128,128]{1,0:T(8,128)S(1)}, f32[128,128]{1,0:T(8,128)S(1)}, u32[]{:S(2)}, u32[]{:S(2)}) %collective-permute-start.6) | collective-permute-done | bytes 65568 | tf_op jit(solution)/shard_map/ppermute | solution.py:383
  46.4 4.7 %neu1.1 = (f32[16,1024]{1,0:T(8,128)S(1)}, f32[16,1024]{1,0:T(8,128)S(1)}) custom-call(f32[14,7,8,128]{3,2,1,0:T(8,128)S(1)} %get-tuple-element.33.refs_0_, f32[14,6,8,128]{3,2,1,0:T(8,128)S(1)} %get-tuple-element.34.refs_1_, f32[4,8,128]{2,1,0:T(8,128)S(1)} %get-tuple-element.35.refs_2_, f32[128,128]{1,0:T(8,128)S(1)} %get-tuple-element.41.refs_3_, ...), custom_call_target="tpu_custom_call" | custom-call | tf_op jit(solution)/shard_map/neu1/pallas_call | solution.py:353
  51.1 1.9 %collective-permute-start.7 = (f32[16,1024]{1,0:T(8,128)S(1)}, f32[16,1024]{1,0:T(8,128)S(1)}, u32[]{:S(2)}, u32[]{:S(2)}) collective-permute-start(f32[16,1024]{1,0:T(8,128)S(1)} %get-tuple-element.45), channel_id=1, source_target_pairs={{1,0},{2,1},{3,2},{4,3},{5,4},{6,5},{7,6},{9,8},{10,9},{11,10},{12... | collective-permute-start | bytes 196616 | tf_op jit(solution)/shard_map/ppermute | solution.py:408
  53.1 0.9 %natural.1 = f32[1,16,1024]{2,1,0:T(8,128)} custom-call(f32[8,2,8,128]{3,2,1,0:T(8,128)S(1)} %get-tuple-element.40.ends_ref), custom_call_target="tpu_custom_call" | custom-call | tf_op jit(solution)/shard_map/natural/pallas_call | solution.py:353
  54.0 3.3 %collective-permute-done.7.got_ref = f32[16,1024]{1,0:T(8,128)S(1)} collective-permute-done((f32[16,1024]{1,0:T(8,128)S(1)}, f32[16,1024]{1,0:T(8,128)S(1)}, u32[]{:S(2)}, u32[]{:S(2)}) %collective-permute-start.7) | collective-permute-done | bytes 65568 | tf_op jit(solution)/shard_map/ppermute | solution.py:408
  57.3 0.6 %join.1 = f32[16,1024]{1,0:T(8,128)} custom-call(f32[16,1024]{1,0:T(8,128)S(1)} %get-tuple-element.44.mine_ref, f32[16,1024]{1,0:T(8,128)S(1)} %collective-permute-done.7.got_ref), custom_call_target="tpu_custom_call" | custom-call | tf_op jit(solution)/shard_map/join/pallas_call | solution.py:353
Async XLA Ops:
  0.6 0.8 %copy-start = (s32[16,1024]{1,0:T(8,128)S(1)}, s32[16,1024]{1,0:T(8,128)}, u32[]{:S(2)}) copy-start(s32[16,1024]{1,0:T(8,128)} %labels_ref.1) | copy-start | bytes 196612
  1.5 0.8 %copy-start.1 = (f32[16,1024]{1,0:T(8,128)S(1)}, f32[16,1024]{1,0:T(8,128)}, u32[]{:S(2)}) copy-start(f32[16,1024]{1,0:T(8,128)} %sigma_ref.1) | copy-start | bytes 196612
  2.3 0.8 %copy-start.2 = (f32[16,1024]{1,0:T(8,128)S(1)}, f32[16,1024]{1,0:T(8,128)}, u32[]{:S(2)}) copy-start(f32[16,1024]{1,0:T(8,128)} %coil_ref.1) | copy-start | bytes 196612
  3.2 0.8 %copy-start.3 = (f32[1,16,1024]{2,1,0:T(8,128)S(1)}, f32[1,16,1024]{2,1,0:T(8,128)}, u32[]{:S(2)}) copy-start(f32[1,16,1024]{2,1,0:T(8,128)} %start_ref.1) | copy-start | bytes 196612
  4.0 0.7 %copy-start.5 = (f32[4]{0:T(128)S(1)}, f32[4]{0:T(128)}, u32[]{:S(2)}) copy-start(f32[4]{0:T(128)} %table_ref.1) | copy-start | bytes 52
  6.0 0.7 %copy-start.4 = (f32[16]{0:T(128)S(1)}, f32[16]{0:T(128)}, u32[]{:S(2)}) copy-start(f32[16]{0:T(128)} %refs_5_.3) | copy-start | bytes 196
  11.5 4.4 %collective-permute-start.1 = (f32[128,128]{1,0:T(8,128)S(1)}, f32[128,128]{1,0:T(8,128)S(1)}, u32[]{:S(2)}, u32[]{:S(2)}) collective-permute-start(f32[128,128]{1,0:T(8,128)S(1)} %get-tuple-element.36.refs_3_), channel_id=1, source_target_pairs={{0,1},{1,0},{2,3},{3,2},{4,5},{5,4},{6,7},{7,6},{8,9},{9,8},{10,11... | collective-permute-start | bytes 196616 | tf_op jit(solution)/shard_map/ppermute | solution.py:383
  13.1 7.0 %collective-permute-start.2 = (f32[128,128]{1,0:T(8,128)S(1)}, f32[128,128]{1,0:T(8,128)S(1)}, u32[]{:S(2)}, u32[]{:S(2)}) collective-permute-start(f32[128,128]{1,0:T(8,128)S(1)} %get-tuple-element.37.refs_4_), channel_id=1, source_target_pairs={{1,2},{2,1},{3,4},{4,3},{5,6},{6,5},{0,0},{7,7},{9,10},{10,9},{11,... | collective-permute-start | bytes 196616 | tf_op jit(solution)/shard_map/ppermute | solution.py:383
  15.0 12.0 %collective-permute-start = (f32[8,2,8,128]{3,2,1,0:T(8,128)S(1)}, f32[8,2,8,128]{3,2,1,0:T(8,128)S(1)}, u32[]{:S(2)}, u32[]{:S(2)}) collective-permute-start(f32[8,2,8,128]{3,2,1,0:T(8,128)S(1)} %get-tuple-element.32), channel_id=1, source_target_pairs={{0,8},{8,16},{16,24},{24,0},{1,9},{9,17},{17,25},{25,1},{2,10},{10... | collective-permute-start | bytes 196616 | tf_op jit(solution)/shard_map/ppermute | solution.py:389
  24.6 4.3 %collective-permute-start.3 = (f32[128,128]{1,0:T(8,128)S(1)}, f32[128,128]{1,0:T(8,128)S(1)}, u32[]{:S(2)}, u32[]{:S(2)}) collective-permute-start(f32[128,128]{1,0:T(8,128)S(1)} %get-tuple-element.38.refs_6_), channel_id=1, source_target_pairs={{0,1},{1,0},{2,3},{3,2},{4,5},{5,4},{6,7},{7,6},{8,9},{9,8},{10,11... | collective-permute-start | bytes 196616 | tf_op jit(solution)/shard_map/ppermute | solution.py:383
  25.1 7.0 %collective-permute-start.4 = (f32[128,128]{1,0:T(8,128)S(1)}, f32[128,128]{1,0:T(8,128)S(1)}, u32[]{:S(2)}, u32[]{:S(2)}) collective-permute-start(f32[128,128]{1,0:T(8,128)S(1)} %get-tuple-element.39.refs_7_), channel_id=1, source_target_pairs={{1,2},{2,1},{3,4},{4,3},{5,6},{6,5},{0,0},{7,7},{9,10},{10,9},{11,... | collective-permute-start | bytes 196616 | tf_op jit(solution)/shard_map/ppermute | solution.py:383
  37.9 5.0 %collective-permute-start.5 = (f32[128,128]{1,0:T(8,128)S(1)}, f32[128,128]{1,0:T(8,128)S(1)}, u32[]{:S(2)}, u32[]{:S(2)}) collective-permute-start(f32[128,128]{1,0:T(8,128)S(1)} %get-tuple-element.41.refs_3_), channel_id=1, source_target_pairs={{0,1},{1,0},{2,3},{3,2},{4,5},{5,4},{6,7},{7,6},{8,9},{9,8},{10,11... | collective-permute-start | bytes 196616 | tf_op jit(solution)/shard_map/ppermute | solution.py:383
  39.4 7.0 %collective-permute-start.6 = (f32[128,128]{1,0:T(8,128)S(1)}, f32[128,128]{1,0:T(8,128)S(1)}, u32[]{:S(2)}, u32[]{:S(2)}) collective-permute-start(f32[128,128]{1,0:T(8,128)S(1)} %get-tuple-element.42.refs_4_), channel_id=1, source_target_pairs={{1,2},{2,1},{3,4},{4,3},{5,6},{6,5},{0,0},{7,7},{9,10},{10,9},{11,... | collective-permute-start | bytes 196616 | tf_op jit(solution)/shard_map/ppermute | solution.py:383
  51.1 6.2 %collective-permute-start.7 = (f32[16,1024]{1,0:T(8,128)S(1)}, f32[16,1024]{1,0:T(8,128)S(1)}, u32[]{:S(2)}, u32[]{:S(2)}) collective-permute-start(f32[16,1024]{1,0:T(8,128)S(1)} %get-tuple-element.45), channel_id=1, source_target_pairs={{1,0},{2,1},{3,2},{4,3},{5,4},{6,5},{7,6},{9,8},{10,9},{11,10},{12... | collective-permute-start | bytes 196616 | tf_op jit(solution)/shard_map/ppermute | solution.py:408

commit v2 on v1

--- a/solution.py
+++ b/solution.py
@@ -43,40 +43,37 @@
     return pltpu.roll(tile, 1, 0)
 
 
-def swap_groups(tiles):
-    group = tile_index(1) // 16
-    for bit in (1, 2, 4):
-        new = []
-        for j, tile in enumerate(tiles):
-            other = tiles[j ^ bit]
-            if j & bit:
-                new.append(jnp.where((group & bit) != 0, tile, pltpu.roll(other, LANES - 16 * bit, 1)))
-            else:
-                new.append(jnp.where((group & bit) == 0, tile, pltpu.roll(other, 16 * bit, 1)))
-        tiles = new
-    return tiles
-
-
 def to_blocks(tiles):
     lane = tile_index(1)
-    order = 8 * (lane % 16) + lane // 16
-    return swap_groups([jnp.take_along_axis(tile, order, axis=1) for tile in tiles])
+    out = []
+    for r in range(BLOCK):
+        order = 8 * (lane % 16) + r
+        tile = jnp.take_along_axis(tiles[0], order, axis=1)
+        for j in range(1, BLOCK):
+            tile = jnp.where(lane // 16 == j, jnp.take_along_axis(tiles[j], order, axis=1), tile)
+        out.append(tile)
+    return out
 
 
 def from_blocks(tiles):
     lane = tile_index(1)
-    order = 16 * (lane % 8) + lane // 8
-    return [jnp.take_along_axis(tile, order, axis=1) for tile in swap_groups(tiles)]
-
-
-def load_field(ref, scratch):
+    out = []
     for j in range(BLOCK):
-        scratch[16 * j : 16 * j + 16, :] = ref[:, LANES * j : LANES * j + LANES]
-    halves = [
-        to_blocks([scratch[pl.ds(16 * j + e, SUB, stride=2), :] for j in range(BLOCK)])
-        for e in range(2)
-    ]
-    return halves
+        order = 16 * j + lane // 8
+        tile = jnp.take_along_axis(tiles[0], order, axis=1)
+        for r in range(1, BLOCK):
+            tile = jnp.where(lane % 8 == r, jnp.take_along_axis(tiles[r], order, axis=1), tile)
+        out.append(tile)
+    return out
+
+
+def put_field(value, scratch, out):
+    for j in range(BLOCK):
+        scratch[16 * j : 16 * j + 16, :] = value[:, LANES * j : LANES * j + LANES]
+    for e in range(2):
+        tiles = to_blocks([scratch[pl.ds(16 * j + e, SUB, stride=2), :] for j in range(BLOCK)])
+        for r in range(BLOCK):
+            out[r, e] = tiles[r]
 
 
 def harmonic(first_nu, second_nu):
@@ -101,15 +98,37 @@
     return place % 2 == 0, place > 0, place < count - 1
 
 
-def plain_kernel(labels_ref, table_ref, sigma_ref, coil_ref, start_ref, nu_out, sigma_out, coil_out, start_out, s0, s1, s2, s3):
-    nu = jnp.zeros(labels_ref.shape, F32)
+def first_kernel(
+    labels_hbm, table_hbm, sigma_hbm, coil_hbm, start_hbm, wave_hbm,
+    nu_out, sigma_out, start_out, c_out, r_out, edge_out, scale_out, wave_out,
+    labels_ref, table_ref, sigma_ref, coil_ref, start_ref, wave_ref, cur_ref, s0, s1, s2, s3, sems,
+):
+    copies = [
+        pltpu.make_async_copy(source, target, sems.at[i])
+        for i, (source, target) in enumerate((
+            (table_hbm, table_ref), (labels_hbm, labels_ref), (sigma_hbm, sigma_ref),
+            (coil_hbm, coil_ref), (start_hbm, start_ref), (wave_hbm, wave_ref),
+        ))
+    ]
+    for copy in copies:
+        copy.start()
+    copies[0].wait()
+    copies[1].wait()
+    labels = labels_ref[...]
+    nu = jnp.zeros(labels.shape, F32)
     for material in range(table_ref.shape[0]):
-        nu = nu + jnp.where(labels_ref[...] == material, table_ref[material], 0.0)
-    for value, scratch, out in ((nu, s0, nu_out), (sigma_ref[...], s1, sigma_out), (coil_ref[...], s2, coil_out), (start_ref[0], s3, start_out)):
-        halves = load_field(value, scratch)
-        for e in range(2):
-            for r in range(BLOCK):
-                out[r, e] = halves[e][r]
+        nu = nu + jnp.where(labels == material, table_ref[material], 0.0)
+    put_field(nu, s0, nu_out)
+    copies[2].wait()
+    put_field(sigma_ref[...], s1, sigma_out)
+    copies[3].wait()
+    put_field(coil_ref[...], s2, cur_ref)
+    copies[4].wait()
+    put_field(start_ref[0], s3, start_out)
+    copies[5].wait()
+    for t in range(wave_ref.shape[0]):
+        wave_out[t : t + 1, :] = jnp.full((1, LANES), wave_ref[t], F32)
+    coef_kernel(False, nu_out, sigma_out, cur_ref, c_out, r_out, edge_out, scale_out)
 
 
 def unit_up(r):
@@ -120,7 +139,7 @@
     return r % BLOCK in (2, 4, 6)
 
 
-def coef_kernel(neumann, nu_ref, sigma_ref, coil_ref, c_out, r_out, scale_out, edge_out):
+def coef_kernel(neumann, nu_ref, sigma_ref, coil_ref, c_out, r_out, edge_out, scale_out):
     _, has_left, has_right = flags()
     sub = tile_index(0)
     lane = tile_index(1)
@@ -187,12 +206,17 @@
     put(r_out, FACE_E, [jnp.where((sub == 0) & has_left, rec_e[r], 0.0) for r in span])
     put(r_out, FACE_O, [jnp.where((sub == SUB - 1) & has_right, rec_o[r], 0.0) for r in span])
     for r in range(BLOCK):
-        scale_out[r, 0] = scale_e[r]
-        scale_out[r, 1] = scale_o[r]
+        if not neumann:
+            scale_out[r, 0] = scale_e[r]
+            scale_out[r, 1] = scale_o[r]
         edge_out[0, r : r + 1] = 2.0 * nu_e[r][0:1]
         edge_out[1, r : r + 1] = 2.0 * nu_o[r][SUB - 1 : SUB]
         edge_out[2, r : r + 1] = scale_e[r][0:1]
         edge_out[3, r : r + 1] = scale_o[r][SUB - 1 : SUB]
+
+
+def neumann_coef_kernel(nu_ref, sigma_ref, c_out, r_out, edge_out):
+    coef_kernel(True, nu_ref, sigma_ref, None, c_out, r_out, edge_out, None)
 
 
 def advance(field_e, field_o, rhs, c_ref):
@@ -235,8 +259,9 @@
             b_e = r_ref[i, SIG_E] * now_e[r]
             b_o = r_ref[i, SIG_O] * now_o[r]
             if wave_ref is not None:
-                b_e = b_e + r_ref[i, COIL_E] * wave_ref[t]
-                b_o = b_o + r_ref[i, COIL_O] * wave_ref[t]
+                wave = wave_ref[pl.ds(t, 1), :]
+                b_e = b_e + r_ref[i, COIL_E] * wave
+                b_o = b_o + r_ref[i, COIL_O] * wave
             if left is not None:
                 at = pl.ds(t * 3 * BLOCK + BLOCK + r, 1)
                 b_e = b_e + r_ref[i, FACE_E] * left[at, :]
@@ -248,7 +273,7 @@
             last[pl.ds(t * BLOCK + r, 1), :] = now_o[r][SUB - 1 : SUB]
         return tuple(now_e[r] for r in range(BLOCK)) + tuple(now_o[r] for r in range(BLOCK))
 
-    return lax.fori_loop(0, steps, step, start)
+    return lax.fori_loop(0, steps, step, start, unroll=2)
 
 
 def put_face(ref, t, tile):
@@ -268,7 +293,7 @@
         left = right = None
     else:
         (start_ref, c_ref, r_ref, scale_ref, edge_ref, wave_ref, ev_own, od_own, ev_got, od_got,
-         ends, ev_out, od_out, g_left, g_right, first, last, left, right) = refs
+         ends, ev_out, od_out, g_right, first, last, left, right, g_left) = refs
     even, _, _ = flags()
     if sweep > 0:
         for t in range(steps):
@@ -343,19 +368,15 @@
     out[...] = jnp.where(has_right, mine_ref[...] + got_ref[...], 0.0)
 
 
-def call(kernel, name, inputs, outputs, scratch=(), smem=()):
-    specs = [
-        pl.BlockSpec(memory_space=pltpu.SMEM if i in smem else pltpu.VMEM)
-        for i in range(len(inputs))
-    ]
+def call(kernel, name, inputs, outputs, scratch=(), space=pltpu.VMEM):
     single = not isinstance(outputs, list)
     shapes = [jax.ShapeDtypeStruct(s, F32) for s in ([outputs] if single else outputs)]
     result = pl.pallas_call(
         kernel,
         out_shape=shapes,
-        in_specs=specs,
+        in_specs=[pl.BlockSpec(memory_space=space)] * len(inputs),
         out_specs=[pl.BlockSpec(memory_space=pltpu.VMEM)] * len(shapes),
-        scratch_shapes=[pltpu.VMEM(s, F32) for s in scratch],
+        scratch_shapes=[pltpu.VMEM(s, F32) if isinstance(s, tuple) else s for s in scratch],
         compiler_params=pltpu.CompilerParams(vmem_limit_bytes=6 << 20),
         name=name,
     )(*inputs)
@@ -372,19 +393,24 @@
     field = (BLOCK, 2, SUB, LANES)
     series = (steps * BLOCK, LANES)
     wide = (3 * steps * BLOCK, LANES)
-    nu, sig, cur, state = call(
-        plain_kernel, "plain", [labels, nu_table, sigma, coil, start_states], [field] * 4, [(128, LANES)] * 4, smem=(1,)
-    )
-    shapes = [(ROWS, 7, SUB, LANES), (ROWS, 6, SUB, LANES), field, (4, BLOCK, LANES)]
-    c_dir, r_dir, scale_dir, edge_dir = call(functools.partial(coef_kernel, False), "coef_dir", [nu, sig, cur], shapes)
-    c_neu, r_neu, _, edge_neu = call(functools.partial(coef_kernel, True), "coef_neu", [nu, sig, cur], shapes)
+    coefs = [(ROWS, 7, SUB, LANES), (ROWS, 6, SUB, LANES), (4, BLOCK, LANES)]
+    nu, sig, state, c_dir, r_dir, edge_dir, scale_dir, wave = call(
+        first_kernel, "first", [labels, nu_table, sigma, coil, start_states, waveform],
+        [field, field, field, coefs[0], coefs[1], coefs[2], field, (steps, LANES)],
+        [
+            pltpu.VMEM(labels.shape, jnp.int32), pltpu.SMEM(nu_table.shape, F32), sigma.shape, coil.shape,
+            start_states.shape, pltpu.SMEM(waveform.shape, F32), field,
+        ] + [(128, LANES)] * 4 + [pltpu.SemaphoreType.DMA((6,))],
+        space=pltpu.HBM,
+    )
+    c_neu, r_neu, edge_neu = call(neumann_coef_kernel, "coef_neu", [nu, sig], coefs)
 
     def swapped(ev, od):
         return lax.ppermute(ev, "space", even_faces), lax.ppermute(od, "space", odd_faces)
 
     ends, ev, od = call(
         functools.partial(dirichlet_kernel, 0, steps), "dir0",
-        [state, c_dir, r_dir, scale_dir, edge_dir, waveform], [field, series, series], [series] * 2, smem=(5,),
+        [state, c_dir, r_dir, scale_dir, edge_dir, wave], [field, series, series], [series] * 2,
     )
     state = lax.ppermute(ends, "tm", [(i, (i + 1) % windows) for i in range(windows)])
     ev_got, od_got = swapped(ev, od)
@@ -393,10 +419,10 @@
         [c_neu, r_neu, edge_neu, ev, od, ev_got, od_got], [series] * 2, [series] * 2 + [wide] * 2,
     )
     ev_got, od_got = swapped(ev, od)
-    ends, ev, od, _, g_right = call(
+    ends, ev, od, g_right = call(
         functools.partial(dirichlet_kernel, 1, steps), "dir1",
-        [state, c_dir, r_dir, scale_dir, edge_dir, waveform, ev, od, ev_got, od_got],
-        [field, series, series, series, series], [series] * 2 + [wide] * 2, smem=(5,),
+        [state, c_dir, r_dir, scale_dir, edge_dir, wave, ev, od, ev_got, od_got],
+        [field, series, series, series], [series] * 2 + [wide] * 2 + [series],
     )
     ev_got, od_got = swapped(ev, od)
     end_states = call(natural_kernel, "natural", [ends], (1, columns, rows), [(128, LANES)])

time: 58.3 us -> 56.8 us (0.974)
  Pallas kernels: 23.4 us -> 21.3 us
    pallas_call x9 -> x8, Pallas kernels: 23.4 us -> 21.3 us  [call(): pl.pallas_call(kernel, out_shape=shapes, in_specs=[pl.BlockSpec(memory_sp...]
  transfers between devices with their start and end apart: 8 -> 8, of which waited for: 6 -> 7; matrix products, arithmetic and copies ran while one was open for 0% -> 0% of each run, Pallas kernels for 11% -> 10%
where the time goes in v2:
time: 56.8 us; the launch traced here: 56.5 us
  Pallas kernels  21.3 us (38%)
  waiting for transfers between devices  18.3 us (32%)
  starting transfers between devices  11.4 us (20%)
  local copies, waits for them, and re-layouts  4.66 us (8%)
  between operations  0.73 us (1%)
    pallas_call x8, Pallas kernels, call(): pl.pallas_call(kernel, out_shape=shapes, in_specs=[pl.BlockSpec(memory_sp...  21.3 us
    ppermute x3, waiting for transfers between devices, swapped(): lax.ppermute(od, 'space', odd_faces)  11.2 us
    ppermute x3, starting transfers between devices, swapped(): lax.ppermute(od, 'space', odd_faces)  5.73 us
    unnamed x12, local copies, waits for them, and re-layouts  4.66 us
    ppermute x3, waiting for transfers between devices, swapped(): lax.ppermute(ev, 'space', even_faces)  3.82 us
    ppermute x3, starting transfers between devices, swapped(): lax.ppermute(ev, 'space', even_faces)  3.74 us
    ppermute x1, waiting for transfers between devices, body(): got = lax.ppermute(first, 'space', [(i, i - 1) for i in range(1, count)])  3.32 us
    ppermute x1, starting transfers between devices, body(): got = lax.ppermute(first, 'space', [(i, i - 1) for i in range(1, count)])  1.92 us
  transfers between devices with their start and end apart: 8, of which 7 were waited for; matrix products, arithmetic and copies ran while one was open for 0% of the time, Pallas kernels for 10%

profile of v2, /device:TPU:8, one launch (start us, length us, event | category | flops | bytes accessed | tf_op | source)
XLA Modules:
  0.0 56.5 jit_solution(12192167515464583074)
XLA Ops:
  0.6 0.0 copy-start
  0.6 0.8 %copy-done = s32[16,1024]{1,0:T(8,128)S(1)} copy-done((s32[16,1024]{1,0:T(8,128)S(1)}, s32[16,1024]{1,0:T(8,128)}, u32[]{:S(2)}) %copy-start) | copy-done | bytes 65560
  1.5 0.0 copy-start.1
  1.5 0.8 %copy-done.1 = f32[16,1024]{1,0:T(8,128)S(1)} copy-done((f32[16,1024]{1,0:T(8,128)S(1)}, f32[16,1024]{1,0:T(8,128)}, u32[]{:S(2)}) %copy-start.1) | copy-done | bytes 65560
  2.3 0.0 copy-start.2
  2.3 0.8 %copy-done.2 = f32[16,1024]{1,0:T(8,128)S(1)} copy-done((f32[16,1024]{1,0:T(8,128)S(1)}, f32[16,1024]{1,0:T(8,128)}, u32[]{:S(2)}) %copy-start.2) | copy-done | bytes 65560
  3.2 0.0 copy-start.3
  3.2 0.8 %copy-done.3 = f32[1,16,1024]{2,1,0:T(8,128)S(1)} copy-done((f32[1,16,1024]{2,1,0:T(8,128)S(1)}, f32[1,16,1024]{2,1,0:T(8,128)}, u32[]{:S(2)}) %copy-start.3) | copy-done | bytes 65560
  4.0 0.0 copy-start.4
  4.0 0.7 %copy-done.4 = f32[4]{0:T(128)S(1)} copy-done((f32[4]{0:T(128)S(1)}, f32[4]{0:T(128)}, u32[]{:S(2)}) %copy-start.4) | copy-done | bytes 40
  4.6 0.0 copy-start.5
  4.7 0.7 %copy-done.5 = f32[16]{0:T(128)S(1)} copy-done((f32[16]{0:T(128)S(1)}, f32[16]{0:T(128)}, u32[]{:S(2)}) %copy-start.5) | copy-done | bytes 88
  5.3 2.0 %first.1 = (f32[8,2,8,128]{3,2,1,0:T(8,128)S(1)}, f32[8,2,8,128]{3,2,1,0:T(8,128)S(1)}, f32[8,2,8,128]{3,2,1,0:T(8,128)S(1)}, f32[14,7,8,128]{3,2,1,0:T(8,128)S(...) custom-call(s32[16,1024]{1,0:T(8,128)S(1)} %copy-done, ...), custom_call_target="tpu_custom_call" | custom-call | tf_op jit(solution)/shard_map/first/pallas_call | solution.py:374
  7.3 4.0 %dir0.1 = (f32[8,2,8,128]{3,2,1,0:T(8,128)S(1)}, f32[128,128]{1,0:T(8,128)S(1)}, f32[128,128]{1,0:T(8,128)S(1)}) custom-call(f32[8,2,8,128]{3,2,1,0:T(8,128)S(1)} %get-tuple-element.24.refs_0_, f32[14,7,8,128]{3,2,1,0:T(8,128)S(1)} %get-tuple-element.25.refs_1_, f32[14,6,8,128]{3,2,1,0:T(8,128)S(1)} %get-tuple-element.26.refs_2_, ...), custom_call_target="tpu_custom_call" | custom-call | tf_op jit(solution)/shard_map/dir0/pallas_call | solution.py:374
  11.3 1.6 %collective-permute-start.1 = (f32[128,128]{1,0:T(8,128)S(1)}, f32[128,128]{1,0:T(8,128)S(1)}, u32[]{:S(2)}, u32[]{:S(2)}) collective-permute-start(f32[128,128]{1,0:T(8,128)S(1)} %get-tuple-element.36.refs_3_), channel_id=1, source_target_pairs={{0,1},{1,0},{2,3},{3,2},{4,5},{5,4},{6,7},{7,6},{8,9},{9,8},{10,11... | collective-permute-start | bytes 196616 | tf_op jit(solution)/shard_map/ppermute | solution.py:409
  12.9 1.9 %collective-permute-start.2 = (f32[128,128]{1,0:T(8,128)S(1)}, f32[128,128]{1,0:T(8,128)S(1)}, u32[]{:S(2)}, u32[]{:S(2)}) collective-permute-start(f32[128,128]{1,0:T(8,128)S(1)} %get-tuple-element.37.refs_4_), channel_id=1, source_target_pairs={{1,2},{2,1},{3,4},{4,3},{5,6},{6,5},{0,0},{7,7},{9,10},{10,9},{11,... | collective-permute-start | bytes 196616 | tf_op jit(solution)/shard_map/ppermute | solution.py:409
  14.8 0.1 collective-permute-start
  14.9 0.3 coef_neu.1
  15.2 0.5 collective-permute-done.1.refs_5_
  15.7 4.3 %collective-permute-done.2.refs_6_ = f32[128,128]{1,0:T(8,128)S(1)} collective-permute-done((f32[128,128]{1,0:T(8,128)S(1)}, f32[128,128]{1,0:T(8,128)S(1)}, u32[]{:S(2)}, u32[]{:S(2)}) %collective-permute-start.2) | collective-permute-done | bytes 65568 | tf_op jit(solution)/shard_map/ppermute | solution.py:409
  20.0 4.4 %neu0.1 = (f32[128,128]{1,0:T(8,128)S(1)}, f32[128,128]{1,0:T(8,128)S(1)}) custom-call(f32[14,7,8,128]{3,2,1,0:T(8,128)S(1)} %get-tuple-element.33.refs_0_, f32[14,6,8,128]{3,2,1,0:T(8,128)S(1)} %get-tuple-element.34.refs_1_, f32[4,8,128]{2,1,0:T(8,128)S(1)} %get-tuple-element.35.refs_2_, f32[128,128]{1,0:T(8,128)S(1)} %get-tuple-element.36.refs_3_, ...), custom_call_target="tpu_custom_call" | custom-call | tf_op jit(solution)/shard_map/neu0/pallas_call | solution.py:374
  24.3 0.6 %collective-permute-start.3 = (f32[128,128]{1,0:T(8,128)S(1)}, f32[128,128]{1,0:T(8,128)S(1)}, u32[]{:S(2)}, u32[]{:S(2)}) collective-permute-start(f32[128,128]{1,0:T(8,128)S(1)} %get-tuple-element.38.refs_6_), channel_id=1, source_target_pairs={{0,1},{1,0},{2,3},{3,2},{4,5},{5,4},{6,7},{7,6},{8,9},{9,8},{10,11... | collective-permute-start | bytes 196616 | tf_op jit(solution)/shard_map/ppermute | solution.py:409
  24.9 1.9 %collective-permute-start.4 = (f32[128,128]{1,0:T(8,128)S(1)}, f32[128,128]{1,0:T(8,128)S(1)}, u32[]{:S(2)}, u32[]{:S(2)}) collective-permute-start(f32[128,128]{1,0:T(8,128)S(1)} %get-tuple-element.39.refs_7_), channel_id=1, source_target_pairs={{1,2},{2,1},{3,4},{4,3},{5,6},{6,5},{0,0},{7,7},{9,10},{10,9},{11,... | collective-permute-start | bytes 196616 | tf_op jit(solution)/shard_map/ppermute | solution.py:409
  26.8 0.0 collective-permute-done.refs_0_
  26.8 1.8 %collective-permute-done.3.refs_8_ = f32[128,128]{1,0:T(8,128)S(1)} collective-permute-done((f32[128,128]{1,0:T(8,128)S(1)}, f32[128,128]{1,0:T(8,128)S(1)}, u32[]{:S(2)}, u32[]{:S(2)}) %collective-permute-start.3) | collective-permute-done | bytes 65568 | tf_op jit(solution)/shard_map/ppermute | solution.py:409
  28.7 3.3 %collective-permute-done.4.refs_9_ = f32[128,128]{1,0:T(8,128)S(1)} collective-permute-done((f32[128,128]{1,0:T(8,128)S(1)}, f32[128,128]{1,0:T(8,128)S(1)}, u32[]{:S(2)}, u32[]{:S(2)}) %collective-permute-start.4) | collective-permute-done | bytes 65568 | tf_op jit(solution)/shard_map/ppermute | solution.py:409
  32.0 4.2 %dir1.1 = (f32[8,2,8,128]{3,2,1,0:T(8,128)S(1)}, f32[128,128]{1,0:T(8,128)S(1)}, f32[128,128]{1,0:T(8,128)S(1)}, f32[128,128]{1,0:T(8,128)S(1)}) custom-call(f32[8,2,8,128]{3,2,1,0:T(8,128)S(1)} %collective-permute-done.refs_0_, f32[14,7,8,128]{3,2,1,0:T(8,128)S(1)} %get-tuple-element.25.refs_1_, f32[14,6,8,128]{3,2,1,0:T(8,128)S(1)} %get-tuple-element.26.refs_2_, ...), custom_call_target="tpu_custom_call" | custom-call | tf_op jit(solution)/shard_map/dir1/pallas_call | solution.py:374
  36.2 1.6 %collective-permute-start.5 = (f32[128,128]{1,0:T(8,128)S(1)}, f32[128,128]{1,0:T(8,128)S(1)}, u32[]{:S(2)}, u32[]{:S(2)}) collective-permute-start(f32[128,128]{1,0:T(8,128)S(1)} %get-tuple-element.41.refs_3_), channel_id=1, source_target_pairs={{0,1},{1,0},{2,3},{3,2},{4,5},{5,4},{6,7},{7,6},{8,9},{9,8},{10,11... | collective-permute-start | bytes 196616 | tf_op jit(solution)/shard_map/ppermute | solution.py:409
  37.8 1.9 %collective-permute-start.6 = (f32[128,128]{1,0:T(8,128)S(1)}, f32[128,128]{1,0:T(8,128)S(1)}, u32[]{:S(2)}, u32[]{:S(2)}) collective-permute-start(f32[128,128]{1,0:T(8,128)S(1)} %get-tuple-element.42.refs_4_), channel_id=1, source_target_pairs={{1,2},{2,1},{3,4},{4,3},{5,6},{6,5},{0,0},{7,7},{9,10},{10,9},{11,... | collective-permute-start | bytes 196616 | tf_op jit(solution)/shard_map/ppermute | solution.py:409
  39.7 1.5 %collective-permute-done.5.refs_5_ = f32[128,128]{1,0:T(8,128)S(1)} collective-permute-done((f32[128,128]{1,0:T(8,128)S(1)}, f32[128,128]{1,0:T(8,128)S(1)}, u32[]{:S(2)}, u32[]{:S(2)}) %collective-permute-start.5) | collective-permute-done | bytes 65568 | tf_op jit(solution)/shard_map/ppermute | solution.py:409
  41.2 3.6 %collective-permute-done.6.refs_6_ = f32[128,128]{1,0:T(8,128)S(1)} collective-permute-done((f32[128,128]{1,0:T(8,128)S(1)}, f32[128,128]{1,0:T(8,128)S(1)}, u32[]{:S(2)}, u32[]{:S(2)}) %collective-permute-start.6) | collective-permute-done | bytes 65568 | tf_op jit(solution)/shard_map/ppermute | solution.py:409
  44.8 4.9 %neu1.1 = (f32[16,1024]{1,0:T(8,128)S(1)}, f32[16,1024]{1,0:T(8,128)S(1)}) custom-call(f32[14,7,8,128]{3,2,1,0:T(8,128)S(1)} %get-tuple-element.33.refs_0_, f32[14,6,8,128]{3,2,1,0:T(8,128)S(1)} %get-tuple-element.34.refs_1_, f32[4,8,128]{2,1,0:T(8,128)S(1)} %get-tuple-element.35.refs_2_, f32[128,128]{1,0:T(8,128)S(1)} %get-tuple-element.41.refs_3_, ...), custom_call_target="tpu_custom_call" | custom-call | tf_op jit(solution)/shard_map/neu1/pallas_call | solution.py:374
  49.7 1.9 %collective-permute-start.7 = (f32[16,1024]{1,0:T(8,128)S(1)}, f32[16,1024]{1,0:T(8,128)S(1)}, u32[]{:S(2)}, u32[]{:S(2)}) collective-permute-start(f32[16,1024]{1,0:T(8,128)S(1)} %get-tuple-element.45), channel_id=1, source_target_pairs={{1,0},{2,1},{3,2},{4,3},{5,4},{6,5},{7,6},{9,8},{10,9},{11,10},{12... | collective-permute-start | bytes 196616 | tf_op jit(solution)/shard_map/ppermute | solution.py:434
  51.6 0.9 %natural.1 = f32[1,16,1024]{2,1,0:T(8,128)} custom-call(f32[8,2,8,128]{3,2,1,0:T(8,128)S(1)} %get-tuple-element.40.ends_ref), custom_call_target="tpu_custom_call" | custom-call | tf_op jit(solution)/shard_map/natural/pallas_call | solution.py:374
  52.5 3.3 %collective-permute-done.7.got_ref = f32[16,1024]{1,0:T(8,128)S(1)} collective-permute-done((f32[16,1024]{1,0:T(8,128)S(1)}, f32[16,1024]{1,0:T(8,128)S(1)}, u32[]{:S(2)}, u32[]{:S(2)}) %collective-permute-start.7) | collective-permute-done | bytes 65568 | tf_op jit(solution)/shard_map/ppermute | solution.py:434
  55.8 0.6 %join.1 = f32[16,1024]{1,0:T(8,128)} custom-call(f32[16,1024]{1,0:T(8,128)S(1)} %get-tuple-element.44.mine_ref, f32[16,1024]{1,0:T(8,128)S(1)} %collective-permute-done.7.got_ref), custom_call_target="tpu_custom_call" | custom-call | tf_op jit(solution)/shard_map/join/pallas_call | solution.py:374
Async XLA Ops:
  0.6 0.8 %copy-start = (s32[16,1024]{1,0:T(8,128)S(1)}, s32[16,1024]{1,0:T(8,128)}, u32[]{:S(2)}) copy-start(s32[16,1024]{1,0:T(8,128)} %labels_hbm.1) | copy-start | bytes 196612
  1.5 0.8 %copy-start.1 = (f32[16,1024]{1,0:T(8,128)S(1)}, f32[16,1024]{1,0:T(8,128)}, u32[]{:S(2)}) copy-start(f32[16,1024]{1,0:T(8,128)} %sigma_hbm.1) | copy-start | bytes 196612
  2.3 0.8 %copy-start.2 = (f32[16,1024]{1,0:T(8,128)S(1)}, f32[16,1024]{1,0:T(8,128)}, u32[]{:S(2)}) copy-start(f32[16,1024]{1,0:T(8,128)} %coil_hbm.1) | copy-start | bytes 196612
  3.2 0.8 %copy-start.3 = (f32[1,16,1024]{2,1,0:T(8,128)S(1)}, f32[1,16,1024]{2,1,0:T(8,128)}, u32[]{:S(2)}) copy-start(f32[1,16,1024]{2,1,0:T(8,128)} %start_hbm.1) | copy-start | bytes 196612
  4.0 0.7 %copy-start.4 = (f32[4]{0:T(128)S(1)}, f32[4]{0:T(128)}, u32[]{:S(2)}) copy-start(f32[4]{0:T(128)} %table_hbm.1) | copy-start | bytes 52
  4.6 0.7 %copy-start.5 = (f32[16]{0:T(128)S(1)}, f32[16]{0:T(128)}, u32[]{:S(2)}) copy-start(f32[16]{0:T(128)} %wave_hbm.1) | copy-start | bytes 196
  11.3 4.3 %collective-permute-start.1 = (f32[128,128]{1,0:T(8,128)S(1)}, f32[128,128]{1,0:T(8,128)S(1)}, u32[]{:S(2)}, u32[]{:S(2)}) collective-permute-start(f32[128,128]{1,0:T(8,128)S(1)} %get-tuple-element.36.refs_3_), channel_id=1, source_target_pairs={{0,1},{1,0},{2,3},{3,2},{4,5},{5,4},{6,7},{7,6},{8,9},{9,8},{10,11... | collective-permute-start | bytes 196616 | tf_op jit(solution)/shard_map/ppermute | solution.py:409
  12.9 7.0 %collective-permute-start.2 = (f32[128,128]{1,0:T(8,128)S(1)}, f32[128,128]{1,0:T(8,128)S(1)}, u32[]{:S(2)}, u32[]{:S(2)}) collective-permute-start(f32[128,128]{1,0:T(8,128)S(1)} %get-tuple-element.37.refs_4_), channel_id=1, source_target_pairs={{1,2},{2,1},{3,4},{4,3},{5,6},{6,5},{0,0},{7,7},{9,10},{10,9},{11,... | collective-permute-start | bytes 196616 | tf_op jit(solution)/shard_map/ppermute | solution.py:409
  14.8 12.0 %collective-permute-start = (f32[8,2,8,128]{3,2,1,0:T(8,128)S(1)}, f32[8,2,8,128]{3,2,1,0:T(8,128)S(1)}, u32[]{:S(2)}, u32[]{:S(2)}) collective-permute-start(f32[8,2,8,128]{3,2,1,0:T(8,128)S(1)} %get-tuple-element.30), channel_id=1, source_target_pairs={{0,8},{8,16},{16,24},{24,0},{1,9},{9,17},{17,25},{25,1},{2,10},{10... | collective-permute-start | bytes 196616 | tf_op jit(solution)/shard_map/ppermute | solution.py:415
  24.3 4.3 %collective-permute-start.3 = (f32[128,128]{1,0:T(8,128)S(1)}, f32[128,128]{1,0:T(8,128)S(1)}, u32[]{:S(2)}, u32[]{:S(2)}) collective-permute-start(f32[128,128]{1,0:T(8,128)S(1)} %get-tuple-element.38.refs_6_), channel_id=1, source_target_pairs={{0,1},{1,0},{2,3},{3,2},{4,5},{5,4},{6,7},{7,6},{8,9},{9,8},{10,11... | collective-permute-start | bytes 196616 | tf_op jit(solution)/shard_map/ppermute | solution.py:409
  24.9 7.0 %collective-permute-start.4 = (f32[128,128]{1,0:T(8,128)S(1)}, f32[128,128]{1,0:T(8,128)S(1)}, u32[]{:S(2)}, u32[]{:S(2)}) collective-permute-start(f32[128,128]{1,0:T(8,128)S(1)} %get-tuple-element.39.refs_7_), channel_id=1, source_target_pairs={{1,2},{2,1},{3,4},{4,3},{5,6},{6,5},{0,0},{7,7},{9,10},{10,9},{11,... | collective-permute-start | bytes 196616 | tf_op jit(solution)/shard_map/ppermute | solution.py:409
  36.2 5.0 %collective-permute-start.5 = (f32[128,128]{1,0:T(8,128)S(1)}, f32[128,128]{1,0:T(8,128)S(1)}, u32[]{:S(2)}, u32[]{:S(2)}) collective-permute-start(f32[128,128]{1,0:T(8,128)S(1)} %get-tuple-element.41.refs_3_), channel_id=1, source_target_pairs={{0,1},{1,0},{2,3},{3,2},{4,5},{5,4},{6,7},{7,6},{8,9},{9,8},{10,11... | collective-permute-start | bytes 196616 | tf_op jit(solution)/shard_map/ppermute | solution.py:409
  37.8 7.0 %collective-permute-start.6 = (f32[128,128]{1,0:T(8,128)S(1)}, f32[128,128]{1,0:T(8,128)S(1)}, u32[]{:S(2)}, u32[]{:S(2)}) collective-permute-start(f32[128,128]{1,0:T(8,128)S(1)} %get-tuple-element.42.refs_4_), channel_id=1, source_target_pairs={{1,2},{2,1},{3,4},{4,3},{5,6},{6,5},{0,0},{7,7},{9,10},{10,9},{11,... | collective-permute-start | bytes 196616 | tf_op jit(solution)/shard_map/ppermute | solution.py:409
  49.7 6.2 %collective-permute-start.7 = (f32[16,1024]{1,0:T(8,128)S(1)}, f32[16,1024]{1,0:T(8,128)S(1)}, u32[]{:S(2)}, u32[]{:S(2)}) collective-permute-start(f32[16,1024]{1,0:T(8,128)S(1)} %get-tuple-element.45), channel_id=1, source_target_pairs={{1,0},{2,1},{3,2},{4,3},{5,4},{6,5},{7,6},{9,8},{10,9},{11,10},{12... | collective-permute-start | bytes 196616 | tf_op jit(solution)/shard_map/ppermute | solution.py:434

commit v3 on v2

--- a/solution.py
+++ b/solution.py
@@ -395,7 +395,11 @@
     wide = (3 * steps * BLOCK, LANES)
     coefs = [(ROWS, 7, SUB, LANES), (ROWS, 6, SUB, LANES), (4, BLOCK, LANES)]
     nu, sig, state, c_dir, r_dir, edge_dir, scale_dir, wave = call(
-        first_kernel, "first", [labels, nu_table, sigma, coil, start_states, waveform],
+        first_kernel, "first",
+        [
+            pltpu.with_memory_space_constraint(array, pltpu.HBM)
+            for array in (labels, nu_table, sigma, coil, start_states, waveform)
+        ],
         [field, field, field, coefs[0], coefs[1], coefs[2], field, (steps, LANES)],
         [
             pltpu.VMEM(labels.shape, jnp.int32), pltpu.SMEM(nu_table.shape, F32), sigma.shape, coil.shape,

time: 56.8 us -> 52.3 us (0.921)
  local copies, waits for them, and re-layouts: 4.66 us -> 0 us
    unnamed x12 -> x0, local copies, waits for them, and re-layouts: 4.66 us -> none
  transfers between devices with their start and end apart: 8 -> 8, of which waited for: 7 -> 7; matrix products, arithmetic and copies ran while one was open for 0% -> 0% of each run, Pallas kernels for 10% -> 11%
where the time goes in v3:
time: 52.3 us; the launch traced here: 52.1 us
  Pallas kernels  21.6 us (41%)
  waiting for transfers between devices  18.3 us (35%)
  starting transfers between devices  11.4 us (22%)
  between operations  0.72 us (1%)
    pallas_call x8, Pallas kernels, call(): pl.pallas_call(kernel, out_shape=shapes, in_specs=[pl.BlockSpec(memory_sp...  21.6 us
    ppermute x3, waiting for transfers between devices, swapped(): lax.ppermute(od, 'space', odd_faces)  11.2 us
    ppermute x3, starting transfers between devices, swapped(): lax.ppermute(od, 'space', odd_faces)  5.73 us
    ppermute x3, waiting for transfers between devices, swapped(): lax.ppermute(ev, 'space', even_faces)  3.82 us
    ppermute x3, starting transfers between devices, swapped(): lax.ppermute(ev, 'space', even_faces)  3.74 us
    ppermute x1, waiting for transfers between devices, body(): got = lax.ppermute(first, 'space', [(i, i - 1) for i in range(1, count)])  3.32 us
    ppermute x1, starting transfers between devices, body(): got = lax.ppermute(first, 'space', [(i, i - 1) for i in range(1, count)])  1.92 us
  transfers between devices with their start and end apart: 8, of which 7 were waited for; matrix products, arithmetic and copies ran while one was open for 0% of the time, Pallas kernels for 11%

profile of v3, /device:TPU:8, one launch (start us, length us, event | category | flops | bytes accessed | tf_op | source)
XLA Modules:
  0.0 52.1 jit_solution(5403384636684122543)
XLA Ops:
  0.6 2.3 %first.1 = (f32[8,2,8,128]{3,2,1,0:T(8,128)S(1)}, f32[8,2,8,128]{3,2,1,0:T(8,128)S(1)}, f32[8,2,8,128]{3,2,1,0:T(8,128)S(1)}, f32[14,7,8,128]{3,2,1,0:T(8,128)S(...) custom-call(s32[16,1024]{1,0:T(8,128)} %labels_hbm.1, ...), custom_call_target="tpu_custom_call" | custom-call | tf_op jit(solution)/shard_map/first/pallas_call | solution.py:374
  2.9 4.0 %dir0.1 = (f32[8,2,8,128]{3,2,1,0:T(8,128)S(1)}, f32[128,128]{1,0:T(8,128)S(1)}, f32[128,128]{1,0:T(8,128)S(1)}) custom-call(f32[8,2,8,128]{3,2,1,0:T(8,128)S(1)} %get-tuple-element.24.refs_0_, f32[14,7,8,128]{3,2,1,0:T(8,128)S(1)} %get-tuple-element.25.refs_1_, f32[14,6,8,128]{3,2,1,0:T(8,128)S(1)} %get-tuple-element.26.refs_2_, ...), custom_call_target="tpu_custom_call" | custom-call | tf_op jit(solution)/shard_map/dir0/pallas_call | solution.py:374
  7.0 1.6 %collective-permute-start.1 = (f32[128,128]{1,0:T(8,128)S(1)}, f32[128,128]{1,0:T(8,128)S(1)}, u32[]{:S(2)}, u32[]{:S(2)}) collective-permute-start(f32[128,128]{1,0:T(8,128)S(1)} %get-tuple-element.36.refs_3_), channel_id=1, source_target_pairs={{0,1},{1,0},{2,3},{3,2},{4,5},{5,4},{6,7},{7,6},{8,9},{9,8},{10,11... | collective-permute-start | bytes 196616 | tf_op jit(solution)/shard_map/ppermute | solution.py:413
  8.5 1.9 %collective-permute-start.2 = (f32[128,128]{1,0:T(8,128)S(1)}, f32[128,128]{1,0:T(8,128)S(1)}, u32[]{:S(2)}, u32[]{:S(2)}) collective-permute-start(f32[128,128]{1,0:T(8,128)S(1)} %get-tuple-element.37.refs_4_), channel_id=1, source_target_pairs={{1,2},{2,1},{3,4},{4,3},{5,6},{6,5},{0,0},{7,7},{9,10},{10,9},{11,... | collective-permute-start | bytes 196616 | tf_op jit(solution)/shard_map/ppermute | solution.py:413
  10.5 0.1 collective-permute-start
  10.5 0.3 coef_neu.1
  10.8 0.5 collective-permute-done.1.refs_5_
  11.3 4.3 %collective-permute-done.2.refs_6_ = f32[128,128]{1,0:T(8,128)S(1)} collective-permute-done((f32[128,128]{1,0:T(8,128)S(1)}, f32[128,128]{1,0:T(8,128)S(1)}, u32[]{:S(2)}, u32[]{:S(2)}) %collective-permute-start.2) | collective-permute-done | bytes 65568 | tf_op jit(solution)/shard_map/ppermute | solution.py:413
  15.6 4.4 %neu0.1 = (f32[128,128]{1,0:T(8,128)S(1)}, f32[128,128]{1,0:T(8,128)S(1)}) custom-call(f32[14,7,8,128]{3,2,1,0:T(8,128)S(1)} %get-tuple-element.33.refs_0_, f32[14,6,8,128]{3,2,1,0:T(8,128)S(1)} %get-tuple-element.34.refs_1_, f32[4,8,128]{2,1,0:T(8,128)S(1)} %get-tuple-element.35.refs_2_, f32[128,128]{1,0:T(8,128)S(1)} %get-tuple-element.36.refs_3_, ...), custom_call_target="tpu_custom_call" | custom-call | tf_op jit(solution)/shard_map/neu0/pallas_call | solution.py:374
  20.0 0.6 %collective-permute-start.3 = (f32[128,128]{1,0:T(8,128)S(1)}, f32[128,128]{1,0:T(8,128)S(1)}, u32[]{:S(2)}, u32[]{:S(2)}) collective-permute-start(f32[128,128]{1,0:T(8,128)S(1)} %get-tuple-element.38.refs_6_), channel_id=1, source_target_pairs={{0,1},{1,0},{2,3},{3,2},{4,5},{5,4},{6,7},{7,6},{8,9},{9,8},{10,11... | collective-permute-start | bytes 196616 | tf_op jit(solution)/shard_map/ppermute | solution.py:413
  20.5 1.9 %collective-permute-start.4 = (f32[128,128]{1,0:T(8,128)S(1)}, f32[128,128]{1,0:T(8,128)S(1)}, u32[]{:S(2)}, u32[]{:S(2)}) collective-permute-start(f32[128,128]{1,0:T(8,128)S(1)} %get-tuple-element.39.refs_7_), channel_id=1, source_target_pairs={{1,2},{2,1},{3,4},{4,3},{5,6},{6,5},{0,0},{7,7},{9,10},{10,9},{11,... | collective-permute-start | bytes 196616 | tf_op jit(solution)/shard_map/ppermute | solution.py:413
  22.5 0.0 collective-permute-done.refs_0_
  22.5 1.8 %collective-permute-done.3.refs_8_ = f32[128,128]{1,0:T(8,128)S(1)} collective-permute-done((f32[128,128]{1,0:T(8,128)S(1)}, f32[128,128]{1,0:T(8,128)S(1)}, u32[]{:S(2)}, u32[]{:S(2)}) %collective-permute-start.3) | collective-permute-done | bytes 65568 | tf_op jit(solution)/shard_map/ppermute | solution.py:413
  24.3 3.3 %collective-permute-done.4.refs_9_ = f32[128,128]{1,0:T(8,128)S(1)} collective-permute-done((f32[128,128]{1,0:T(8,128)S(1)}, f32[128,128]{1,0:T(8,128)S(1)}, u32[]{:S(2)}, u32[]{:S(2)}) %collective-permute-start.4) | collective-permute-done | bytes 65568 | tf_op jit(solution)/shard_map/ppermute | solution.py:413
  27.6 4.2 %dir1.1 = (f32[8,2,8,128]{3,2,1,0:T(8,128)S(1)}, f32[128,128]{1,0:T(8,128)S(1)}, f32[128,128]{1,0:T(8,128)S(1)}, f32[128,128]{1,0:T(8,128)S(1)}) custom-call(f32[8,2,8,128]{3,2,1,0:T(8,128)S(1)} %collective-permute-done.refs_0_, f32[14,7,8,128]{3,2,1,0:T(8,128)S(1)} %get-tuple-element.25.refs_1_, f32[14,6,8,128]{3,2,1,0:T(8,128)S(1)} %get-tuple-element.26.refs_2_, ...), custom_call_target="tpu_custom_call" | custom-call | tf_op jit(solution)/shard_map/dir1/pallas_call | solution.py:374
  31.8 1.6 %collective-permute-start.5 = (f32[128,128]{1,0:T(8,128)S(1)}, f32[128,128]{1,0:T(8,128)S(1)}, u32[]{:S(2)}, u32[]{:S(2)}) collective-permute-start(f32[128,128]{1,0:T(8,128)S(1)} %get-tuple-element.41.refs_3_), channel_id=1, source_target_pairs={{0,1},{1,0},{2,3},{3,2},{4,5},{5,4},{6,7},{7,6},{8,9},{9,8},{10,11... | collective-permute-start | bytes 196616 | tf_op jit(solution)/shard_map/ppermute | solution.py:413
  33.4 1.9 %collective-permute-start.6 = (f32[128,128]{1,0:T(8,128)S(1)}, f32[128,128]{1,0:T(8,128)S(1)}, u32[]{:S(2)}, u32[]{:S(2)}) collective-permute-start(f32[128,128]{1,0:T(8,128)S(1)} %get-tuple-element.42.refs_4_), channel_id=1, source_target_pairs={{1,2},{2,1},{3,4},{4,3},{5,6},{6,5},{0,0},{7,7},{9,10},{10,9},{11,... | collective-permute-start | bytes 196616 | tf_op jit(solution)/shard_map/ppermute | solution.py:413
  35.3 1.5 %collective-permute-done.5.refs_5_ = f32[128,128]{1,0:T(8,128)S(1)} collective-permute-done((f32[128,128]{1,0:T(8,128)S(1)}, f32[128,128]{1,0:T(8,128)S(1)}, u32[]{:S(2)}, u32[]{:S(2)}) %collective-permute-start.5) | collective-permute-done | bytes 65568 | tf_op jit(solution)/shard_map/ppermute | solution.py:413
  36.8 3.6 %collective-permute-done.6.refs_6_ = f32[128,128]{1,0:T(8,128)S(1)} collective-permute-done((f32[128,128]{1,0:T(8,128)S(1)}, f32[128,128]{1,0:T(8,128)S(1)}, u32[]{:S(2)}, u32[]{:S(2)}) %collective-permute-start.6) | collective-permute-done | bytes 65568 | tf_op jit(solution)/shard_map/ppermute | solution.py:413
  40.4 4.9 %neu1.1 = (f32[16,1024]{1,0:T(8,128)S(1)}, f32[16,1024]{1,0:T(8,128)S(1)}) custom-call(f32[14,7,8,128]{3,2,1,0:T(8,128)S(1)} %get-tuple-element.33.refs_0_, f32[14,6,8,128]{3,2,1,0:T(8,128)S(1)} %get-tuple-element.34.refs_1_, f32[4,8,128]{2,1,0:T(8,128)S(1)} %get-tuple-element.35.refs_2_, f32[128,128]{1,0:T(8,128)S(1)} %get-tuple-element.41.refs_3_, ...), custom_call_target="tpu_custom_call" | custom-call | tf_op jit(solution)/shard_map/neu1/pallas_call | solution.py:374
  45.3 1.9 %collective-permute-start.7 = (f32[16,1024]{1,0:T(8,128)S(1)}, f32[16,1024]{1,0:T(8,128)S(1)}, u32[]{:S(2)}, u32[]{:S(2)}) collective-permute-start(f32[16,1024]{1,0:T(8,128)S(1)} %get-tuple-element.45), channel_id=1, source_target_pairs={{1,0},{2,1},{3,2},{4,3},{5,4},{6,5},{7,6},{9,8},{10,9},{11,10},{12... | collective-permute-start | bytes 196616 | tf_op jit(solution)/shard_map/ppermute | solution.py:438
  47.2 0.9 %natural.1 = f32[1,16,1024]{2,1,0:T(8,128)} custom-call(f32[8,2,8,128]{3,2,1,0:T(8,128)S(1)} %get-tuple-element.40.ends_ref), custom_call_target="tpu_custom_call" | custom-call | tf_op jit(solution)/shard_map/natural/pallas_call | solution.py:374
  48.1 3.3 %collective-permute-done.7.got_ref = f32[16,1024]{1,0:T(8,128)S(1)} collective-permute-done((f32[16,1024]{1,0:T(8,128)S(1)}, f32[16,1024]{1,0:T(8,128)S(1)}, u32[]{:S(2)}, u32[]{:S(2)}) %collective-permute-start.7) | collective-permute-done | bytes 65568 | tf_op jit(solution)/shard_map/ppermute | solution.py:438
  51.4 0.6 %join.1 = f32[16,1024]{1,0:T(8,128)} custom-call(f32[16,1024]{1,0:T(8,128)S(1)} %get-tuple-element.44.mine_ref, f32[16,1024]{1,0:T(8,128)S(1)} %collective-permute-done.7.got_ref), custom_call_target="tpu_custom_call" | custom-call | tf_op jit(solution)/shard_map/join/pallas_call | solution.py:374
Async XLA Ops:
  7.0 4.3 %collective-permute-start.1 = (f32[128,128]{1,0:T(8,128)S(1)}, f32[128,128]{1,0:T(8,128)S(1)}, u32[]{:S(2)}, u32[]{:S(2)}) collective-permute-start(f32[128,128]{1,0:T(8,128)S(1)} %get-tuple-element.36.refs_3_), channel_id=1, source_target_pairs={{0,1},{1,0},{2,3},{3,2},{4,5},{5,4},{6,7},{7,6},{8,9},{9,8},{10,11... | collective-permute-start | bytes 196616 | tf_op jit(solution)/shard_map/ppermute | solution.py:413
  8.5 7.0 %collective-permute-start.2 = (f32[128,128]{1,0:T(8,128)S(1)}, f32[128,128]{1,0:T(8,128)S(1)}, u32[]{:S(2)}, u32[]{:S(2)}) collective-permute-start(f32[128,128]{1,0:T(8,128)S(1)} %get-tuple-element.37.refs_4_), channel_id=1, source_target_pairs={{1,2},{2,1},{3,4},{4,3},{5,6},{6,5},{0,0},{7,7},{9,10},{10,9},{11,... | collective-permute-start | bytes 196616 | tf_op jit(solution)/shard_map/ppermute | solution.py:413
  10.5 12.0 %collective-permute-start = (f32[8,2,8,128]{3,2,1,0:T(8,128)S(1)}, f32[8,2,8,128]{3,2,1,0:T(8,128)S(1)}, u32[]{:S(2)}, u32[]{:S(2)}) collective-permute-start(f32[8,2,8,128]{3,2,1,0:T(8,128)S(1)} %get-tuple-element.30), channel_id=1, source_target_pairs={{0,8},{8,16},{16,24},{24,0},{1,9},{9,17},{17,25},{25,1},{2,10},{10... | collective-permute-start | bytes 196616 | tf_op jit(solution)/shard_map/ppermute | solution.py:419
  20.0 4.3 %collective-permute-start.3 = (f32[128,128]{1,0:T(8,128)S(1)}, f32[128,128]{1,0:T(8,128)S(1)}, u32[]{:S(2)}, u32[]{:S(2)}) collective-permute-start(f32[128,128]{1,0:T(8,128)S(1)} %get-tuple-element.38.refs_6_), channel_id=1, source_target_pairs={{0,1},{1,0},{2,3},{3,2},{4,5},{5,4},{6,7},{7,6},{8,9},{9,8},{10,11... | collective-permute-start | bytes 196616 | tf_op jit(solution)/shard_map/ppermute | solution.py:413
  20.5 7.0 %collective-permute-start.4 = (f32[128,128]{1,0:T(8,128)S(1)}, f32[128,128]{1,0:T(8,128)S(1)}, u32[]{:S(2)}, u32[]{:S(2)}) collective-permute-start(f32[128,128]{1,0:T(8,128)S(1)} %get-tuple-element.39.refs_7_), channel_id=1, source_target_pairs={{1,2},{2,1},{3,4},{4,3},{5,6},{6,5},{0,0},{7,7},{9,10},{10,9},{11,... | collective-permute-start | bytes 196616 | tf_op jit(solution)/shard_map/ppermute | solution.py:413
  31.8 5.0 %collective-permute-start.5 = (f32[128,128]{1,0:T(8,128)S(1)}, f32[128,128]{1,0:T(8,128)S(1)}, u32[]{:S(2)}, u32[]{:S(2)}) collective-permute-start(f32[128,128]{1,0:T(8,128)S(1)} %get-tuple-element.41.refs_3_), channel_id=1, source_target_pairs={{0,1},{1,0},{2,3},{3,2},{4,5},{5,4},{6,7},{7,6},{8,9},{9,8},{10,11... | collective-permute-start | bytes 196616 | tf_op jit(solution)/shard_map/ppermute | solution.py:413
  33.4 7.0 %collective-permute-start.6 = (f32[128,128]{1,0:T(8,128)S(1)}, f32[128,128]{1,0:T(8,128)S(1)}, u32[]{:S(2)}, u32[]{:S(2)}) collective-permute-start(f32[128,128]{1,0:T(8,128)S(1)} %get-tuple-element.42.refs_4_), channel_id=1, source_target_pairs={{1,2},{2,1},{3,4},{4,3},{5,6},{6,5},{0,0},{7,7},{9,10},{10,9},{11,... | collective-permute-start | bytes 196616 | tf_op jit(solution)/shard_map/ppermute | solution.py:413
  45.3 6.2 %collective-permute-start.7 = (f32[16,1024]{1,0:T(8,128)S(1)}, f32[16,1024]{1,0:T(8,128)S(1)}, u32[]{:S(2)}, u32[]{:S(2)}) collective-permute-start(f32[16,1024]{1,0:T(8,128)S(1)} %get-tuple-element.45), channel_id=1, source_target_pairs={{1,0},{2,1},{3,2},{4,3},{5,4},{6,5},{7,6},{9,8},{10,9},{11,10},{12... | collective-permute-start | bytes 196616 | tf_op jit(solution)/shard_map/ppermute | solution.py:438

commit v4 on v3

--- a/solution.py
+++ b/solution.py
@@ -363,9 +363,9 @@
         out[0, :, LANES * j : LANES * j + LANES] = scratch[16 * j : 16 * j + 16, :]
 
 
-def join_kernel(mine_ref, got_ref, out):
-    _, _, has_right = flags()
-    out[...] = jnp.where(has_right, mine_ref[...] + got_ref[...], 0.0)
+def join_kernel(mine_ref, ev_ref, od_ref, out):
+    even, _, has_right = flags()
+    out[...] = jnp.where(has_right, mine_ref[...] + jnp.where(even, ev_ref[...], od_ref[...]), 0.0)
 
 
 def call(kernel, name, inputs, outputs, scratch=(), space=pltpu.VMEM):
@@ -389,7 +389,12 @@
     count = lax.axis_size("space")
     windows = lax.axis_size("tm")
     even_faces = [(i, i ^ 1) for i in range(count)]
-    odd_faces = [(i, i + 1 if i % 2 else i - 1) for i in range(1, count - 1)] + [(0, 0), (count - 1, count - 1)]
+    odd_faces = []
+    for w in range(windows):
+        for i in range(count):
+            inner = 0 < i < count - 1
+            partner = (w, i + 1 if i % 2 else i - 1) if inner else (w ^ 1, i)
+            odd_faces.append((w * count + i, partner[0] * count + partner[1]))
     field = (BLOCK, 2, SUB, LANES)
     series = (steps * BLOCK, LANES)
     wide = (3 * steps * BLOCK, LANES)
@@ -410,7 +415,7 @@
     c_neu, r_neu, edge_neu = call(neumann_coef_kernel, "coef_neu", [nu, sig], coefs)
 
     def swapped(ev, od):
-        return lax.ppermute(ev, "space", even_faces), lax.ppermute(od, "space", odd_faces)
+        return lax.ppermute(ev, "space", even_faces), lax.ppermute(od, ("tm", "space"), odd_faces)
 
     ends, ev, od = call(
         functools.partial(dirichlet_kernel, 0, steps), "dir0",
@@ -435,8 +440,8 @@
         [c_neu, r_neu, edge_neu, ev, od, ev_got, od_got, g_right],
         [(steps, rows)] * 2, [series] * 2 + [wide] * 2 + [series] * 2,
     )
-    got = lax.ppermute(first, "space", [(i, i - 1) for i in range(1, count)])
-    traces = call(join_kernel, "join", [mine, got], (steps, rows))
+    ev_got, od_got = swapped(first, first)
+    traces = call(join_kernel, "join", [mine, ev_got, od_got], (steps, rows))
     return end_states, traces
 
 

time: 52.3 us -> 47.2 us (0.902)
  the two profiles are of different devices: /device:TPU:8 before, /device:TPU:0 now
where the time goes in v4:
time: 47.2 us; the launch traced here: 47.1 us
  Pallas kernels  21.6 us (46%)
  starting transfers between devices  16.7 us (35%)
  waiting for transfers between devices  8.11 us (17%)
  between operations  0.68 us (1%)
    pallas_call x8, Pallas kernels, call(): pl.pallas_call(kernel, out_shape=shapes, in_specs=[pl.BlockSpec(memory_sp...  21.6 us
    ppermute x4, starting transfers between devices, swapped(): lax.ppermute(ev, 'space', even_faces)  16.1 us
    ppermute x4, waiting for transfers between devices, swapped(): lax.ppermute(ev, 'space', even_faces)  8.09 us
  transfers between devices with their start and end apart: 9, of which 4 were waited for; matrix products, arithmetic and copies ran while one was open for 0% of the time, Pallas kernels for 12%

profile of v4, /device:TPU:0, one launch (start us, length us, event | category | flops | bytes accessed | tf_op | source)
XLA Modules:
  0.0 47.1 jit_solution(15927338254042358827)
XLA Ops:
  0.6 2.3 %first.1 = (f32[8,2,8,128]{3,2,1,0:T(8,128)S(1)}, f32[8,2,8,128]{3,2,1,0:T(8,128)S(1)}, f32[8,2,8,128]{3,2,1,0:T(8,128)S(1)}, f32[14,7,8,128]{3,2,1,0:T(8,128)S(...) custom-call(s32[16,1024]{1,0:T(8,128)} %labels_hbm.1, ...), custom_call_target="tpu_custom_call" | custom-call | tf_op jit(solution)/shard_map/first/pallas_call | solution.py:374
  2.9 4.0 %dir0.1 = (f32[8,2,8,128]{3,2,1,0:T(8,128)S(1)}, f32[128,128]{1,0:T(8,128)S(1)}, f32[128,128]{1,0:T(8,128)S(1)}) custom-call(f32[8,2,8,128]{3,2,1,0:T(8,128)S(1)} %get-tuple-element.24.refs_0_, f32[14,7,8,128]{3,2,1,0:T(8,128)S(1)} %get-tuple-element.25.refs_1_, f32[14,6,8,128]{3,2,1,0:T(8,128)S(1)} %get-tuple-element.26.refs_2_, ...), custom_call_target="tpu_custom_call" | custom-call | tf_op jit(solution)/shard_map/dir0/pallas_call | solution.py:374
  7.0 3.0 %collective-permute-start.1 = (f32[128,128]{1,0:T(8,128)S(1)}, f32[128,128]{1,0:T(8,128)S(1)}, u32[]{:S(2)}, u32[]{:S(2)}) collective-permute-start(f32[128,128]{1,0:T(8,128)S(1)} %get-tuple-element.36.refs_3_), channel_id=1, source_target_pairs={{0,1},{1,0},{2,3},{3,2},{4,5},{5,4},{6,7},{7,6},{8,9},{9,8},{10,11... | collective-permute-start | bytes 196616 | tf_op jit(solution)/shard_map/ppermute | solution.py:418
  10.0 0.0 collective-permute-start.2
  10.0 0.5 %collective-permute-start = (f32[8,2,8,128]{3,2,1,0:T(8,128)S(1)}, f32[8,2,8,128]{3,2,1,0:T(8,128)S(1)}, u32[]{:S(2)}, u32[]{:S(2)}) collective-permute-start(f32[8,2,8,128]{3,2,1,0:T(8,128)S(1)} %get-tuple-element.30), channel_id=1, source_target_pairs={{0,8},{8,16},{16,24},{24,0},{1,9},{9,17},{17,25},{25,1},{2,10},{10... | collective-permute-start | bytes 196616 | tf_op jit(solution)/shard_map/ppermute | solution.py:424
  10.5 0.3 coef_neu.1
  10.8 2.3 %collective-permute-done.1.refs_5_ = f32[128,128]{1,0:T(8,128)S(1)} collective-permute-done((f32[128,128]{1,0:T(8,128)S(1)}, f32[128,128]{1,0:T(8,128)S(1)}, u32[]{:S(2)}, u32[]{:S(2)}) %collective-permute-start.1) | collective-permute-done | bytes 65568 | tf_op jit(solution)/shard_map/ppermute | solution.py:418
  13.1 0.0 collective-permute-done.2.refs_6_
  13.1 4.4 %neu0.1 = (f32[128,128]{1,0:T(8,128)S(1)}, f32[128,128]{1,0:T(8,128)S(1)}) custom-call(f32[14,7,8,128]{3,2,1,0:T(8,128)S(1)} %get-tuple-element.33.refs_0_, f32[14,6,8,128]{3,2,1,0:T(8,128)S(1)} %get-tuple-element.34.refs_1_, f32[4,8,128]{2,1,0:T(8,128)S(1)} %get-tuple-element.35.refs_2_, f32[128,128]{1,0:T(8,128)S(1)} %get-tuple-element.36.refs_3_, ...), custom_call_target="tpu_custom_call" | custom-call | tf_op jit(solution)/shard_map/neu0/pallas_call | solution.py:374
  17.5 2.5 %collective-permute-start.3 = (f32[128,128]{1,0:T(8,128)S(1)}, f32[128,128]{1,0:T(8,128)S(1)}, u32[]{:S(2)}, u32[]{:S(2)}) collective-permute-start(f32[128,128]{1,0:T(8,128)S(1)} %get-tuple-element.38.refs_6_), channel_id=1, source_target_pairs={{0,1},{1,0},{2,3},{3,2},{4,5},{5,4},{6,7},{7,6},{8,9},{9,8},{10,11... | collective-permute-start | bytes 196616 | tf_op jit(solution)/shard_map/ppermute | solution.py:418
  20.0 0.0 collective-permute-start.4
  20.0 0.0 collective-permute-done.refs_0_
  20.0 2.2 %collective-permute-done.3.refs_8_ = f32[128,128]{1,0:T(8,128)S(1)} collective-permute-done((f32[128,128]{1,0:T(8,128)S(1)}, f32[128,128]{1,0:T(8,128)S(1)}, u32[]{:S(2)}, u32[]{:S(2)}) %collective-permute-start.3) | collective-permute-done | bytes 65568 | tf_op jit(solution)/shard_map/ppermute | solution.py:418
  22.2 0.0 collective-permute-done.4.refs_9_
  22.2 4.2 %dir1.1 = (f32[8,2,8,128]{3,2,1,0:T(8,128)S(1)}, f32[128,128]{1,0:T(8,128)S(1)}, f32[128,128]{1,0:T(8,128)S(1)}, f32[128,128]{1,0:T(8,128)S(1)}) custom-call(f32[8,2,8,128]{3,2,1,0:T(8,128)S(1)} %collective-permute-done.refs_0_, f32[14,7,8,128]{3,2,1,0:T(8,128)S(1)} %get-tuple-element.25.refs_1_, f32[14,6,8,128]{3,2,1,0:T(8,128)S(1)} %get-tuple-element.26.refs_2_, ...), custom_call_target="tpu_custom_call" | custom-call | tf_op jit(solution)/shard_map/dir1/pallas_call | solution.py:374
  26.4 3.2 %collective-permute-start.5 = (f32[128,128]{1,0:T(8,128)S(1)}, f32[128,128]{1,0:T(8,128)S(1)}, u32[]{:S(2)}, u32[]{:S(2)}) collective-permute-start(f32[128,128]{1,0:T(8,128)S(1)} %get-tuple-element.41.refs_3_), channel_id=1, source_target_pairs={{0,1},{1,0},{2,3},{3,2},{4,5},{5,4},{6,7},{7,6},{8,9},{9,8},{10,11... | collective-permute-start | bytes 196616 | tf_op jit(solution)/shard_map/ppermute | solution.py:418
  29.7 0.0 collective-permute-start.6
  29.7 2.2 %collective-permute-done.5.refs_5_ = f32[128,128]{1,0:T(8,128)S(1)} collective-permute-done((f32[128,128]{1,0:T(8,128)S(1)}, f32[128,128]{1,0:T(8,128)S(1)}, u32[]{:S(2)}, u32[]{:S(2)}) %collective-permute-start.5) | collective-permute-done | bytes 65568 | tf_op jit(solution)/shard_map/ppermute | solution.py:418
  31.9 0.0 collective-permute-done.6.refs_6_
  31.9 4.9 %neu1.1 = (f32[16,1024]{1,0:T(8,128)S(1)}, f32[16,1024]{1,0:T(8,128)S(1)}) custom-call(f32[14,7,8,128]{3,2,1,0:T(8,128)S(1)} %get-tuple-element.33.refs_0_, f32[14,6,8,128]{3,2,1,0:T(8,128)S(1)} %get-tuple-element.34.refs_1_, f32[4,8,128]{2,1,0:T(8,128)S(1)} %get-tuple-element.35.refs_2_, f32[128,128]{1,0:T(8,128)S(1)} %get-tuple-element.41.refs_3_, ...), custom_call_target="tpu_custom_call" | custom-call | tf_op jit(solution)/shard_map/neu1/pallas_call | solution.py:374
  36.8 0.1 collective-permute-start.8
  36.8 7.3 %collective-permute-start.7 = (f32[16,1024]{1,0:T(8,128)S(1)}, f32[16,1024]{1,0:T(8,128)S(1)}, u32[]{:S(2)}, u32[]{:S(2)}) collective-permute-start(f32[16,1024]{1,0:T(8,128)S(1)} %get-tuple-element.45), channel_id=1, source_target_pairs={{0,1},{1,0},{2,3},{3,2},{4,5},{5,4},{6,7},{7,6},{8,9},{9,8},{10,11... | collective-permute-start | bytes 196616 | tf_op jit(solution)/shard_map/ppermute | solution.py:418
  44.2 0.9 %natural.1 = f32[1,16,1024]{2,1,0:T(8,128)} custom-call(f32[8,2,8,128]{3,2,1,0:T(8,128)S(1)} %get-tuple-element.40.ends_ref), custom_call_target="tpu_custom_call" | custom-call | tf_op jit(solution)/shard_map/natural/pallas_call | solution.py:374
  45.1 0.0 collective-permute-done.8.od_ref
  45.1 1.3 %collective-permute-done.7.ev_ref = f32[16,1024]{1,0:T(8,128)S(1)} collective-permute-done((f32[16,1024]{1,0:T(8,128)S(1)}, f32[16,1024]{1,0:T(8,128)S(1)}, u32[]{:S(2)}, u32[]{:S(2)}) %collective-permute-start.7) | collective-permute-done | bytes 65568 | tf_op jit(solution)/shard_map/ppermute | solution.py:418
  46.4 0.6 %join.1 = f32[16,1024]{1,0:T(8,128)} custom-call(f32[16,1024]{1,0:T(8,128)S(1)} %get-tuple-element.44.mine_ref, f32[16,1024]{1,0:T(8,128)S(1)} %collective-permute-done.7.ev_ref, f32[16,1024]{1,0:T(8,128)S(1)} %collective-permute-done.8.od_ref), custom_call_target="tpu_custom_call" | custom-call | tf_op jit(solution)/shard_map/join/pallas_call | solution.py:374
Async XLA Ops:
  7.0 6.1 %collective-permute-start.1 = (f32[128,128]{1,0:T(8,128)S(1)}, f32[128,128]{1,0:T(8,128)S(1)}, u32[]{:S(2)}, u32[]{:S(2)}) collective-permute-start(f32[128,128]{1,0:T(8,128)S(1)} %get-tuple-element.36.refs_3_), channel_id=1, source_target_pairs={{0,1},{1,0},{2,3},{3,2},{4,5},{5,4},{6,7},{7,6},{8,9},{9,8},{10,11... | collective-permute-start | bytes 196616 | tf_op jit(solution)/shard_map/ppermute | solution.py:418
  10.0 3.1 %collective-permute-start.2 = (f32[128,128]{1,0:T(8,128)S(1)}, f32[128,128]{1,0:T(8,128)S(1)}, u32[]{:S(2)}, u32[]{:S(2)}) collective-permute-start(f32[128,128]{1,0:T(8,128)S(1)} %get-tuple-element.37.refs_4_), channel_id=1, source_target_pairs={{0,8},{1,2},{2,1},{3,4},{4,3},{5,6},{6,5},{7,15},{8,0},{9,10},{10,... | collective-permute-start | bytes 196616 | tf_op jit(solution)/shard_map/ppermute | solution.py:418
  10.0 10.0 %collective-permute-start = (f32[8,2,8,128]{3,2,1,0:T(8,128)S(1)}, f32[8,2,8,128]{3,2,1,0:T(8,128)S(1)}, u32[]{:S(2)}, u32[]{:S(2)}) collective-permute-start(f32[8,2,8,128]{3,2,1,0:T(8,128)S(1)} %get-tuple-element.30), channel_id=1, source_target_pairs={{0,8},{8,16},{16,24},{24,0},{1,9},{9,17},{17,25},{25,1},{2,10},{10... | collective-permute-start | bytes 196616 | tf_op jit(solution)/shard_map/ppermute | solution.py:424
  17.5 4.8 %collective-permute-start.3 = (f32[128,128]{1,0:T(8,128)S(1)}, f32[128,128]{1,0:T(8,128)S(1)}, u32[]{:S(2)}, u32[]{:S(2)}) collective-permute-start(f32[128,128]{1,0:T(8,128)S(1)} %get-tuple-element.38.refs_6_), channel_id=1, source_target_pairs={{0,1},{1,0},{2,3},{3,2},{4,5},{5,4},{6,7},{7,6},{8,9},{9,8},{10,11... | collective-permute-start | bytes 196616 | tf_op jit(solution)/shard_map/ppermute | solution.py:418
  20.0 2.2 %collective-permute-start.4 = (f32[128,128]{1,0:T(8,128)S(1)}, f32[128,128]{1,0:T(8,128)S(1)}, u32[]{:S(2)}, u32[]{:S(2)}) collective-permute-start(f32[128,128]{1,0:T(8,128)S(1)} %get-tuple-element.39.refs_7_), channel_id=1, source_target_pairs={{0,8},{1,2},{2,1},{3,4},{4,3},{5,6},{6,5},{7,15},{8,0},{9,10},{10,... | collective-permute-start | bytes 196616 | tf_op jit(solution)/shard_map/ppermute | solution.py:418
  26.4 5.5 %collective-permute-start.5 = (f32[128,128]{1,0:T(8,128)S(1)}, f32[128,128]{1,0:T(8,128)S(1)}, u32[]{:S(2)}, u32[]{:S(2)}) collective-permute-start(f32[128,128]{1,0:T(8,128)S(1)} %get-tuple-element.41.refs_3_), channel_id=1, source_target_pairs={{0,1},{1,0},{2,3},{3,2},{4,5},{5,4},{6,7},{7,6},{8,9},{9,8},{10,11... | collective-permute-start | bytes 196616 | tf_op jit(solution)/shard_map/ppermute | solution.py:418
  29.7 2.2 %collective-permute-start.6 = (f32[128,128]{1,0:T(8,128)S(1)}, f32[128,128]{1,0:T(8,128)S(1)}, u32[]{:S(2)}, u32[]{:S(2)}) collective-permute-start(f32[128,128]{1,0:T(8,128)S(1)} %get-tuple-element.42.refs_4_), channel_id=1, source_target_pairs={{0,8},{1,2},{2,1},{3,4},{4,3},{5,6},{6,5},{7,15},{8,0},{9,10},{10,... | collective-permute-start | bytes 196616 | tf_op jit(solution)/shard_map/ppermute | solution.py:418
  36.8 8.3 %collective-permute-start.8 = (f32[16,1024]{1,0:T(8,128)S(1)}, f32[16,1024]{1,0:T(8,128)S(1)}, u32[]{:S(2)}, u32[]{:S(2)}) collective-permute-start(f32[16,1024]{1,0:T(8,128)S(1)} %get-tuple-element.45), channel_id=1, source_target_pairs={{0,8},{1,2},{2,1},{3,4},{4,3},{5,6},{6,5},{7,15},{8,0},{9,10},{10,... | collective-permute-start | bytes 196616 | tf_op jit(solution)/shard_map/ppermute | solution.py:418
  36.8 9.6 %collective-permute-start.7 = (f32[16,1024]{1,0:T(8,128)S(1)}, f32[16,1024]{1,0:T(8,128)S(1)}, u32[]{:S(2)}, u32[]{:S(2)}) collective-permute-start(f32[16,1024]{1,0:T(8,128)S(1)} %get-tuple-element.45), channel_id=1, source_target_pairs={{0,1},{1,0},{2,3},{3,2},{4,5},{5,4},{6,7},{7,6},{8,9},{9,8},{10,11... | collective-permute-start | bytes 196616 | tf_op jit(solution)/shard_map/ppermute | solution.py:418

commit v5 on v4

--- a/solution.py
+++ b/solution.py
@@ -43,28 +43,31 @@
     return pltpu.roll(tile, 1, 0)
 
 
+def swap_groups(tiles):
+    group = tile_index(1) // 16
+    for bit in (1, 2, 4):
+        low = (group & bit) == 0
+        new = []
+        for j, tile in enumerate(tiles):
+            other = tiles[j ^ bit]
+            if j & bit:
+                new.append(jnp.where(low, pltpu.roll(other, LANES - 16 * bit, 1), tile))
+            else:
+                new.append(jnp.where(low, tile, pltpu.roll(other, 16 * bit, 1)))
+        tiles = new
+    return tiles
+
+
 def to_blocks(tiles):
     lane = tile_index(1)
-    out = []
-    for r in range(BLOCK):
-        order = 8 * (lane % 16) + r
-        tile = jnp.take_along_axis(tiles[0], order, axis=1)
-        for j in range(1, BLOCK):
-            tile = jnp.where(lane // 16 == j, jnp.take_along_axis(tiles[j], order, axis=1), tile)
-        out.append(tile)
-    return out
+    order = 8 * (lane % 16) + lane // 16
+    return swap_groups([jnp.take_along_axis(tile, order, axis=1) for tile in tiles])
 
 
 def from_blocks(tiles):
     lane = tile_index(1)
-    out = []
-    for j in range(BLOCK):
-        order = 16 * j + lane // 8
-        tile = jnp.take_along_axis(tiles[0], order, axis=1)
-        for r in range(1, BLOCK):
-            tile = jnp.where(lane % 8 == r, jnp.take_along_axis(tiles[r], order, axis=1), tile)
-        out.append(tile)
-    return out
+    order = 16 * (lane % 8) + lane // 8
+    return [jnp.take_along_axis(tile, order, axis=1) for tile in swap_groups(tiles)]
 
 
 def put_field(value, scratch, out):
@@ -112,20 +115,16 @@
     ]
     for copy in copies:
         copy.start()
-    copies[0].wait()
-    copies[1].wait()
+    for copy in copies:
+        copy.wait()
     labels = labels_ref[...]
     nu = jnp.zeros(labels.shape, F32)
     for material in range(table_ref.shape[0]):
         nu = nu + jnp.where(labels == material, table_ref[material], 0.0)
     put_field(nu, s0, nu_out)
-    copies[2].wait()
     put_field(sigma_ref[...], s1, sigma_out)
-    copies[3].wait()
     put_field(coil_ref[...], s2, cur_ref)
-    copies[4].wait()
     put_field(start_ref[0], s3, start_out)
-    copies[5].wait()
     for t in range(wave_ref.shape[0]):
         wave_out[t : t + 1, :] = jnp.full((1, LANES), wave_ref[t], F32)
     coef_kernel(False, nu_out, sigma_out, cur_ref, c_out, r_out, edge_out, scale_out)
@@ -198,13 +197,17 @@
     put(c_out, DN_O, [dn_o[r] * around_o[r] * rec_o[r] for r in span])
     put(c_out, UP_E, [up_e[r] * around_e[r + 2] * rec_e[r] for r in span], lambda r: not unit_up(r))
     put(c_out, DN_E, [dn_e[r] * around_e[r] * rec_e[r] for r in span], lambda r: not unit_down(r))
-    put(r_out, SIG_E, [sigma_ref[r, 0] * inv_e[r] for r in span])
-    put(r_out, SIG_O, [sigma_ref[r, 1] * inv_o[r] for r in span])
+    def keep(slot, tiles):
+        for r in range(BLOCK):
+            r_out[r, slot] = tiles[r]
+
+    keep(SIG_E, [sigma_ref[r, 0] * inv_e[r] for r in span])
+    keep(SIG_O, [sigma_ref[r, 1] * inv_o[r] for r in span])
     if not neumann:
-        put(r_out, COIL_E, [coil_ref[r, 0] * rec_e[r] for r in span])
-        put(r_out, COIL_O, [coil_ref[r, 1] * rec_o[r] for r in span])
-    put(r_out, FACE_E, [jnp.where((sub == 0) & has_left, rec_e[r], 0.0) for r in span])
-    put(r_out, FACE_O, [jnp.where((sub == SUB - 1) & has_right, rec_o[r], 0.0) for r in span])
+        keep(COIL_E, [coil_ref[r, 0] * rec_e[r] for r in span])
+        keep(COIL_O, [coil_ref[r, 1] * rec_o[r] for r in span])
+    keep(FACE_E, [jnp.where((sub == 0) & has_left, rec_e[r], 0.0) for r in span])
+    keep(FACE_O, [jnp.where((sub == SUB - 1) & has_right, rec_o[r], 0.0) for r in span])
     for r in range(BLOCK):
         if not neumann:
             scale_out[r, 0] = scale_e[r]
@@ -253,20 +256,22 @@
     def step(t, carry):
         now_e = haloed(dict(enumerate(carry[:BLOCK])))
         now_o = haloed(dict(enumerate(carry[BLOCK:])))
-        rhs = {}
-        for r in range(LOW, HIGH):
-            i = r - LOW
-            b_e = r_ref[i, SIG_E] * now_e[r]
-            b_o = r_ref[i, SIG_O] * now_o[r]
+        own = []
+        for r in range(BLOCK):
+            b_e = r_ref[r, SIG_E] * now_e[r]
+            b_o = r_ref[r, SIG_O] * now_o[r]
             if wave_ref is not None:
                 wave = wave_ref[pl.ds(t, 1), :]
-                b_e = b_e + r_ref[i, COIL_E] * wave
-                b_o = b_o + r_ref[i, COIL_O] * wave
+                b_e = b_e + r_ref[r, COIL_E] * wave
+                b_o = b_o + r_ref[r, COIL_O] * wave
             if left is not None:
-                at = pl.ds(t * 3 * BLOCK + BLOCK + r, 1)
-                b_e = b_e + r_ref[i, FACE_E] * left[at, :]
-                b_o = b_o + r_ref[i, FACE_O] * right[at, :]
-            rhs[r] = (b_e, b_o)
+                at = pl.ds(t * BLOCK + r, 1)
+                b_e = b_e + r_ref[r, FACE_E] * left[at, :]
+                b_o = b_o + r_ref[r, FACE_O] * right[at, :]
+            own.append((b_e, b_o))
+        rhs_e = spread([pair[0] for pair in own])
+        rhs_o = spread([pair[1] for pair in own])
+        rhs = {r: (rhs_e[r], rhs_o[r]) for r in range(LOW, HIGH)}
         now_e, now_o = advance(now_e, now_o, rhs, c_ref)
         for r in range(BLOCK):
             first[pl.ds(t * BLOCK + r, 1), :] = now_e[r][0:1]
@@ -274,13 +279,6 @@
         return tuple(now_e[r] for r in range(BLOCK)) + tuple(now_o[r] for r in range(BLOCK))
 
     return lax.fori_loop(0, steps, step, start, unroll=2)
-
-
-def put_face(ref, t, tile):
-    base = t * 3 * BLOCK
-    ref[base : base + BLOCK, :] = prev_lane(tile)
-    ref[base + BLOCK : base + 2 * BLOCK, :] = tile
-    ref[base + 2 * BLOCK : base + 3 * BLOCK, :] = next_lane(tile)
 
 
 def at_step(ref, t):
@@ -303,8 +301,8 @@
             at_right = jnp.where(even, ev, od)
             g_left[t * BLOCK : (t + 1) * BLOCK, :] = at_left
             g_right[t * BLOCK : (t + 1) * BLOCK, :] = at_right
-            put_face(left, t, edge_ref[0] * at_left)
-            put_face(right, t, edge_ref[1] * at_right)
+            left[t * BLOCK : (t + 1) * BLOCK, :] = edge_ref[0] * at_left
+            right[t * BLOCK : (t + 1) * BLOCK, :] = edge_ref[1] * at_right
     start = tuple(start_ref[r, e] / scale_ref[r, e] for e in range(2) for r in range(BLOCK))
     final = march(start, c_ref, r_ref, wave_ref, left, right, first, last, steps)
     for e in range(2):
@@ -332,8 +330,8 @@
     for t in range(steps):
         ev = at_step(ev_own, t) + at_step(ev_got, t)
         od = at_step(od_own, t) + at_step(od_got, t)
-        put_face(left, t, jnp.where(even, od, ev))
-        put_face(right, t, jnp.where(even, ev, od))
+        left[t * BLOCK : (t + 1) * BLOCK, :] = jnp.where(even, od, ev)
+        right[t * BLOCK : (t + 1) * BLOCK, :] = jnp.where(even, ev, od)
     zero = jnp.zeros((SUB, LANES), F32)
     march((zero,) * (2 * BLOCK), c_ref, r_ref, None, left, right, first, last, steps)
     if sweep + 1 < SWEEPS:
@@ -397,8 +395,7 @@
             odd_faces.append((w * count + i, partner[0] * count + partner[1]))
     field = (BLOCK, 2, SUB, LANES)
     series = (steps * BLOCK, LANES)
-    wide = (3 * steps * BLOCK, LANES)
-    coefs = [(ROWS, 7, SUB, LANES), (ROWS, 6, SUB, LANES), (4, BLOCK, LANES)]
+    coefs = [(ROWS, 7, SUB, LANES), (BLOCK, 6, SUB, LANES), (4, BLOCK, LANES)]
     nu, sig, state, c_dir, r_dir, edge_dir, scale_dir, wave = call(
         first_kernel, "first",
         [
@@ -425,20 +422,20 @@
     ev_got, od_got = swapped(ev, od)
     ev, od = call(
         functools.partial(neumann_kernel, 0, steps), "neu0",
-        [c_neu, r_neu, edge_neu, ev, od, ev_got, od_got], [series] * 2, [series] * 2 + [wide] * 2,
+        [c_neu, r_neu, edge_neu, ev, od, ev_got, od_got], [series] * 2, [series] * 2 + [series] * 2,
     )
     ev_got, od_got = swapped(ev, od)
     ends, ev, od, g_right = call(
         functools.partial(dirichlet_kernel, 1, steps), "dir1",
         [state, c_dir, r_dir, scale_dir, edge_dir, wave, ev, od, ev_got, od_got],
-        [field, series, series, series], [series] * 2 + [wide] * 2 + [series],
+        [field, series, series, series], [series] * 2 + [series] * 2 + [series],
     )
     ev_got, od_got = swapped(ev, od)
     end_states = call(natural_kernel, "natural", [ends], (1, columns, rows), [(128, LANES)])
     mine, first = call(
         functools.partial(neumann_kernel, 1, steps), "neu1",
         [c_neu, r_neu, edge_neu, ev, od, ev_got, od_got, g_right],
-        [(steps, rows)] * 2, [series] * 2 + [wide] * 2 + [series] * 2,
+        [(steps, rows)] * 2, [series] * 2 + [series] * 2 + [series] * 2,
     )
     ev_got, od_got = swapped(first, first)
     traces = call(join_kernel, "join", [mine, ev_got, od_got], (steps, rows))

time: 47.2 us -> 46.4 us (0.983)
  Pallas kernels: 21.6 us -> 20.7 us
    pallas_call x8, Pallas kernels: 21.6 us -> 20.7 us  [call(): pl.pallas_call(kernel, out_shape=shapes, in_specs=[pl.BlockSpec(memory_sp...]
  transfers between devices with their start and end apart: 9 -> 9, of which waited for: 4 -> 4; matrix products, arithmetic and copies ran while one was open for 0% -> 0% of each run, Pallas kernels for 12% -> 11%
where the time goes in v5:
time: 46.4 us; the launch traced here: 46.2 us
  Pallas kernels  20.7 us (45%)
  starting transfers between devices  16.7 us (36%)
  waiting for transfers between devices  8.09 us (17%)
  between operations  0.68 us (1%)
    pallas_call x8, Pallas kernels, call(): pl.pallas_call(kernel, out_shape=shapes, in_specs=[pl.BlockSpec(memory_sp...  20.7 us
    ppermute x4, starting transfers between devices, swapped(): lax.ppermute(ev, 'space', even_faces)  16.1 us
    ppermute x4, waiting for transfers between devices, swapped(): lax.ppermute(ev, 'space', even_faces)  8.08 us
  transfers between devices with their start and end apart: 9, of which 4 were waited for; matrix products, arithmetic and copies ran while one was open for 0% of the time, Pallas kernels for 11%

profile of v5, /device:TPU:0, one launch (start us, length us, event | category | flops | bytes accessed | tf_op | source)
XLA Modules:
  0.0 46.2 jit_solution(16142756736450592661)
XLA Ops:
  0.6 2.0 %first.1 = (f32[8,2,8,128]{3,2,1,0:T(8,128)S(1)}, f32[8,2,8,128]{3,2,1,0:T(8,128)S(1)}, f32[8,2,8,128]{3,2,1,0:T(8,128)S(1)}, f32[14,7,8,128]{3,2,1,0:T(8,128)S(...) custom-call(s32[16,1024]{1,0:T(8,128)} %labels_hbm.1, ...), custom_call_target="tpu_custom_call" | custom-call | tf_op jit(solution)/shard_map/first/pallas_call | solution.py:372
  2.6 4.2 %dir0.1 = (f32[8,2,8,128]{3,2,1,0:T(8,128)S(1)}, f32[128,128]{1,0:T(8,128)S(1)}, f32[128,128]{1,0:T(8,128)S(1)}) custom-call(f32[8,2,8,128]{3,2,1,0:T(8,128)S(1)} %get-tuple-element.24.refs_0_, f32[14,7,8,128]{3,2,1,0:T(8,128)S(1)} %get-tuple-element.25.refs_1_, f32[8,6,8,128]{3,2,1,0:T(8,128)S(1)} %get-tuple-element.26.refs_2_, ...), custom_call_target="tpu_custom_call" | custom-call | tf_op jit(solution)/shard_map/dir0/pallas_call | solution.py:372
  6.8 3.0 %collective-permute-start.1 = (f32[128,128]{1,0:T(8,128)S(1)}, f32[128,128]{1,0:T(8,128)S(1)}, u32[]{:S(2)}, u32[]{:S(2)}) collective-permute-start(f32[128,128]{1,0:T(8,128)S(1)} %get-tuple-element.36.refs_3_), channel_id=1, source_target_pairs={{0,1},{1,0},{2,3},{3,2},{4,5},{5,4},{6,7},{7,6},{8,9},{9,8},{10,11... | collective-permute-start | bytes 196616 | tf_op jit(solution)/shard_map/ppermute | solution.py:415
  9.9 0.0 collective-permute-start.2
  9.9 0.5 %collective-permute-start = (f32[8,2,8,128]{3,2,1,0:T(8,128)S(1)}, f32[8,2,8,128]{3,2,1,0:T(8,128)S(1)}, u32[]{:S(2)}, u32[]{:S(2)}) collective-permute-start(f32[8,2,8,128]{3,2,1,0:T(8,128)S(1)} %get-tuple-element.30), channel_id=1, source_target_pairs={{0,8},{8,16},{16,24},{24,0},{1,9},{9,17},{17,25},{25,1},{2,10},{10... | collective-permute-start | bytes 196616 | tf_op jit(solution)/shard_map/ppermute | solution.py:421
  10.4 0.3 coef_neu.1
  10.7 2.3 %collective-permute-done.1.refs_5_ = f32[128,128]{1,0:T(8,128)S(1)} collective-permute-done((f32[128,128]{1,0:T(8,128)S(1)}, f32[128,128]{1,0:T(8,128)S(1)}, u32[]{:S(2)}, u32[]{:S(2)}) %collective-permute-start.1) | collective-permute-done | bytes 65568 | tf_op jit(solution)/shard_map/ppermute | solution.py:415
  13.0 0.0 collective-permute-done.2.refs_6_
  13.0 4.0 %neu0.1 = (f32[128,128]{1,0:T(8,128)S(1)}, f32[128,128]{1,0:T(8,128)S(1)}) custom-call(f32[14,7,8,128]{3,2,1,0:T(8,128)S(1)} %get-tuple-element.33.refs_0_, f32[8,6,8,128]{3,2,1,0:T(8,128)S(1)} %get-tuple-element.34.refs_1_, f32[4,8,128]{2,1,0:T(8,128)S(1)} %get-tuple-element.35.refs_2_, f32[128,128]{1,0:T(8,128)S(1)} %get-tuple-element.36.refs_3_, ...), custom_call_target="tpu_custom_call" | custom-call | tf_op jit(solution)/shard_map/neu0/pallas_call | solution.py:372
  17.0 2.5 %collective-permute-start.3 = (f32[128,128]{1,0:T(8,128)S(1)}, f32[128,128]{1,0:T(8,128)S(1)}, u32[]{:S(2)}, u32[]{:S(2)}) collective-permute-start(f32[128,128]{1,0:T(8,128)S(1)} %get-tuple-element.38.refs_6_), channel_id=1, source_target_pairs={{0,1},{1,0},{2,3},{3,2},{4,5},{5,4},{6,7},{7,6},{8,9},{9,8},{10,11... | collective-permute-start | bytes 196616 | tf_op jit(solution)/shard_map/ppermute | solution.py:415
  19.5 0.0 collective-permute-start.4
  19.5 0.0 collective-permute-done.refs_0_
  19.5 2.2 %collective-permute-done.3.refs_8_ = f32[128,128]{1,0:T(8,128)S(1)} collective-permute-done((f32[128,128]{1,0:T(8,128)S(1)}, f32[128,128]{1,0:T(8,128)S(1)}, u32[]{:S(2)}, u32[]{:S(2)}) %collective-permute-start.3) | collective-permute-done | bytes 65568 | tf_op jit(solution)/shard_map/ppermute | solution.py:415
  21.8 0.0 collective-permute-done.4.refs_9_
  21.8 4.3 %dir1.1 = (f32[8,2,8,128]{3,2,1,0:T(8,128)S(1)}, f32[128,128]{1,0:T(8,128)S(1)}, f32[128,128]{1,0:T(8,128)S(1)}, f32[128,128]{1,0:T(8,128)S(1)}) custom-call(f32[8,2,8,128]{3,2,1,0:T(8,128)S(1)} %collective-permute-done.refs_0_, f32[14,7,8,128]{3,2,1,0:T(8,128)S(1)} %get-tuple-element.25.refs_1_, f32[8,6,8,128]{3,2,1,0:T(8,128)S(1)} %get-tuple-element.26.refs_2_, ...), custom_call_target="tpu_custom_call" | custom-call | tf_op jit(solution)/shard_map/dir1/pallas_call | solution.py:372
  26.1 3.2 %collective-permute-start.5 = (f32[128,128]{1,0:T(8,128)S(1)}, f32[128,128]{1,0:T(8,128)S(1)}, u32[]{:S(2)}, u32[]{:S(2)}) collective-permute-start(f32[128,128]{1,0:T(8,128)S(1)} %get-tuple-element.41.refs_3_), channel_id=1, source_target_pairs={{0,1},{1,0},{2,3},{3,2},{4,5},{5,4},{6,7},{7,6},{8,9},{9,8},{10,11... | collective-permute-start | bytes 196616 | tf_op jit(solution)/shard_map/ppermute | solution.py:415
  29.3 0.0 collective-permute-start.6
  29.3 2.2 %collective-permute-done.5.refs_5_ = f32[128,128]{1,0:T(8,128)S(1)} collective-permute-done((f32[128,128]{1,0:T(8,128)S(1)}, f32[128,128]{1,0:T(8,128)S(1)}, u32[]{:S(2)}, u32[]{:S(2)}) %collective-permute-start.5) | collective-permute-done | bytes 65568 | tf_op jit(solution)/shard_map/ppermute | solution.py:415
  31.5 0.0 collective-permute-done.6.refs_6_
  31.5 4.3 %neu1.1 = (f32[16,1024]{1,0:T(8,128)S(1)}, f32[16,1024]{1,0:T(8,128)S(1)}) custom-call(f32[14,7,8,128]{3,2,1,0:T(8,128)S(1)} %get-tuple-element.33.refs_0_, f32[8,6,8,128]{3,2,1,0:T(8,128)S(1)} %get-tuple-element.34.refs_1_, f32[4,8,128]{2,1,0:T(8,128)S(1)} %get-tuple-element.35.refs_2_, f32[128,128]{1,0:T(8,128)S(1)} %get-tuple-element.41.refs_3_, ...), custom_call_target="tpu_custom_call" | custom-call | tf_op jit(solution)/shard_map/neu1/pallas_call | solution.py:372
  35.9 0.1 collective-permute-start.8
  36.0 7.3 %collective-permute-start.7 = (f32[16,1024]{1,0:T(8,128)S(1)}, f32[16,1024]{1,0:T(8,128)S(1)}, u32[]{:S(2)}, u32[]{:S(2)}) collective-permute-start(f32[16,1024]{1,0:T(8,128)S(1)} %get-tuple-element.45), channel_id=1, source_target_pairs={{0,1},{1,0},{2,3},{3,2},{4,5},{5,4},{6,7},{7,6},{8,9},{9,8},{10,11... | collective-permute-start | bytes 196616 | tf_op jit(solution)/shard_map/ppermute | solution.py:415
  43.3 0.9 %natural.1 = f32[1,16,1024]{2,1,0:T(8,128)} custom-call(f32[8,2,8,128]{3,2,1,0:T(8,128)S(1)} %get-tuple-element.40.ends_ref), custom_call_target="tpu_custom_call" | custom-call | tf_op jit(solution)/shard_map/natural/pallas_call | solution.py:372
  44.2 0.0 collective-permute-done.8.od_ref
  44.2 1.3 %collective-permute-done.7.ev_ref = f32[16,1024]{1,0:T(8,128)S(1)} collective-permute-done((f32[16,1024]{1,0:T(8,128)S(1)}, f32[16,1024]{1,0:T(8,128)S(1)}, u32[]{:S(2)}, u32[]{:S(2)}) %collective-permute-start.7) | collective-permute-done | bytes 65568 | tf_op jit(solution)/shard_map/ppermute | solution.py:415
  45.5 0.6 %join.1 = f32[16,1024]{1,0:T(8,128)} custom-call(f32[16,1024]{1,0:T(8,128)S(1)} %get-tuple-element.44.mine_ref, f32[16,1024]{1,0:T(8,128)S(1)} %collective-permute-done.7.ev_ref, f32[16,1024]{1,0:T(8,128)S(1)} %collective-permute-done.8.od_ref), custom_call_target="tpu_custom_call" | custom-call | tf_op jit(solution)/shard_map/join/pallas_call | solution.py:372
Async XLA Ops:
  6.8 6.1 %collective-permute-start.1 = (f32[128,128]{1,0:T(8,128)S(1)}, f32[128,128]{1,0:T(8,128)S(1)}, u32[]{:S(2)}, u32[]{:S(2)}) collective-permute-start(f32[128,128]{1,0:T(8,128)S(1)} %get-tuple-element.36.refs_3_), channel_id=1, source_target_pairs={{0,1},{1,0},{2,3},{3,2},{4,5},{5,4},{6,7},{7,6},{8,9},{9,8},{10,11... | collective-permute-start | bytes 196616 | tf_op jit(solution)/shard_map/ppermute | solution.py:415
  9.9 3.1 %collective-permute-start.2 = (f32[128,128]{1,0:T(8,128)S(1)}, f32[128,128]{1,0:T(8,128)S(1)}, u32[]{:S(2)}, u32[]{:S(2)}) collective-permute-start(f32[128,128]{1,0:T(8,128)S(1)} %get-tuple-element.37.refs_4_), channel_id=1, source_target_pairs={{0,8},{1,2},{2,1},{3,4},{4,3},{5,6},{6,5},{7,15},{8,0},{9,10},{10,... | collective-permute-start | bytes 196616 | tf_op jit(solution)/shard_map/ppermute | solution.py:415
  9.9 9.7 %collective-permute-start = (f32[8,2,8,128]{3,2,1,0:T(8,128)S(1)}, f32[8,2,8,128]{3,2,1,0:T(8,128)S(1)}, u32[]{:S(2)}, u32[]{:S(2)}) collective-permute-start(f32[8,2,8,128]{3,2,1,0:T(8,128)S(1)} %get-tuple-element.30), channel_id=1, source_target_pairs={{0,8},{8,16},{16,24},{24,0},{1,9},{9,17},{17,25},{25,1},{2,10},{10... | collective-permute-start | bytes 196616 | tf_op jit(solution)/shard_map/ppermute | solution.py:421
  17.0 4.8 %collective-permute-start.3 = (f32[128,128]{1,0:T(8,128)S(1)}, f32[128,128]{1,0:T(8,128)S(1)}, u32[]{:S(2)}, u32[]{:S(2)}) collective-permute-start(f32[128,128]{1,0:T(8,128)S(1)} %get-tuple-element.38.refs_6_), channel_id=1, source_target_pairs={{0,1},{1,0},{2,3},{3,2},{4,5},{5,4},{6,7},{7,6},{8,9},{9,8},{10,11... | collective-permute-start | bytes 196616 | tf_op jit(solution)/shard_map/ppermute | solution.py:415
  19.5 2.2 %collective-permute-start.4 = (f32[128,128]{1,0:T(8,128)S(1)}, f32[128,128]{1,0:T(8,128)S(1)}, u32[]{:S(2)}, u32[]{:S(2)}) collective-permute-start(f32[128,128]{1,0:T(8,128)S(1)} %get-tuple-element.39.refs_7_), channel_id=1, source_target_pairs={{0,8},{1,2},{2,1},{3,4},{4,3},{5,6},{6,5},{7,15},{8,0},{9,10},{10,... | collective-permute-start | bytes 196616 | tf_op jit(solution)/shard_map/ppermute | solution.py:415
  26.1 5.5 %collective-permute-start.5 = (f32[128,128]{1,0:T(8,128)S(1)}, f32[128,128]{1,0:T(8,128)S(1)}, u32[]{:S(2)}, u32[]{:S(2)}) collective-permute-start(f32[128,128]{1,0:T(8,128)S(1)} %get-tuple-element.41.refs_3_), channel_id=1, source_target_pairs={{0,1},{1,0},{2,3},{3,2},{4,5},{5,4},{6,7},{7,6},{8,9},{9,8},{10,11... | collective-permute-start | bytes 196616 | tf_op jit(solution)/shard_map/ppermute | solution.py:415
  29.3 2.2 %collective-permute-start.6 = (f32[128,128]{1,0:T(8,128)S(1)}, f32[128,128]{1,0:T(8,128)S(1)}, u32[]{:S(2)}, u32[]{:S(2)}) collective-permute-start(f32[128,128]{1,0:T(8,128)S(1)} %get-tuple-element.42.refs_4_), channel_id=1, source_target_pairs={{0,8},{1,2},{2,1},{3,4},{4,3},{5,6},{6,5},{7,15},{8,0},{9,10},{10,... | collective-permute-start | bytes 196616 | tf_op jit(solution)/shard_map/ppermute | solution.py:415
  35.9 8.4 %collective-permute-start.8 = (f32[16,1024]{1,0:T(8,128)S(1)}, f32[16,1024]{1,0:T(8,128)S(1)}, u32[]{:S(2)}, u32[]{:S(2)}) collective-permute-start(f32[16,1024]{1,0:T(8,128)S(1)} %get-tuple-element.45), channel_id=1, source_target_pairs={{0,8},{1,2},{2,1},{3,4},{4,3},{5,6},{6,5},{7,15},{8,0},{9,10},{10,... | collective-permute-start | bytes 196616 | tf_op jit(solution)/shard_map/ppermute | solution.py:415
  36.0 9.6 %collective-permute-start.7 = (f32[16,1024]{1,0:T(8,128)S(1)}, f32[16,1024]{1,0:T(8,128)S(1)}, u32[]{:S(2)}, u32[]{:S(2)}) collective-permute-start(f32[16,1024]{1,0:T(8,128)S(1)} %get-tuple-element.45), channel_id=1, source_target_pairs={{0,1},{1,0},{2,3},{3,2},{4,5},{5,4},{6,7},{7,6},{8,9},{9,8},{10,11... | collective-permute-start | bytes 196616 | tf_op jit(solution)/shard_map/ppermute | solution.py:415

commit v6 on v5

--- a/solution.py
+++ b/solution.py
@@ -19,8 +19,9 @@
 HIGH = BLOCK + DEPTH - 1
 ROWS = HIGH - LOW
 Q_E, P_O, Q_O, UP_O, DN_O, UP_E, DN_E = range(7)
-SIG_E, SIG_O, COIL_E, COIL_O, FACE_E, FACE_O = range(6)
+COIL_E, COIL_O, FACE_E, FACE_O = range(4)
 F32 = jnp.float32
+UNROLL = 4
 
 
 def tile_index(axis):
@@ -103,7 +104,7 @@
 
 def first_kernel(
     labels_hbm, table_hbm, sigma_hbm, coil_hbm, start_hbm, wave_hbm,
-    nu_out, sigma_out, start_out, c_out, r_out, edge_out, scale_out, wave_out,
+    nu_out, sigma_out, start_out, c_out, s_out, r_out, edge_out, scale_out, wave_out,
     labels_ref, table_ref, sigma_ref, coil_ref, start_ref, wave_ref, cur_ref, s0, s1, s2, s3, sems,
 ):
     copies = [
@@ -127,7 +128,7 @@
     put_field(start_ref[0], s3, start_out)
     for t in range(wave_ref.shape[0]):
         wave_out[t : t + 1, :] = jnp.full((1, LANES), wave_ref[t], F32)
-    coef_kernel(False, nu_out, sigma_out, cur_ref, c_out, r_out, edge_out, scale_out)
+    coef_kernel(False, nu_out, sigma_out, cur_ref, c_out, s_out, r_out, edge_out, scale_out)
 
 
 def unit_up(r):
@@ -138,7 +139,7 @@
     return r % BLOCK in (2, 4, 6)
 
 
-def coef_kernel(neumann, nu_ref, sigma_ref, coil_ref, c_out, r_out, edge_out, scale_out):
+def coef_kernel(neumann, nu_ref, sigma_ref, coil_ref, c_out, s_out, r_out, edge_out, scale_out):
     _, has_left, has_right = flags()
     sub = tile_index(0)
     lane = tile_index(1)
@@ -197,17 +198,13 @@
     put(c_out, DN_O, [dn_o[r] * around_o[r] * rec_o[r] for r in span])
     put(c_out, UP_E, [up_e[r] * around_e[r + 2] * rec_e[r] for r in span], lambda r: not unit_up(r))
     put(c_out, DN_E, [dn_e[r] * around_e[r] * rec_e[r] for r in span], lambda r: not unit_down(r))
-    def keep(slot, tiles):
-        for r in range(BLOCK):
-            r_out[r, slot] = tiles[r]
-
-    keep(SIG_E, [sigma_ref[r, 0] * inv_e[r] for r in span])
-    keep(SIG_O, [sigma_ref[r, 1] * inv_o[r] for r in span])
+    put(s_out, 0, [sigma_ref[r, 0] * inv_e[r] for r in span])
+    put(s_out, 1, [sigma_ref[r, 1] * inv_o[r] for r in span])
     if not neumann:
-        keep(COIL_E, [coil_ref[r, 0] * rec_e[r] for r in span])
-        keep(COIL_O, [coil_ref[r, 1] * rec_o[r] for r in span])
-    keep(FACE_E, [jnp.where((sub == 0) & has_left, rec_e[r], 0.0) for r in span])
-    keep(FACE_O, [jnp.where((sub == SUB - 1) & has_right, rec_o[r], 0.0) for r in span])
+        put(r_out, COIL_E, [coil_ref[r, 0] * rec_e[r] for r in span])
+        put(r_out, COIL_O, [coil_ref[r, 1] * rec_o[r] for r in span])
+    put(r_out, FACE_E, [jnp.where((sub == 0) & has_left, rec_e[r], 0.0) for r in span])
+    put(r_out, FACE_O, [jnp.where((sub == SUB - 1) & has_right, rec_o[r], 0.0) for r in span])
     for r in range(BLOCK):
         if not neumann:
             scale_out[r, 0] = scale_e[r]
@@ -218,8 +215,8 @@
         edge_out[3, r : r + 1] = scale_o[r][SUB - 1 : SUB]
 
 
-def neumann_coef_kernel(nu_ref, sigma_ref, c_out, r_out, edge_out):
-    coef_kernel(True, nu_ref, sigma_ref, None, c_out, r_out, edge_out, None)
+def neumann_coef_kernel(nu_ref, sigma_ref, c_out, s_out, r_out, edge_out):
+    coef_kernel(True, nu_ref, sigma_ref, None, c_out, s_out, r_out, edge_out, None)
 
 
 def advance(field_e, field_o, rhs, c_ref):
@@ -232,14 +229,16 @@
             new_e, new_o = {}, {}
             for r in range(k - DEPTH, BLOCK + DEPTH - k):
                 i = r - LOW
-                up = now_e[r + 1] if unit_up(r) else c_ref[i, UP_E] * now_e[r + 1]
-                down = now_e[r - 1] if unit_down(r) else c_ref[i, DN_E] * now_e[r - 1]
-                new_e[r] = (rhs[r][0] + now_o[r]) + (up + down) + c_ref[i, Q_E] * prev_sub(now_o[r])
-                new_o[r] = (
-                    (rhs[r][1] + c_ref[i, P_O] * now_e[r])
-                    + (c_ref[i, UP_O] * now_o[r + 1] + c_ref[i, DN_O] * now_o[r - 1])
-                    + c_ref[i, Q_O] * next_sub(now_e[r])
-                )
+                up_e = now_e[r + 1] if unit_up(r) else c_ref[i, UP_E] * now_e[r + 1]
+                dn_e = now_e[r - 1] if unit_down(r) else c_ref[i, DN_E] * now_e[r - 1]
+                up_o = c_ref[i, UP_O] * now_o[r + 1]
+                dn_o = c_ref[i, DN_O] * now_o[r - 1]
+                soon_e, late_e = (dn_e, up_e) if 2 * r >= BLOCK else (up_e, dn_e)
+                soon_o, late_o = (dn_o, up_o) if 2 * r >= BLOCK else (up_o, dn_o)
+                beside_e = now_o[r] + c_ref[i, Q_E] * prev_sub(now_o[r])
+                beside_o = c_ref[i, P_O] * now_e[r] + c_ref[i, Q_O] * next_sub(now_e[r])
+                new_e[r] = ((rhs[r][0] + soon_e) + beside_e) + late_e
+                new_o[r] = ((rhs[r][1] + soon_o) + beside_o) + late_o
             now_e, now_o = new_e, new_o
     return now_e, now_o
 
@@ -252,33 +251,60 @@
     return out
 
 
-def march(start, c_ref, r_ref, wave_ref, left, right, first, last, steps):
-    def step(t, carry):
+def march(start, c_ref, s_ref, r_ref, wave_ref, left, right, first, last, halo, steps):
+    def given_at(t, r):
+        f_e = f_o = None
+        if wave_ref is not None:
+            wave = wave_ref[pl.ds(t, 1), :]
+            f_e = r_ref[r - LOW, COIL_E] * wave
+            f_o = r_ref[r - LOW, COIL_O] * wave
+        if left is not None:
+            at = pl.ds(t * BLOCK + r, 1)
+            from_left = r_ref[r - LOW, FACE_E] * left[at, :]
+            from_right = r_ref[r - LOW, FACE_O] * right[at, :]
+            f_e = from_left if f_e is None else f_e + from_left
+            f_o = from_right if f_o is None else f_o + from_right
+        return f_e, f_o
+
+    halo_rows = [r for r in range(LOW, HIGH) if not 0 <= r < BLOCK]
+
+    def put_halo(t, slot):
+        for n, r in enumerate(halo_rows if halo is not None else ()):
+            shift = prev_lane if r < 0 else next_lane
+            for e, tile in enumerate(given_at(t, r % BLOCK)):
+                halo[slot, n, e] = shift(tile)
+
+    def step(t, slot, carry):
         now_e = haloed(dict(enumerate(carry[:BLOCK])))
         now_o = haloed(dict(enumerate(carry[BLOCK:])))
-        own = []
-        for r in range(BLOCK):
-            b_e = r_ref[r, SIG_E] * now_e[r]
-            b_o = r_ref[r, SIG_O] * now_o[r]
-            if wave_ref is not None:
-                wave = wave_ref[pl.ds(t, 1), :]
-                b_e = b_e + r_ref[r, COIL_E] * wave
-                b_o = b_o + r_ref[r, COIL_O] * wave
-            if left is not None:
-                at = pl.ds(t * BLOCK + r, 1)
-                b_e = b_e + r_ref[r, FACE_E] * left[at, :]
-                b_o = b_o + r_ref[r, FACE_O] * right[at, :]
-            own.append((b_e, b_o))
-        rhs_e = spread([pair[0] for pair in own])
-        rhs_o = spread([pair[1] for pair in own])
-        rhs = {r: (rhs_e[r], rhs_o[r]) for r in range(LOW, HIGH)}
+        given = {r: given_at(t, r) for r in range(BLOCK)}
+        for n, r in enumerate(halo_rows):
+            if halo is not None:
+                given[r] = halo[slot, n, 0], halo[slot, n, 1]
+            elif left is None:
+                given[r] = given_at(t, r)
+        rhs = {
+            r: (s_ref[r - LOW, 0] * now_e[r] + f_e, s_ref[r - LOW, 1] * now_o[r] + f_o)
+            for r, (f_e, f_o) in given.items()
+        }
+        for r in halo_rows:
+            if r not in rhs:
+                shift = prev_lane if r < 0 else next_lane
+                rhs[r] = shift(rhs[r % BLOCK][0]), shift(rhs[r % BLOCK][1])
         now_e, now_o = advance(now_e, now_o, rhs, c_ref)
+        put_halo(jnp.minimum(t + 1, steps - 1), 1 - slot)
         for r in range(BLOCK):
             first[pl.ds(t * BLOCK + r, 1), :] = now_e[r][0:1]
             last[pl.ds(t * BLOCK + r, 1), :] = now_o[r][SUB - 1 : SUB]
         return tuple(now_e[r] for r in range(BLOCK)) + tuple(now_o[r] for r in range(BLOCK))
 
-    return lax.fori_loop(0, steps, step, start, unroll=2)
+    def some_steps(i, carry):
+        for j in range(UNROLL):
+            carry = step(UNROLL * i + j, j % 2, carry)
+        return carry
+
+    put_halo(0, 0)
+    return lax.fori_loop(0, steps // UNROLL, some_steps, start)
 
 
 def at_step(ref, t):
@@ -287,11 +313,12 @@
 
 def dirichlet_kernel(sweep, steps, *refs):
     if sweep == 0:
-        (start_ref, c_ref, r_ref, scale_ref, edge_ref, wave_ref, ends, ev_out, od_out, first, last) = refs
+        (start_ref, c_ref, s_ref, r_ref, scale_ref, edge_ref, wave_ref, ends, ev_out, od_out, first, last) = refs
+        halo = None
         left = right = None
     else:
-        (start_ref, c_ref, r_ref, scale_ref, edge_ref, wave_ref, ev_own, od_own, ev_got, od_got,
-         ends, ev_out, od_out, g_right, first, last, left, right, g_left) = refs
+        (start_ref, c_ref, s_ref, r_ref, scale_ref, edge_ref, wave_ref, ev_own, od_own, ev_got, od_got,
+         ends, ev_out, od_out, g_right, first, last, left, right, g_left, halo) = refs
     even, _, _ = flags()
     if sweep > 0:
         for t in range(steps):
@@ -304,7 +331,7 @@
             left[t * BLOCK : (t + 1) * BLOCK, :] = edge_ref[0] * at_left
             right[t * BLOCK : (t + 1) * BLOCK, :] = edge_ref[1] * at_right
     start = tuple(start_ref[r, e] / scale_ref[r, e] for e in range(2) for r in range(BLOCK))
-    final = march(start, c_ref, r_ref, wave_ref, left, right, first, last, steps)
+    final = march(start, c_ref, s_ref, r_ref, wave_ref, left, right, first, last, halo, steps)
     for e in range(2):
         for r in range(BLOCK):
             ends[r, e] = final[e * BLOCK + r] * scale_ref[r, e]
@@ -322,9 +349,10 @@
 
 def neumann_kernel(sweep, steps, *refs):
     if sweep + 1 < SWEEPS:
-        (c_ref, r_ref, edge_ref, ev_own, od_own, ev_got, od_got, ev_out, od_out, first, last, left, right) = refs
+        (c_ref, s_ref, r_ref, edge_ref, ev_own, od_own, ev_got, od_got, ev_out, od_out,
+         first, last, left, right) = refs
     else:
-        (c_ref, r_ref, edge_ref, ev_own, od_own, ev_got, od_got, g_right, mine_out, first_out,
+        (c_ref, s_ref, r_ref, edge_ref, ev_own, od_own, ev_got, od_got, g_right, mine_out, ev_out, od_out,
          first, last, left, right, s0, s1) = refs
     even, _, _ = flags()
     for t in range(steps):
@@ -333,7 +361,7 @@
         left[t * BLOCK : (t + 1) * BLOCK, :] = jnp.where(even, od, ev)
         right[t * BLOCK : (t + 1) * BLOCK, :] = jnp.where(even, ev, od)
     zero = jnp.zeros((SUB, LANES), F32)
-    march((zero,) * (2 * BLOCK), c_ref, r_ref, None, left, right, first, last, steps)
+    march((zero,) * (2 * BLOCK), c_ref, s_ref, r_ref, None, left, right, first, last, None, steps)
     if sweep + 1 < SWEEPS:
         for t in range(steps):
             to_left = edge_ref[2] * at_step(first, t)
@@ -344,12 +372,13 @@
         for t in range(steps):
             s0[t * BLOCK : (t + 1) * BLOCK, :] = THETA * (edge_ref[2] * at_step(first, t))
             s1[t * BLOCK : (t + 1) * BLOCK, :] = at_step(g_right, t) + THETA * (edge_ref[3] * at_step(last, t))
-        for scratch, out in ((s0, first_out), (s1, mine_out)):
+        for scratch, outs in ((s0, (ev_out, od_out)), (s1, (mine_out,))):
             for half in range(steps // SUB):
                 base = half * SUB * BLOCK
                 tiles = from_blocks([scratch[pl.ds(base + r, SUB, stride=BLOCK), :] for r in range(BLOCK)])
                 for j in range(BLOCK):
-                    out[half * SUB : (half + 1) * SUB, j * LANES : (j + 1) * LANES] = tiles[j]
+                    for out in outs:
+                        out[half * SUB : (half + 1) * SUB, j * LANES : (j + 1) * LANES] = tiles[j]
 
 
 def natural_kernel(ends_ref, out, scratch):
@@ -395,49 +424,50 @@
             odd_faces.append((w * count + i, partner[0] * count + partner[1]))
     field = (BLOCK, 2, SUB, LANES)
     series = (steps * BLOCK, LANES)
-    coefs = [(ROWS, 7, SUB, LANES), (BLOCK, 6, SUB, LANES), (4, BLOCK, LANES)]
-    nu, sig, state, c_dir, r_dir, edge_dir, scale_dir, wave = call(
+    halo = (2, ROWS - BLOCK, 2, SUB, LANES)
+    coefs = [(ROWS, 7, SUB, LANES), (ROWS, 2, SUB, LANES), (ROWS, 4, SUB, LANES), (4, BLOCK, LANES)]
+    nu, sig, state, c_dir, s_dir, r_dir, edge_dir, scale_dir, wave = call(
         first_kernel, "first",
         [
             pltpu.with_memory_space_constraint(array, pltpu.HBM)
             for array in (labels, nu_table, sigma, coil, start_states, waveform)
         ],
-        [field, field, field, coefs[0], coefs[1], coefs[2], field, (steps, LANES)],
+        [field, field, field] + coefs + [field, (steps, LANES)],
         [
             pltpu.VMEM(labels.shape, jnp.int32), pltpu.SMEM(nu_table.shape, F32), sigma.shape, coil.shape,
             start_states.shape, pltpu.SMEM(waveform.shape, F32), field,
         ] + [(128, LANES)] * 4 + [pltpu.SemaphoreType.DMA((6,))],
         space=pltpu.HBM,
     )
-    c_neu, r_neu, edge_neu = call(neumann_coef_kernel, "coef_neu", [nu, sig], coefs)
+    c_neu, s_neu, r_neu, edge_neu = call(neumann_coef_kernel, "coef_neu", [nu, sig], coefs)
 
     def swapped(ev, od):
         return lax.ppermute(ev, "space", even_faces), lax.ppermute(od, ("tm", "space"), odd_faces)
 
     ends, ev, od = call(
         functools.partial(dirichlet_kernel, 0, steps), "dir0",
-        [state, c_dir, r_dir, scale_dir, edge_dir, wave], [field, series, series], [series] * 2,
+        [state, c_dir, s_dir, r_dir, scale_dir, edge_dir, wave], [field, series, series], [series] * 2,
     )
     state = lax.ppermute(ends, "tm", [(i, (i + 1) % windows) for i in range(windows)])
     ev_got, od_got = swapped(ev, od)
     ev, od = call(
         functools.partial(neumann_kernel, 0, steps), "neu0",
-        [c_neu, r_neu, edge_neu, ev, od, ev_got, od_got], [series] * 2, [series] * 2 + [series] * 2,
+        [c_neu, s_neu, r_neu, edge_neu, ev, od, ev_got, od_got], [series] * 2, [series] * 4,
     )
     ev_got, od_got = swapped(ev, od)
     ends, ev, od, g_right = call(
         functools.partial(dirichlet_kernel, 1, steps), "dir1",
-        [state, c_dir, r_dir, scale_dir, edge_dir, wave, ev, od, ev_got, od_got],
-        [field, series, series, series], [series] * 2 + [series] * 2 + [series],
+        [state, c_dir, s_dir, r_dir, scale_dir, edge_dir, wave, ev, od, ev_got, od_got],
+        [field, series, series, series], [series] * 5 + [halo],
     )
     ev_got, od_got = swapped(ev, od)
     end_states = call(natural_kernel, "natural", [ends], (1, columns, rows), [(128, LANES)])
-    mine, first = call(
+    mine, ev, od = call(
         functools.partial(neumann_kernel, 1, steps), "neu1",
-        [c_neu, r_neu, edge_neu, ev, od, ev_got, od_got, g_right],
-        [(steps, rows)] * 2, [series] * 2 + [series] * 2 + [series] * 2,
-    )
-    ev_got, od_got = swapped(first, first)
+        [c_neu, s_neu, r_neu, edge_neu, ev, od, ev_got, od_got, g_right],
+        [(steps, rows)] * 3, [series] * 6,
+    )
+    ev_got, od_got = swapped(ev, od)
     traces = call(join_kernel, "join", [mine, ev_got, od_got], (steps, rows))
     return end_states, traces
 

time: 46.4 us -> 44.5 us (0.959)
  the two profiles are of different devices: /device:TPU:0 before, /device:TPU:8 now
where the time goes in v6:
time: 44.5 us; the launch traced here: 44.4 us
  Pallas kernels  20 us (45%)
  waiting for transfers between devices  19.4 us (44%)
  starting transfers between devices  4.33 us (10%)
  between operations  0.68 us (2%)
    pallas_call x8, Pallas kernels, call(): pl.pallas_call(kernel, out_shape=shapes, in_specs=[pl.BlockSpec(memory_sp...  20 us
    ppermute x4, waiting for transfers between devices, swapped(): lax.ppermute(ev, 'space', even_faces)  11.9 us
    ppermute x4, waiting for transfers between devices, swapped(): lax.ppermute(od, ('tm', 'space'), odd_faces)  7.5 us
    ppermute x4, starting transfers between devices, swapped(): lax.ppermute(ev, 'space', even_faces)  4.31 us
  transfers between devices with their start and end apart: 9, of which 8 were waited for; matrix products, arithmetic and copies ran while one was open for 0% of the time, Pallas kernels for 12%

profile of v6, /device:TPU:8, one launch (start us, length us, event | category | flops | bytes accessed | tf_op | source)
XLA Modules:
  0.0 44.4 jit_solution(13585868213229967931)
XLA Ops:
  0.6 2.0 %first.1 = (f32[8,2,8,128]{3,2,1,0:T(8,128)S(1)}, f32[8,2,8,128]{3,2,1,0:T(8,128)S(1)}, f32[8,2,8,128]{3,2,1,0:T(8,128)S(1)}, f32[14,7,8,128]{3,2,1,0:T(8,128)S(...) custom-call(s32[16,1024]{1,0:T(8,128)} %labels_hbm.1, ...), custom_call_target="tpu_custom_call" | custom-call | tf_op jit(solution)/shard_map/first/pallas_call | solution.py:401
  2.7 3.8 %dir0.1 = (f32[8,2,8,128]{3,2,1,0:T(8,128)S(1)}, f32[128,128]{1,0:T(8,128)S(1)}, f32[128,128]{1,0:T(8,128)S(1)}) custom-call(f32[8,2,8,128]{3,2,1,0:T(8,128)S(1)} %get-tuple-element.27.refs_0_, f32[14,7,8,128]{3,2,1,0:T(8,128)S(1)} %get-tuple-element.28.refs_1_, f32[14,2,8,128]{3,2,1,0:T(8,128)S(1)} %get-tuple-element.29.refs_2_, ...), custom_call_target="tpu_custom_call" | custom-call | tf_op jit(solution)/shard_map/dir0/pallas_call | solution.py:401
  6.4 1.6 %collective-permute-start.1 = (f32[128,128]{1,0:T(8,128)S(1)}, f32[128,128]{1,0:T(8,128)S(1)}, u32[]{:S(2)}, u32[]{:S(2)}) collective-permute-start(f32[128,128]{1,0:T(8,128)S(1)} %get-tuple-element.41.refs_4_), channel_id=1, source_target_pairs={{0,1},{1,0},{2,3},{3,2},{4,5},{5,4},{6,7},{7,6},{8,9},{9,8},{10,11... | collective-permute-start | bytes 196616 | tf_op jit(solution)/shard_map/ppermute | solution.py:445
  8.0 0.0 collective-permute-start.2
  8.0 0.0 collective-permute-start
  8.0 0.3 coef_neu.1
  8.3 2.4 %collective-permute-done.1.refs_6_ = f32[128,128]{1,0:T(8,128)S(1)} collective-permute-done((f32[128,128]{1,0:T(8,128)S(1)}, f32[128,128]{1,0:T(8,128)S(1)}, u32[]{:S(2)}, u32[]{:S(2)}) %collective-permute-start.1) | collective-permute-done | bytes 65568 | tf_op jit(solution)/shard_map/ppermute | solution.py:445
  10.8 2.4 %collective-permute-done.2.refs_7_ = f32[128,128]{1,0:T(8,128)S(1)} collective-permute-done((f32[128,128]{1,0:T(8,128)S(1)}, f32[128,128]{1,0:T(8,128)S(1)}, u32[]{:S(2)}, u32[]{:S(2)}) %collective-permute-start.2) | collective-permute-done | bytes 65568 | tf_op jit(solution)/shard_map/ppermute | solution.py:445
  13.2 4.0 %neu0.1 = (f32[128,128]{1,0:T(8,128)S(1)}, f32[128,128]{1,0:T(8,128)S(1)}) custom-call(f32[14,7,8,128]{3,2,1,0:T(8,128)S(1)} %get-tuple-element.37.refs_0_, f32[14,2,8,128]{3,2,1,0:T(8,128)S(1)} %get-tuple-element.38.refs_1_, f32[14,4,8,128]{3,2,1,0:T(8,128)S(1)} %get-tuple-element.39.refs_2_, f32[4,8,128]{2,1,0:T(8,128)S(1)} %get-tuple-element.40.refs_3_, ...), custom_call_target="tpu_custom_call" | custom-call | tf_op jit(solution)/shard_map/neu0/pallas_call | solution.py:401
  17.2 0.6 %collective-permute-start.3 = (f32[128,128]{1,0:T(8,128)S(1)}, f32[128,128]{1,0:T(8,128)S(1)}, u32[]{:S(2)}, u32[]{:S(2)}) collective-permute-start(f32[128,128]{1,0:T(8,128)S(1)} %get-tuple-element.43.refs_7_), channel_id=1, source_target_pairs={{0,1},{1,0},{2,3},{3,2},{4,5},{5,4},{6,7},{7,6},{8,9},{9,8},{10,11... | collective-permute-start | bytes 196616 | tf_op jit(solution)/shard_map/ppermute | solution.py:445
  17.8 0.0 collective-permute-start.4
  17.8 0.0 collective-permute-done.refs_0_
  17.8 3.9 %collective-permute-done.3.refs_9_ = f32[128,128]{1,0:T(8,128)S(1)} collective-permute-done((f32[128,128]{1,0:T(8,128)S(1)}, f32[128,128]{1,0:T(8,128)S(1)}, u32[]{:S(2)}, u32[]{:S(2)}) %collective-permute-start.3) | collective-permute-done | bytes 65568 | tf_op jit(solution)/shard_map/ppermute | solution.py:445
  21.7 1.3 %collective-permute-done.4.refs_10_ = f32[128,128]{1,0:T(8,128)S(1)} collective-permute-done((f32[128,128]{1,0:T(8,128)S(1)}, f32[128,128]{1,0:T(8,128)S(1)}, u32[]{:S(2)}, u32[]{:S(2)}) %collective-permute-start.4) | collective-permute-done | bytes 65568 | tf_op jit(solution)/shard_map/ppermute | solution.py:445
  22.9 3.9 %dir1.1 = (f32[8,2,8,128]{3,2,1,0:T(8,128)S(1)}, f32[128,128]{1,0:T(8,128)S(1)}, f32[128,128]{1,0:T(8,128)S(1)}, f32[128,128]{1,0:T(8,128)S(1)}) custom-call(f32[8,2,8,128]{3,2,1,0:T(8,128)S(1)} %collective-permute-done.refs_0_, f32[14,7,8,128]{3,2,1,0:T(8,128)S(1)} %get-tuple-element.28.refs_1_, f32[14,2,8,128]{3,2,1,0:T(8,128)S(1)} %get-tuple-element.29.refs_2_, ...), custom_call_target="tpu_custom_call" | custom-call | tf_op jit(solution)/shard_map/dir1/pallas_call | solution.py:401
  26.9 1.6 %collective-permute-start.5 = (f32[128,128]{1,0:T(8,128)S(1)}, f32[128,128]{1,0:T(8,128)S(1)}, u32[]{:S(2)}, u32[]{:S(2)}) collective-permute-start(f32[128,128]{1,0:T(8,128)S(1)} %get-tuple-element.46.refs_4_), channel_id=1, source_target_pairs={{0,1},{1,0},{2,3},{3,2},{4,5},{5,4},{6,7},{7,6},{8,9},{9,8},{10,11... | collective-permute-start | bytes 196616 | tf_op jit(solution)/shard_map/ppermute | solution.py:445
  28.5 0.0 collective-permute-start.6
  28.5 2.7 %collective-permute-done.5.refs_6_ = f32[128,128]{1,0:T(8,128)S(1)} collective-permute-done((f32[128,128]{1,0:T(8,128)S(1)}, f32[128,128]{1,0:T(8,128)S(1)}, u32[]{:S(2)}, u32[]{:S(2)}) %collective-permute-start.5) | collective-permute-done | bytes 65568 | tf_op jit(solution)/shard_map/ppermute | solution.py:445
  31.2 2.4 %collective-permute-done.6.refs_7_ = f32[128,128]{1,0:T(8,128)S(1)} collective-permute-done((f32[128,128]{1,0:T(8,128)S(1)}, f32[128,128]{1,0:T(8,128)S(1)}, u32[]{:S(2)}, u32[]{:S(2)}) %collective-permute-start.6) | collective-permute-done | bytes 65568 | tf_op jit(solution)/shard_map/ppermute | solution.py:445
  33.6 4.3 %neu1.1 = (f32[16,1024]{1,0:T(8,128)S(1)}, f32[16,1024]{1,0:T(8,128)S(1)}, f32[16,1024]{1,0:T(8,128)S(1)}) custom-call(f32[14,7,8,128]{3,2,1,0:T(8,128)S(1)} %get-tuple-element.37.refs_0_, f32[14,2,8,128]{3,2,1,0:T(8,128)S(1)} %get-tuple-element.38.refs_1_, f32[14,4,8,128]{3,2,1,0:T(8,128)S(1)} %get-tuple-element.39.refs_2_, ...), custom_call_target="tpu_custom_call" | custom-call | tf_op jit(solution)/shard_map/neu1/pallas_call | solution.py:401
  38.0 0.6 %collective-permute-start.7 = (f32[16,1024]{1,0:T(8,128)S(1)}, f32[16,1024]{1,0:T(8,128)S(1)}, u32[]{:S(2)}, u32[]{:S(2)}) collective-permute-start(f32[16,1024]{1,0:T(8,128)S(1)} %get-tuple-element.50), channel_id=1, source_target_pairs={{0,1},{1,0},{2,3},{3,2},{4,5},{5,4},{6,7},{7,6},{8,9},{9,8},{10,11... | collective-permute-start | bytes 196616 | tf_op jit(solution)/shard_map/ppermute | solution.py:445
  38.5 0.0 collective-permute-start.8
  38.6 0.9 %natural.1 = f32[1,16,1024]{2,1,0:T(8,128)} custom-call(f32[8,2,8,128]{3,2,1,0:T(8,128)S(1)} %get-tuple-element.45.ends_ref), custom_call_target="tpu_custom_call" | custom-call | tf_op jit(solution)/shard_map/natural/pallas_call | solution.py:401
  39.5 2.8 %collective-permute-done.7.ev_ref = f32[16,1024]{1,0:T(8,128)S(1)} collective-permute-done((f32[16,1024]{1,0:T(8,128)S(1)}, f32[16,1024]{1,0:T(8,128)S(1)}, u32[]{:S(2)}, u32[]{:S(2)}) %collective-permute-start.7) | collective-permute-done | bytes 65568 | tf_op jit(solution)/shard_map/ppermute | solution.py:445
  42.3 1.4 %collective-permute-done.8.od_ref = f32[16,1024]{1,0:T(8,128)S(1)} collective-permute-done((f32[16,1024]{1,0:T(8,128)S(1)}, f32[16,1024]{1,0:T(8,128)S(1)}, u32[]{:S(2)}, u32[]{:S(2)}) %collective-permute-start.8) | collective-permute-done | bytes 65568 | tf_op jit(solution)/shard_map/ppermute | solution.py:445
  43.7 0.6 %join.1 = f32[16,1024]{1,0:T(8,128)} custom-call(f32[16,1024]{1,0:T(8,128)S(1)} %get-tuple-element.49.mine_ref, f32[16,1024]{1,0:T(8,128)S(1)} %collective-permute-done.7.ev_ref, f32[16,1024]{1,0:T(8,128)S(1)} %collective-permute-done.8.od_ref), custom_call_target="tpu_custom_call" | custom-call | tf_op jit(solution)/shard_map/join/pallas_call | solution.py:401
Async XLA Ops:
  6.4 4.3 %collective-permute-start.1 = (f32[128,128]{1,0:T(8,128)S(1)}, f32[128,128]{1,0:T(8,128)S(1)}, u32[]{:S(2)}, u32[]{:S(2)}) collective-permute-start(f32[128,128]{1,0:T(8,128)S(1)} %get-tuple-element.41.refs_4_), channel_id=1, source_target_pairs={{0,1},{1,0},{2,3},{3,2},{4,5},{5,4},{6,7},{7,6},{8,9},{9,8},{10,11... | collective-permute-start | bytes 196616 | tf_op jit(solution)/shard_map/ppermute | solution.py:445
  8.0 5.2 %collective-permute-start.2 = (f32[128,128]{1,0:T(8,128)S(1)}, f32[128,128]{1,0:T(8,128)S(1)}, u32[]{:S(2)}, u32[]{:S(2)}) collective-permute-start(f32[128,128]{1,0:T(8,128)S(1)} %get-tuple-element.42.refs_5_), channel_id=1, source_target_pairs={{0,8},{1,2},{2,1},{3,4},{4,3},{5,6},{6,5},{7,15},{8,0},{9,10},{10,... | collective-permute-start | bytes 196616 | tf_op jit(solution)/shard_map/ppermute | solution.py:445
  8.0 9.8 %collective-permute-start = (f32[8,2,8,128]{3,2,1,0:T(8,128)S(1)}, f32[8,2,8,128]{3,2,1,0:T(8,128)S(1)}, u32[]{:S(2)}, u32[]{:S(2)}) collective-permute-start(f32[8,2,8,128]{3,2,1,0:T(8,128)S(1)} %get-tuple-element.34), channel_id=1, source_target_pairs={{0,8},{8,16},{16,24},{24,0},{1,9},{9,17},{17,25},{25,1},{2,10},{10... | collective-permute-start | bytes 196616 | tf_op jit(solution)/shard_map/ppermute | solution.py:451
  17.2 4.5 %collective-permute-start.3 = (f32[128,128]{1,0:T(8,128)S(1)}, f32[128,128]{1,0:T(8,128)S(1)}, u32[]{:S(2)}, u32[]{:S(2)}) collective-permute-start(f32[128,128]{1,0:T(8,128)S(1)} %get-tuple-element.43.refs_7_), channel_id=1, source_target_pairs={{0,1},{1,0},{2,3},{3,2},{4,5},{5,4},{6,7},{7,6},{8,9},{9,8},{10,11... | collective-permute-start | bytes 196616 | tf_op jit(solution)/shard_map/ppermute | solution.py:445
  17.8 5.2 %collective-permute-start.4 = (f32[128,128]{1,0:T(8,128)S(1)}, f32[128,128]{1,0:T(8,128)S(1)}, u32[]{:S(2)}, u32[]{:S(2)}) collective-permute-start(f32[128,128]{1,0:T(8,128)S(1)} %get-tuple-element.44.refs_8_), channel_id=1, source_target_pairs={{0,8},{1,2},{2,1},{3,4},{4,3},{5,6},{6,5},{7,15},{8,0},{9,10},{10,... | collective-permute-start | bytes 196616 | tf_op jit(solution)/shard_map/ppermute | solution.py:445
  26.9 4.3 %collective-permute-start.5 = (f32[128,128]{1,0:T(8,128)S(1)}, f32[128,128]{1,0:T(8,128)S(1)}, u32[]{:S(2)}, u32[]{:S(2)}) collective-permute-start(f32[128,128]{1,0:T(8,128)S(1)} %get-tuple-element.46.refs_4_), channel_id=1, source_target_pairs={{0,1},{1,0},{2,3},{3,2},{4,5},{5,4},{6,7},{7,6},{8,9},{9,8},{10,11... | collective-permute-start | bytes 196616 | tf_op jit(solution)/shard_map/ppermute | solution.py:445
  28.5 5.2 %collective-permute-start.6 = (f32[128,128]{1,0:T(8,128)S(1)}, f32[128,128]{1,0:T(8,128)S(1)}, u32[]{:S(2)}, u32[]{:S(2)}) collective-permute-start(f32[128,128]{1,0:T(8,128)S(1)} %get-tuple-element.47.refs_5_), channel_id=1, source_target_pairs={{0,8},{1,2},{2,1},{3,4},{4,3},{5,6},{6,5},{7,15},{8,0},{9,10},{10,... | collective-permute-start | bytes 196616 | tf_op jit(solution)/shard_map/ppermute | solution.py:445
  38.0 4.3 %collective-permute-start.7 = (f32[16,1024]{1,0:T(8,128)S(1)}, f32[16,1024]{1,0:T(8,128)S(1)}, u32[]{:S(2)}, u32[]{:S(2)}) collective-permute-start(f32[16,1024]{1,0:T(8,128)S(1)} %get-tuple-element.50), channel_id=1, source_target_pairs={{0,1},{1,0},{2,3},{3,2},{4,5},{5,4},{6,7},{7,6},{8,9},{9,8},{10,11... | collective-permute-start | bytes 196616 | tf_op jit(solution)/shard_map/ppermute | solution.py:445
  38.5 5.2 %collective-permute-start.8 = (f32[16,1024]{1,0:T(8,128)S(1)}, f32[16,1024]{1,0:T(8,128)S(1)}, u32[]{:S(2)}, u32[]{:S(2)}) collective-permute-start(f32[16,1024]{1,0:T(8,128)S(1)} %get-tuple-element.51), channel_id=1, source_target_pairs={{0,8},{1,2},{2,1},{3,4},{4,3},{5,6},{6,5},{7,15},{8,0},{9,10},{10,... | collective-permute-start | bytes 196616 | tf_op jit(solution)/shard_map/ppermute | solution.py:445

commit v7 on v6

--- a/solution.py
+++ b/solution.py
@@ -152,14 +152,14 @@
     def upward(nu):
         ups = [harmonic(nu[r], nu[r + 1]) for r in range(BLOCK - 1)]
         ups.append(jnp.where(lane == LANES - 1, 0.0, harmonic(nu[BLOCK - 1], next_lane(nu[0]))))
-        downs = [prev_lane(ups[BLOCK - 1])] + ups[:-1]
+        downs = [jnp.where(lane == 0, 0.0, harmonic(prev_lane(nu[BLOCK - 1]), nu[0]))] + ups[:-1]
         return ups, downs
 
     up_e, dn_e = upward(nu_e)
     up_o, dn_o = upward(nu_o)
     left_kept = jnp.logical_not(has_left) if neumann else True
     right_kept = jnp.logical_not(has_right) if neumann else True
-    inv_e, inv_o, sig_e, sig_o = [], [], [], []
+    all_e, all_o = [], []
     for r in range(BLOCK):
         d_e = sigma_ref[r, 0] + pair[r] + cross_e[r] + up_e[r] + dn_e[r]
         d_o = sigma_ref[r, 1] + pair[r] + cross_o[r] + up_o[r] + dn_o[r]
@@ -167,20 +167,22 @@
             on_edge = lane == (0 if r == 0 else LANES - 1)
             d_e = d_e + jnp.where(on_edge, 2.0 * nu_e[r], 0.0)
             d_o = d_o + jnp.where(on_edge, 2.0 * nu_o[r], 0.0)
-        d_e = d_e + jnp.where((sub == 0) & left_kept, 2.0 * nu_e[r], 0.0)
-        d_o = d_o + jnp.where((sub == SUB - 1) & right_kept, 2.0 * nu_o[r], 0.0)
-        inv_e.append(1.0 / d_e)
-        inv_o.append(1.0 / d_o)
-    scale_e, scale_o = [jnp.ones((SUB, LANES), F32)], []
+        all_e.append(d_e + jnp.where((sub == 0) & left_kept, 2.0 * nu_e[r], 0.0))
+        all_o.append(d_o + jnp.where((sub == SUB - 1) & right_kept, 2.0 * nu_o[r], 0.0))
+    inv_e = [1.0 / d for d in all_e]
+    inv_o = [1.0 / d for d in all_o]
+    scale_e, over_e = [jnp.ones((SUB, LANES), F32)], [jnp.ones((SUB, LANES), F32)]
     for r in range(1, BLOCK):
-        if unit_down(r):
-            scale_e.append(scale_e[r - 1] * (dn_e[r] * inv_e[r]))
-        else:
-            scale_e.append(scale_e[r - 1] / (up_e[r - 1] * inv_e[r - 1]))
-    for r in range(BLOCK):
-        scale_o.append(scale_e[r] / (pair[r] * inv_e[r]))
-    rec_e = [inv_e[r] / scale_e[r] for r in range(BLOCK)]
-    rec_o = [inv_o[r] / scale_o[r] for r in range(BLOCK)]
+        link = up_e[r - 1]
+        even = r if r % 2 == 0 else r - 1
+        there, back = link * inv_e[even], all_e[even] / link
+        if even == r:
+            there, back = back, there
+        scale_e.append(scale_e[r - 1] * back)
+        over_e.append(over_e[r - 1] * there)
+    scale_o = [scale_e[r] * (all_e[r] / pair[r]) for r in range(BLOCK)]
+    rec_e = [inv_e[r] * over_e[r] for r in range(BLOCK)]
+    rec_o = [inv_o[r] * (over_e[r] * (pair[r] * inv_e[r])) for r in range(BLOCK)]
     around_e = [prev_lane(scale_e[BLOCK - 1])] + scale_e + [next_lane(scale_e[0])]
     around_o = [prev_lane(scale_o[BLOCK - 1])] + scale_o + [next_lane(scale_o[0])]
 
@@ -347,13 +349,9 @@
         od_out[t * BLOCK : (t + 1) * BLOCK, :] = jnp.where(even, to_left, to_right)
 
 
-def neumann_kernel(sweep, steps, *refs):
-    if sweep + 1 < SWEEPS:
-        (c_ref, s_ref, r_ref, edge_ref, ev_own, od_own, ev_got, od_got, ev_out, od_out,
-         first, last, left, right) = refs
-    else:
-        (c_ref, s_ref, r_ref, edge_ref, ev_own, od_own, ev_got, od_got, g_right, mine_out, ev_out, od_out,
-         first, last, left, right, s0, s1) = refs
+def neumann_kernel(
+    steps, c_ref, s_ref, r_ref, edge_ref, ev_own, od_own, ev_got, od_got, ev_out, od_out, first, last, left, right
+):
     even, _, _ = flags()
     for t in range(steps):
         ev = at_step(ev_own, t) + at_step(ev_got, t)
@@ -362,23 +360,11 @@
         right[t * BLOCK : (t + 1) * BLOCK, :] = jnp.where(even, ev, od)
     zero = jnp.zeros((SUB, LANES), F32)
     march((zero,) * (2 * BLOCK), c_ref, s_ref, r_ref, None, left, right, first, last, None, steps)
-    if sweep + 1 < SWEEPS:
-        for t in range(steps):
-            to_left = edge_ref[2] * at_step(first, t)
-            to_right = edge_ref[3] * at_step(last, t)
-            ev_out[t * BLOCK : (t + 1) * BLOCK, :] = jnp.where(even, to_right, to_left)
-            od_out[t * BLOCK : (t + 1) * BLOCK, :] = jnp.where(even, to_left, to_right)
-    else:
-        for t in range(steps):
-            s0[t * BLOCK : (t + 1) * BLOCK, :] = THETA * (edge_ref[2] * at_step(first, t))
-            s1[t * BLOCK : (t + 1) * BLOCK, :] = at_step(g_right, t) + THETA * (edge_ref[3] * at_step(last, t))
-        for scratch, outs in ((s0, (ev_out, od_out)), (s1, (mine_out,))):
-            for half in range(steps // SUB):
-                base = half * SUB * BLOCK
-                tiles = from_blocks([scratch[pl.ds(base + r, SUB, stride=BLOCK), :] for r in range(BLOCK)])
-                for j in range(BLOCK):
-                    for out in outs:
-                        out[half * SUB : (half + 1) * SUB, j * LANES : (j + 1) * LANES] = tiles[j]
+    for t in range(steps):
+        to_left = edge_ref[2] * at_step(first, t)
+        to_right = edge_ref[3] * at_step(last, t)
+        ev_out[t * BLOCK : (t + 1) * BLOCK, :] = jnp.where(even, to_right, to_left)
+        od_out[t * BLOCK : (t + 1) * BLOCK, :] = jnp.where(even, to_left, to_right)
 
 
 def natural_kernel(ends_ref, out, scratch):
@@ -390,9 +376,18 @@
         out[0, :, LANES * j : LANES * j + LANES] = scratch[16 * j : 16 * j + 16, :]
 
 
-def join_kernel(mine_ref, ev_ref, od_ref, out):
+def join_kernel(steps, g_right, ev_own, od_own, ev_got, od_got, out, scratch):
     even, _, has_right = flags()
-    out[...] = jnp.where(has_right, mine_ref[...] + jnp.where(even, ev_ref[...], od_ref[...]), 0.0)
+    for t in range(steps):
+        ev = at_step(ev_own, t) + at_step(ev_got, t)
+        od = at_step(od_own, t) + at_step(od_got, t)
+        total = at_step(g_right, t) + THETA * jnp.where(even, ev, od)
+        scratch[t * BLOCK : (t + 1) * BLOCK, :] = jnp.where(has_right, total, 0.0)
+    for half in range(steps // SUB):
+        base = half * SUB * BLOCK
+        tiles = from_blocks([scratch[pl.ds(base + r, SUB, stride=BLOCK), :] for r in range(BLOCK)])
+        for j in range(BLOCK):
+            out[half * SUB : (half + 1) * SUB, j * LANES : (j + 1) * LANES] = tiles[j]
 
 
 def call(kernel, name, inputs, outputs, scratch=(), space=pltpu.VMEM):
@@ -450,10 +445,13 @@
     )
     state = lax.ppermute(ends, "tm", [(i, (i + 1) % windows) for i in range(windows)])
     ev_got, od_got = swapped(ev, od)
-    ev, od = call(
-        functools.partial(neumann_kernel, 0, steps), "neu0",
-        [c_neu, s_neu, r_neu, edge_neu, ev, od, ev_got, od_got], [series] * 2, [series] * 4,
-    )
+    def neumann(*series_pairs):
+        return call(
+            functools.partial(neumann_kernel, steps), "neu",
+            [c_neu, s_neu, r_neu, edge_neu, *series_pairs], [series] * 2, [series] * 4,
+        )
+
+    ev, od = neumann(ev, od, ev_got, od_got)
     ev_got, od_got = swapped(ev, od)
     ends, ev, od, g_right = call(
         functools.partial(dirichlet_kernel, 1, steps), "dir1",
@@ -462,13 +460,11 @@
     )
     ev_got, od_got = swapped(ev, od)
     end_states = call(natural_kernel, "natural", [ends], (1, columns, rows), [(128, LANES)])
-    mine, ev, od = call(
-        functools.partial(neumann_kernel, 1, steps), "neu1",
-        [c_neu, s_neu, r_neu, edge_neu, ev, od, ev_got, od_got, g_right],
-        [(steps, rows)] * 3, [series] * 6,
-    )
+    ev, od = neumann(ev, od, ev_got, od_got)
     ev_got, od_got = swapped(ev, od)
-    traces = call(join_kernel, "join", [mine, ev_got, od_got], (steps, rows))
+    traces = call(
+        functools.partial(join_kernel, steps), "join", [g_right, ev, od, ev_got, od_got], (steps, rows), [series]
+    )
     return end_states, traces
 
 

time: 44.5 us -> 44.5 us (level)
  no operation moved by 1% of the time
where the time goes in v7:
time: 44.5 us; the launch traced here: 44.3 us
  Pallas kernels  19.8 us (44%)
  waiting for transfers between devices  19.5 us (44%)
  starting transfers between devices  4.33 us (10%)
  between operations  0.68 us (2%)
    pallas_call x8, Pallas kernels, call(): pl.pallas_call(kernel, out_shape=shapes, in_specs=[pl.BlockSpec(memory_sp...  19.8 us
    ppermute x4, waiting for transfers between devices, swapped(): lax.ppermute(ev, 'space', even_faces)  11.9 us
    ppermute x4, waiting for transfers between devices, swapped(): lax.ppermute(od, ('tm', 'space'), odd_faces)  7.57 us
    ppermute x4, starting transfers between devices, swapped(): lax.ppermute(ev, 'space', even_faces)  4.31 us
  transfers between devices with their start and end apart: 9, of which 8 were waited for; matrix products, arithmetic and copies ran while one was open for 0% of the time, Pallas kernels for 12%

profile of v7, /device:TPU:8, one launch (start us, length us, event | category | flops | bytes accessed | tf_op | source)
XLA Modules:
  0.0 44.3 jit_solution(15309018660185597468)
XLA Ops:
  0.6 2.0 %first.1 = (f32[8,2,8,128]{3,2,1,0:T(8,128)S(1)}, f32[8,2,8,128]{3,2,1,0:T(8,128)S(1)}, f32[8,2,8,128]{3,2,1,0:T(8,128)S(1)}, f32[14,7,8,128]{3,2,1,0:T(8,128)S(...) custom-call(s32[16,1024]{1,0:T(8,128)} %labels_hbm.1, ...), custom_call_target="tpu_custom_call" | custom-call | tf_op jit(solution)/shard_map/first/pallas_call | solution.py:396
  2.6 3.8 %dir0.1 = (f32[8,2,8,128]{3,2,1,0:T(8,128)S(1)}, f32[128,128]{1,0:T(8,128)S(1)}, f32[128,128]{1,0:T(8,128)S(1)}) custom-call(f32[8,2,8,128]{3,2,1,0:T(8,128)S(1)} %get-tuple-element.26.refs_0_, f32[14,7,8,128]{3,2,1,0:T(8,128)S(1)} %get-tuple-element.27.refs_1_, f32[14,2,8,128]{3,2,1,0:T(8,128)S(1)} %get-tuple-element.28.refs_2_, ...), custom_call_target="tpu_custom_call" | custom-call | tf_op jit(solution)/shard_map/dir0/pallas_call | solution.py:396
  6.4 1.6 %collective-permute-start.1 = (f32[128,128]{1,0:T(8,128)S(1)}, f32[128,128]{1,0:T(8,128)S(1)}, u32[]{:S(2)}, u32[]{:S(2)}) collective-permute-start(f32[128,128]{1,0:T(8,128)S(1)} %get-tuple-element.40.ev_own), channel_id=1, source_target_pairs={{0,1},{1,0},{2,3},{3,2},{4,5},{5,4},{6,7},{7,6},{8,9},{9,8},{10,11... | collective-permute-start | bytes 196616 | tf_op jit(solution)/shard_map/ppermute | solution.py:440
  8.0 0.0 collective-permute-start.2
  8.0 0.0 collective-permute-start
  8.0 0.2 coef_neu.1
  8.2 2.5 %collective-permute-done.1.ev_got = f32[128,128]{1,0:T(8,128)S(1)} collective-permute-done((f32[128,128]{1,0:T(8,128)S(1)}, f32[128,128]{1,0:T(8,128)S(1)}, u32[]{:S(2)}, u32[]{:S(2)}) %collective-permute-start.1) | collective-permute-done | bytes 65568 | tf_op jit(solution)/shard_map/ppermute | solution.py:440
  10.7 2.4 %collective-permute-done.2.od_got = f32[128,128]{1,0:T(8,128)S(1)} collective-permute-done((f32[128,128]{1,0:T(8,128)S(1)}, f32[128,128]{1,0:T(8,128)S(1)}, u32[]{:S(2)}, u32[]{:S(2)}) %collective-permute-start.2) | collective-permute-done | bytes 65568 | tf_op jit(solution)/shard_map/ppermute | solution.py:440
  13.1 4.0 %neu.2 = (f32[128,128]{1,0:T(8,128)S(1)}, f32[128,128]{1,0:T(8,128)S(1)}) custom-call(f32[14,7,8,128]{3,2,1,0:T(8,128)S(1)} %get-tuple-element.36.c_ref, f32[14,2,8,128]{3,2,1,0:T(8,128)S(1)} %get-tuple-element.37.s_ref, f32[14,4,8,128]{3,2,1,0:T(8,128)S(1)} %get-tuple-element.38.r_ref, f32[4,8,128]{2,1,0:T(8,128)S(1)} %get-tuple-element.39.edge_ref, ...), custom_call_target="tpu_custom_call" | custom-call | tf_op jit(solution)/shard_map/neu/pallas_call | solution.py:396
  17.2 0.6 %collective-permute-start.3 = (f32[128,128]{1,0:T(8,128)S(1)}, f32[128,128]{1,0:T(8,128)S(1)}, u32[]{:S(2)}, u32[]{:S(2)}) collective-permute-start(f32[128,128]{1,0:T(8,128)S(1)} %get-tuple-element.42.refs_7_), channel_id=1, source_target_pairs={{0,1},{1,0},{2,3},{3,2},{4,5},{5,4},{6,7},{7,6},{8,9},{9,8},{10,11... | collective-permute-start | bytes 196616 | tf_op jit(solution)/shard_map/ppermute | solution.py:440
  17.7 0.0 collective-permute-start.4
  17.7 0.0 collective-permute-done.refs_0_
  17.7 3.8 %collective-permute-done.3.refs_9_ = f32[128,128]{1,0:T(8,128)S(1)} collective-permute-done((f32[128,128]{1,0:T(8,128)S(1)}, f32[128,128]{1,0:T(8,128)S(1)}, u32[]{:S(2)}, u32[]{:S(2)}) %collective-permute-start.3) | collective-permute-done | bytes 65568 | tf_op jit(solution)/shard_map/ppermute | solution.py:440
  21.6 1.3 %collective-permute-done.4.refs_10_ = f32[128,128]{1,0:T(8,128)S(1)} collective-permute-done((f32[128,128]{1,0:T(8,128)S(1)}, f32[128,128]{1,0:T(8,128)S(1)}, u32[]{:S(2)}, u32[]{:S(2)}) %collective-permute-start.4) | collective-permute-done | bytes 65568 | tf_op jit(solution)/shard_map/ppermute | solution.py:440
  22.9 3.9 %dir1.1 = (f32[8,2,8,128]{3,2,1,0:T(8,128)S(1)}, f32[128,128]{1,0:T(8,128)S(1)}, f32[128,128]{1,0:T(8,128)S(1)}, f32[128,128]{1,0:T(8,128)S(1)}) custom-call(f32[8,2,8,128]{3,2,1,0:T(8,128)S(1)} %collective-permute-done.refs_0_, f32[14,7,8,128]{3,2,1,0:T(8,128)S(1)} %get-tuple-element.27.refs_1_, f32[14,2,8,128]{3,2,1,0:T(8,128)S(1)} %get-tuple-element.28.refs_2_, ...), custom_call_target="tpu_custom_call" | custom-call | tf_op jit(solution)/shard_map/dir1/pallas_call | solution.py:396
  26.8 1.6 %collective-permute-start.5 = (f32[128,128]{1,0:T(8,128)S(1)}, f32[128,128]{1,0:T(8,128)S(1)}, u32[]{:S(2)}, u32[]{:S(2)}) collective-permute-start(f32[128,128]{1,0:T(8,128)S(1)} %get-tuple-element.46.ev_own), channel_id=1, source_target_pairs={{0,1},{1,0},{2,3},{3,2},{4,5},{5,4},{6,7},{7,6},{8,9},{9,8},{10,11... | collective-permute-start | bytes 196616 | tf_op jit(solution)/shard_map/ppermute | solution.py:440
  28.4 0.0 collective-permute-start.6
  28.4 2.7 %collective-permute-done.5.ev_got = f32[128,128]{1,0:T(8,128)S(1)} collective-permute-done((f32[128,128]{1,0:T(8,128)S(1)}, f32[128,128]{1,0:T(8,128)S(1)}, u32[]{:S(2)}, u32[]{:S(2)}) %collective-permute-start.5) | collective-permute-done | bytes 65568 | tf_op jit(solution)/shard_map/ppermute | solution.py:440
  31.2 2.4 %collective-permute-done.6.od_got = f32[128,128]{1,0:T(8,128)S(1)} collective-permute-done((f32[128,128]{1,0:T(8,128)S(1)}, f32[128,128]{1,0:T(8,128)S(1)}, u32[]{:S(2)}, u32[]{:S(2)}) %collective-permute-start.6) | collective-permute-done | bytes 65568 | tf_op jit(solution)/shard_map/ppermute | solution.py:440
  33.6 4.0 %neu.3 = (f32[128,128]{1,0:T(8,128)S(1)}, f32[128,128]{1,0:T(8,128)S(1)}) custom-call(f32[14,7,8,128]{3,2,1,0:T(8,128)S(1)} %get-tuple-element.36.c_ref, f32[14,2,8,128]{3,2,1,0:T(8,128)S(1)} %get-tuple-element.37.s_ref, f32[14,4,8,128]{3,2,1,0:T(8,128)S(1)} %get-tuple-element.38.r_ref, f32[4,8,128]{2,1,0:T(8,128)S(1)} %get-tuple-element.39.edge_ref, ...), custom_call_target="tpu_custom_call" | custom-call | tf_op jit(solution)/shard_map/neu/pallas_call | solution.py:396
  37.6 0.6 %collective-permute-start.7 = (f32[128,128]{1,0:T(8,128)S(1)}, f32[128,128]{1,0:T(8,128)S(1)}, u32[]{:S(2)}, u32[]{:S(2)}) collective-permute-start(f32[128,128]{1,0:T(8,128)S(1)} %get-tuple-element.48.ev_own), channel_id=1, source_target_pairs={{0,1},{1,0},{2,3},{3,2},{4,5},{5,4},{6,7},{7,6},{8,9},{9,8},{10,11... | collective-permute-start | bytes 196616 | tf_op jit(solution)/shard_map/ppermute | solution.py:440
  38.2 0.0 collective-permute-start.8
  38.2 0.9 %natural.1 = f32[1,16,1024]{2,1,0:T(8,128)} custom-call(f32[8,2,8,128]{3,2,1,0:T(8,128)S(1)} %get-tuple-element.44.ends_ref), custom_call_target="tpu_custom_call" | custom-call | tf_op jit(solution)/shard_map/natural/pallas_call | solution.py:396
  39.1 2.8 %collective-permute-done.7.ev_got = f32[128,128]{1,0:T(8,128)S(1)} collective-permute-done((f32[128,128]{1,0:T(8,128)S(1)}, f32[128,128]{1,0:T(8,128)S(1)}, u32[]{:S(2)}, u32[]{:S(2)}) %collective-permute-start.7) | collective-permute-done | bytes 65568 | tf_op jit(solution)/shard_map/ppermute | solution.py:440
  42.0 1.4 %collective-permute-done.8.od_got = f32[128,128]{1,0:T(8,128)S(1)} collective-permute-done((f32[128,128]{1,0:T(8,128)S(1)}, f32[128,128]{1,0:T(8,128)S(1)}, u32[]{:S(2)}, u32[]{:S(2)}) %collective-permute-start.8) | collective-permute-done | bytes 65568 | tf_op jit(solution)/shard_map/ppermute | solution.py:440
  43.4 1.0 %join.1 = f32[16,1024]{1,0:T(8,128)} custom-call(f32[128,128]{1,0:T(8,128)S(1)} %get-tuple-element.45.g_right, f32[128,128]{1,0:T(8,128)S(1)} %get-tuple-element.48.ev_own, f32[128,128]{1,0:T(8,128)S(1)} %get-tuple-element.49.od_own, f32[128,128]{1,0:T(8,128)S(1)} %collective-permute-done.7.ev_got, f32[128,128]{1,0:T(8,128)S(1)} %collective-permute-done.8.od_got), custom_call_target="tpu_custom_call" | custom-call | tf_op jit(solution)/shard_map/join/pallas_call | solution.py:396
Async XLA Ops:
  6.4 4.3 %collective-permute-start.1 = (f32[128,128]{1,0:T(8,128)S(1)}, f32[128,128]{1,0:T(8,128)S(1)}, u32[]{:S(2)}, u32[]{:S(2)}) collective-permute-start(f32[128,128]{1,0:T(8,128)S(1)} %get-tuple-element.40.ev_own), channel_id=1, source_target_pairs={{0,1},{1,0},{2,3},{3,2},{4,5},{5,4},{6,7},{7,6},{8,9},{9,8},{10,11... | collective-permute-start | bytes 196616 | tf_op jit(solution)/shard_map/ppermute | solution.py:440
  8.0 5.2 %collective-permute-start.2 = (f32[128,128]{1,0:T(8,128)S(1)}, f32[128,128]{1,0:T(8,128)S(1)}, u32[]{:S(2)}, u32[]{:S(2)}) collective-permute-start(f32[128,128]{1,0:T(8,128)S(1)} %get-tuple-element.41.od_own), channel_id=1, source_target_pairs={{0,8},{1,2},{2,1},{3,4},{4,3},{5,6},{6,5},{7,15},{8,0},{9,10},{10,... | collective-permute-start | bytes 196616 | tf_op jit(solution)/shard_map/ppermute | solution.py:440
  8.0 9.8 %collective-permute-start = (f32[8,2,8,128]{3,2,1,0:T(8,128)S(1)}, f32[8,2,8,128]{3,2,1,0:T(8,128)S(1)}, u32[]{:S(2)}, u32[]{:S(2)}) collective-permute-start(f32[8,2,8,128]{3,2,1,0:T(8,128)S(1)} %get-tuple-element.33), channel_id=1, source_target_pairs={{0,8},{8,16},{16,24},{24,0},{1,9},{9,17},{17,25},{25,1},{2,10},{10... | collective-permute-start | bytes 196616 | tf_op jit(solution)/shard_map/ppermute | solution.py:446
  17.2 4.4 %collective-permute-start.3 = (f32[128,128]{1,0:T(8,128)S(1)}, f32[128,128]{1,0:T(8,128)S(1)}, u32[]{:S(2)}, u32[]{:S(2)}) collective-permute-start(f32[128,128]{1,0:T(8,128)S(1)} %get-tuple-element.42.refs_7_), channel_id=1, source_target_pairs={{0,1},{1,0},{2,3},{3,2},{4,5},{5,4},{6,7},{7,6},{8,9},{9,8},{10,11... | collective-permute-start | bytes 196616 | tf_op jit(solution)/shard_map/ppermute | solution.py:440
  17.7 5.2 %collective-permute-start.4 = (f32[128,128]{1,0:T(8,128)S(1)}, f32[128,128]{1,0:T(8,128)S(1)}, u32[]{:S(2)}, u32[]{:S(2)}) collective-permute-start(f32[128,128]{1,0:T(8,128)S(1)} %get-tuple-element.43.refs_8_), channel_id=1, source_target_pairs={{0,8},{1,2},{2,1},{3,4},{4,3},{5,6},{6,5},{7,15},{8,0},{9,10},{10,... | collective-permute-start | bytes 196616 | tf_op jit(solution)/shard_map/ppermute | solution.py:440
  26.8 4.3 %collective-permute-start.5 = (f32[128,128]{1,0:T(8,128)S(1)}, f32[128,128]{1,0:T(8,128)S(1)}, u32[]{:S(2)}, u32[]{:S(2)}) collective-permute-start(f32[128,128]{1,0:T(8,128)S(1)} %get-tuple-element.46.ev_own), channel_id=1, source_target_pairs={{0,1},{1,0},{2,3},{3,2},{4,5},{5,4},{6,7},{7,6},{8,9},{9,8},{10,11... | collective-permute-start | bytes 196616 | tf_op jit(solution)/shard_map/ppermute | solution.py:440
  28.4 5.2 %collective-permute-start.6 = (f32[128,128]{1,0:T(8,128)S(1)}, f32[128,128]{1,0:T(8,128)S(1)}, u32[]{:S(2)}, u32[]{:S(2)}) collective-permute-start(f32[128,128]{1,0:T(8,128)S(1)} %get-tuple-element.47.od_own), channel_id=1, source_target_pairs={{0,8},{1,2},{2,1},{3,4},{4,3},{5,6},{6,5},{7,15},{8,0},{9,10},{10,... | collective-permute-start | bytes 196616 | tf_op jit(solution)/shard_map/ppermute | solution.py:440
  37.6 4.3 %collective-permute-start.7 = (f32[128,128]{1,0:T(8,128)S(1)}, f32[128,128]{1,0:T(8,128)S(1)}, u32[]{:S(2)}, u32[]{:S(2)}) collective-permute-start(f32[128,128]{1,0:T(8,128)S(1)} %get-tuple-element.48.ev_own), channel_id=1, source_target_pairs={{0,1},{1,0},{2,3},{3,2},{4,5},{5,4},{6,7},{7,6},{8,9},{9,8},{10,11... | collective-permute-start | bytes 196616 | tf_op jit(solution)/shard_map/ppermute | solution.py:440
  38.2 5.2 %collective-permute-start.8 = (f32[128,128]{1,0:T(8,128)S(1)}, f32[128,128]{1,0:T(8,128)S(1)}, u32[]{:S(2)}, u32[]{:S(2)}) collective-permute-start(f32[128,128]{1,0:T(8,128)S(1)} %get-tuple-element.49.od_own), channel_id=1, source_target_pairs={{0,8},{1,2},{2,1},{3,4},{4,3},{5,6},{6,5},{7,15},{8,0},{9,10},{10,... | collective-permute-start | bytes 196616 | tf_op jit(solution)/shard_map/ppermute | solution.py:440

commit v8 on v7

--- a/solution.py
+++ b/solution.py
@@ -205,8 +205,9 @@
     if not neumann:
         put(r_out, COIL_E, [coil_ref[r, 0] * rec_e[r] for r in span])
         put(r_out, COIL_O, [coil_ref[r, 1] * rec_o[r] for r in span])
-    put(r_out, FACE_E, [jnp.where((sub == 0) & has_left, rec_e[r], 0.0) for r in span])
-    put(r_out, FACE_O, [jnp.where((sub == SUB - 1) & has_right, rec_o[r], 0.0) for r in span])
+    for r in span:
+        r_out[r - LOW, FACE_E] = jnp.where((sub == 0) & has_left, rec_e[r], 0.0)
+        r_out[r - LOW, FACE_O] = jnp.where((sub == SUB - 1) & has_right, rec_o[r], 0.0)
     for r in range(BLOCK):
         if not neumann:
             scale_out[r, 0] = scale_e[r]
@@ -222,27 +223,50 @@
 
 
 def advance(field_e, field_o, rhs, c_ref):
+    def updated(now, r, e, zero=None):
+        i = r - LOW
+        if e == 0:
+            up = now[r + 1, 0] if unit_up(r) else c_ref[i, UP_E] * now[r + 1, 0]
+            dn = now[r - 1, 0] if unit_down(r) else c_ref[i, DN_E] * now[r - 1, 0]
+            mid = now[r, 1]
+            beside = mid + c_ref[i, Q_E] * prev_sub(mid)
+        else:
+            up = c_ref[i, UP_O] * now[r + 1, 1]
+            dn = c_ref[i, DN_O] * now[r - 1, 1]
+            mid = now[r, 0]
+            beside = c_ref[i, P_O] * mid + c_ref[i, Q_O] * next_sub(mid)
+        soon, late = (dn, up) if 2 * r >= BLOCK else (up, dn)
+        b = rhs[r][e] if zero is None else rhs[r][e] + zero
+        return ((b + soon) + beside) + late
+
+    field = {(r, 0): v for r, v in field_e.items()}
+    field.update({(r, 1): v for r, v in field_o.items()})
+    chains = [{k: v for k, v in field.items() if sum(k) % 2 == c} for c in range(2)]
     for turn in range(JACOBI // DEPTH):
-        if turn == 0:
-            now_e, now_o = field_e, field_o
-        else:
-            now_e, now_o = haloed(now_e), haloed(now_o)
-        for k in range(1, DEPTH + 1):
-            new_e, new_o = {}, {}
-            for r in range(k - DEPTH, BLOCK + DEPTH - k):
-                i = r - LOW
-                up_e = now_e[r + 1] if unit_up(r) else c_ref[i, UP_E] * now_e[r + 1]
-                dn_e = now_e[r - 1] if unit_down(r) else c_ref[i, DN_E] * now_e[r - 1]
-                up_o = c_ref[i, UP_O] * now_o[r + 1]
-                dn_o = c_ref[i, DN_O] * now_o[r - 1]
-                soon_e, late_e = (dn_e, up_e) if 2 * r >= BLOCK else (up_e, dn_e)
-                soon_o, late_o = (dn_o, up_o) if 2 * r >= BLOCK else (up_o, dn_o)
-                beside_e = now_o[r] + c_ref[i, Q_E] * prev_sub(now_o[r])
-                beside_o = c_ref[i, P_O] * now_e[r] + c_ref[i, Q_O] * next_sub(now_e[r])
-                new_e[r] = ((rhs[r][0] + soon_e) + beside_e) + late_e
-                new_o[r] = ((rhs[r][1] + soon_o) + beside_o) + late_o
-            now_e, now_o = new_e, new_o
-    return now_e, now_o
+        for c in range(2):
+            now = chains[c]
+            if turn:
+                wide = {}
+                for (r, e), v in now.items():
+                    wide[r, e] = v
+                    if r >= BLOCK - DEPTH:
+                        wide[r - BLOCK, e] = prev_lane(v)
+                    if r < DEPTH:
+                        wide[r + BLOCK, e] = next_lane(v)
+                now = wide
+            zero = jnp.minimum(jnp.maximum(ahead, 0.0), 0.0) if c == 1 and turn == 0 else None
+            for k in range(1, DEPTH + 1):
+                colour = (c + turn * DEPTH + k) % 2
+                new = {}
+                for r in range(k - DEPTH, BLOCK + DEPTH - k):
+                    e = (r + colour) % 2
+                    on_halo = k == 1 and not 0 <= r < BLOCK
+                    new[r, e] = updated(now, r, e, zero if on_halo else None)
+                now = new
+            chains[c] = now
+            ahead = next(v for (r, _), v in now.items() if r == BLOCK - 1)
+    done = {**chains[0], **chains[1]}
+    return {r: done[r, 0] for r in range(BLOCK)}, {r: done[r, 1] for r in range(BLOCK)}
 
 
 def haloed(rows):

time: 44.5 us -> 43.6 us (0.980)
  Pallas kernels: 19.8 us -> 19 us
    pallas_call x8, Pallas kernels: 19.8 us -> 19 us  [call(): pl.pallas_call(kernel, out_shape=shapes, in_specs=[pl.BlockSpec(memory_sp...]
  transfers between devices with their start and end apart: 9 -> 9, of which waited for: 8 -> 8; matrix products, arithmetic and copies ran while one was open for 0% -> 0% of each run, Pallas kernels for 12% -> 11%
where the time goes in v8:
time: 43.6 us; the launch traced here: 43.5 us
  waiting for transfers between devices  19.5 us (45%)
  Pallas kernels  19 us (44%)
  starting transfers between devices  4.33 us (10%)
  between operations  0.67 us (2%)
    pallas_call x8, Pallas kernels, call(): pl.pallas_call(kernel, out_shape=shapes, in_specs=[pl.BlockSpec(memory_sp...  19 us
    ppermute x4, waiting for transfers between devices, swapped(): lax.ppermute(ev, 'space', even_faces)  11.9 us
    ppermute x4, waiting for transfers between devices, swapped(): lax.ppermute(od, ('tm', 'space'), odd_faces)  7.57 us
    ppermute x4, starting transfers between devices, swapped(): lax.ppermute(ev, 'space', even_faces)  4.31 us
  transfers between devices with their start and end apart: 9, of which 8 were waited for; matrix products, arithmetic and copies ran while one was open for 0% of the time, Pallas kernels for 11%

profile of v8, /device:TPU:8, one launch (start us, length us, event | category | flops | bytes accessed | tf_op | source)
XLA Modules:
  0.0 43.5 jit_solution(3830580597290249376)
XLA Ops:
  0.6 1.9 %first.1 = (f32[8,2,8,128]{3,2,1,0:T(8,128)S(1)}, f32[8,2,8,128]{3,2,1,0:T(8,128)S(1)}, f32[8,2,8,128]{3,2,1,0:T(8,128)S(1)}, f32[14,7,8,128]{3,2,1,0:T(8,128)S(...) custom-call(s32[16,1024]{1,0:T(8,128)} %labels_hbm.1, ...), custom_call_target="tpu_custom_call" | custom-call | tf_op jit(solution)/shard_map/first/pallas_call | solution.py:420
  2.6 3.6 %dir0.1 = (f32[8,2,8,128]{3,2,1,0:T(8,128)S(1)}, f32[128,128]{1,0:T(8,128)S(1)}, f32[128,128]{1,0:T(8,128)S(1)}) custom-call(f32[8,2,8,128]{3,2,1,0:T(8,128)S(1)} %get-tuple-element.26.refs_0_, f32[14,7,8,128]{3,2,1,0:T(8,128)S(1)} %get-tuple-element.27.refs_1_, f32[14,2,8,128]{3,2,1,0:T(8,128)S(1)} %get-tuple-element.28.refs_2_, ...), custom_call_target="tpu_custom_call" | custom-call | tf_op jit(solution)/shard_map/dir0/pallas_call | solution.py:420
  6.2 1.6 %collective-permute-start.1 = (f32[128,128]{1,0:T(8,128)S(1)}, f32[128,128]{1,0:T(8,128)S(1)}, u32[]{:S(2)}, u32[]{:S(2)}) collective-permute-start(f32[128,128]{1,0:T(8,128)S(1)} %get-tuple-element.40.ev_own), channel_id=1, source_target_pairs={{0,1},{1,0},{2,3},{3,2},{4,5},{5,4},{6,7},{7,6},{8,9},{9,8},{10,11... | collective-permute-start | bytes 196616 | tf_op jit(solution)/shard_map/ppermute | solution.py:464
  7.8 0.0 collective-permute-start.2
  7.8 0.0 collective-permute-start
  7.8 0.2 coef_neu.1
  8.0 2.5 %collective-permute-done.1.ev_got = f32[128,128]{1,0:T(8,128)S(1)} collective-permute-done((f32[128,128]{1,0:T(8,128)S(1)}, f32[128,128]{1,0:T(8,128)S(1)}, u32[]{:S(2)}, u32[]{:S(2)}) %collective-permute-start.1) | collective-permute-done | bytes 65568 | tf_op jit(solution)/shard_map/ppermute | solution.py:464
  10.5 2.4 %collective-permute-done.2.od_got = f32[128,128]{1,0:T(8,128)S(1)} collective-permute-done((f32[128,128]{1,0:T(8,128)S(1)}, f32[128,128]{1,0:T(8,128)S(1)}, u32[]{:S(2)}, u32[]{:S(2)}) %collective-permute-start.2) | collective-permute-done | bytes 65568 | tf_op jit(solution)/shard_map/ppermute | solution.py:464
  12.9 3.8 %neu.2 = (f32[128,128]{1,0:T(8,128)S(1)}, f32[128,128]{1,0:T(8,128)S(1)}) custom-call(f32[14,7,8,128]{3,2,1,0:T(8,128)S(1)} %get-tuple-element.36.c_ref, f32[14,2,8,128]{3,2,1,0:T(8,128)S(1)} %get-tuple-element.37.s_ref, f32[14,4,8,128]{3,2,1,0:T(8,128)S(1)} %get-tuple-element.38.r_ref, f32[4,8,128]{2,1,0:T(8,128)S(1)} %get-tuple-element.39.edge_ref, ...), custom_call_target="tpu_custom_call" | custom-call | tf_op jit(solution)/shard_map/neu/pallas_call | solution.py:420
  16.8 0.6 %collective-permute-start.3 = (f32[128,128]{1,0:T(8,128)S(1)}, f32[128,128]{1,0:T(8,128)S(1)}, u32[]{:S(2)}, u32[]{:S(2)}) collective-permute-start(f32[128,128]{1,0:T(8,128)S(1)} %get-tuple-element.42.refs_7_), channel_id=1, source_target_pairs={{0,1},{1,0},{2,3},{3,2},{4,5},{5,4},{6,7},{7,6},{8,9},{9,8},{10,11... | collective-permute-start | bytes 196616 | tf_op jit(solution)/shard_map/ppermute | solution.py:464
  17.3 0.0 collective-permute-start.4
  17.3 0.0 collective-permute-done.refs_0_
  17.3 3.8 %collective-permute-done.3.refs_9_ = f32[128,128]{1,0:T(8,128)S(1)} collective-permute-done((f32[128,128]{1,0:T(8,128)S(1)}, f32[128,128]{1,0:T(8,128)S(1)}, u32[]{:S(2)}, u32[]{:S(2)}) %collective-permute-start.3) | collective-permute-done | bytes 65568 | tf_op jit(solution)/shard_map/ppermute | solution.py:464
  21.2 1.3 %collective-permute-done.4.refs_10_ = f32[128,128]{1,0:T(8,128)S(1)} collective-permute-done((f32[128,128]{1,0:T(8,128)S(1)}, f32[128,128]{1,0:T(8,128)S(1)}, u32[]{:S(2)}, u32[]{:S(2)}) %collective-permute-start.4) | collective-permute-done | bytes 65568 | tf_op jit(solution)/shard_map/ppermute | solution.py:464
  22.5 3.7 %dir1.1 = (f32[8,2,8,128]{3,2,1,0:T(8,128)S(1)}, f32[128,128]{1,0:T(8,128)S(1)}, f32[128,128]{1,0:T(8,128)S(1)}, f32[128,128]{1,0:T(8,128)S(1)}) custom-call(f32[8,2,8,128]{3,2,1,0:T(8,128)S(1)} %collective-permute-done.refs_0_, f32[14,7,8,128]{3,2,1,0:T(8,128)S(1)} %get-tuple-element.27.refs_1_, f32[14,2,8,128]{3,2,1,0:T(8,128)S(1)} %get-tuple-element.28.refs_2_, ...), custom_call_target="tpu_custom_call" | custom-call | tf_op jit(solution)/shard_map/dir1/pallas_call | solution.py:420
  26.2 1.6 %collective-permute-start.5 = (f32[128,128]{1,0:T(8,128)S(1)}, f32[128,128]{1,0:T(8,128)S(1)}, u32[]{:S(2)}, u32[]{:S(2)}) collective-permute-start(f32[128,128]{1,0:T(8,128)S(1)} %get-tuple-element.46.ev_own), channel_id=1, source_target_pairs={{0,1},{1,0},{2,3},{3,2},{4,5},{5,4},{6,7},{7,6},{8,9},{9,8},{10,11... | collective-permute-start | bytes 196616 | tf_op jit(solution)/shard_map/ppermute | solution.py:464
  27.8 0.0 collective-permute-start.6
  27.8 2.7 %collective-permute-done.5.ev_got = f32[128,128]{1,0:T(8,128)S(1)} collective-permute-done((f32[128,128]{1,0:T(8,128)S(1)}, f32[128,128]{1,0:T(8,128)S(1)}, u32[]{:S(2)}, u32[]{:S(2)}) %collective-permute-start.5) | collective-permute-done | bytes 65568 | tf_op jit(solution)/shard_map/ppermute | solution.py:464
  30.5 2.4 %collective-permute-done.6.od_got = f32[128,128]{1,0:T(8,128)S(1)} collective-permute-done((f32[128,128]{1,0:T(8,128)S(1)}, f32[128,128]{1,0:T(8,128)S(1)}, u32[]{:S(2)}, u32[]{:S(2)}) %collective-permute-start.6) | collective-permute-done | bytes 65568 | tf_op jit(solution)/shard_map/ppermute | solution.py:464
  32.9 3.8 %neu.3 = (f32[128,128]{1,0:T(8,128)S(1)}, f32[128,128]{1,0:T(8,128)S(1)}) custom-call(f32[14,7,8,128]{3,2,1,0:T(8,128)S(1)} %get-tuple-element.36.c_ref, f32[14,2,8,128]{3,2,1,0:T(8,128)S(1)} %get-tuple-element.37.s_ref, f32[14,4,8,128]{3,2,1,0:T(8,128)S(1)} %get-tuple-element.38.r_ref, f32[4,8,128]{2,1,0:T(8,128)S(1)} %get-tuple-element.39.edge_ref, ...), custom_call_target="tpu_custom_call" | custom-call | tf_op jit(solution)/shard_map/neu/pallas_call | solution.py:420
  36.8 0.6 %collective-permute-start.7 = (f32[128,128]{1,0:T(8,128)S(1)}, f32[128,128]{1,0:T(8,128)S(1)}, u32[]{:S(2)}, u32[]{:S(2)}) collective-permute-start(f32[128,128]{1,0:T(8,128)S(1)} %get-tuple-element.48.ev_own), channel_id=1, source_target_pairs={{0,1},{1,0},{2,3},{3,2},{4,5},{5,4},{6,7},{7,6},{8,9},{9,8},{10,11... | collective-permute-start | bytes 196616 | tf_op jit(solution)/shard_map/ppermute | solution.py:464
  37.4 0.0 collective-permute-start.8
  37.4 0.9 %natural.1 = f32[1,16,1024]{2,1,0:T(8,128)} custom-call(f32[8,2,8,128]{3,2,1,0:T(8,128)S(1)} %get-tuple-element.44.ends_ref), custom_call_target="tpu_custom_call" | custom-call | tf_op jit(solution)/shard_map/natural/pallas_call | solution.py:420
  38.3 2.8 %collective-permute-done.7.ev_got = f32[128,128]{1,0:T(8,128)S(1)} collective-permute-done((f32[128,128]{1,0:T(8,128)S(1)}, f32[128,128]{1,0:T(8,128)S(1)}, u32[]{:S(2)}, u32[]{:S(2)}) %collective-permute-start.7) | collective-permute-done | bytes 65568 | tf_op jit(solution)/shard_map/ppermute | solution.py:464
  41.1 1.4 %collective-permute-done.8.od_got = f32[128,128]{1,0:T(8,128)S(1)} collective-permute-done((f32[128,128]{1,0:T(8,128)S(1)}, f32[128,128]{1,0:T(8,128)S(1)}, u32[]{:S(2)}, u32[]{:S(2)}) %collective-permute-start.8) | collective-permute-done | bytes 65568 | tf_op jit(solution)/shard_map/ppermute | solution.py:464
  42.5 1.0 %join.1 = f32[16,1024]{1,0:T(8,128)} custom-call(f32[128,128]{1,0:T(8,128)S(1)} %get-tuple-element.45.g_right, f32[128,128]{1,0:T(8,128)S(1)} %get-tuple-element.48.ev_own, f32[128,128]{1,0:T(8,128)S(1)} %get-tuple-element.49.od_own, f32[128,128]{1,0:T(8,128)S(1)} %collective-permute-done.7.ev_got, f32[128,128]{1,0:T(8,128)S(1)} %collective-permute-done.8.od_got), custom_call_target="tpu_custom_call" | custom-call | tf_op jit(solution)/shard_map/join/pallas_call | solution.py:420
Async XLA Ops:
  6.2 4.3 %collective-permute-start.1 = (f32[128,128]{1,0:T(8,128)S(1)}, f32[128,128]{1,0:T(8,128)S(1)}, u32[]{:S(2)}, u32[]{:S(2)}) collective-permute-start(f32[128,128]{1,0:T(8,128)S(1)} %get-tuple-element.40.ev_own), channel_id=1, source_target_pairs={{0,1},{1,0},{2,3},{3,2},{4,5},{5,4},{6,7},{7,6},{8,9},{9,8},{10,11... | collective-permute-start | bytes 196616 | tf_op jit(solution)/shard_map/ppermute | solution.py:464
  7.8 5.2 %collective-permute-start.2 = (f32[128,128]{1,0:T(8,128)S(1)}, f32[128,128]{1,0:T(8,128)S(1)}, u32[]{:S(2)}, u32[]{:S(2)}) collective-permute-start(f32[128,128]{1,0:T(8,128)S(1)} %get-tuple-element.41.od_own), channel_id=1, source_target_pairs={{0,8},{1,2},{2,1},{3,4},{4,3},{5,6},{6,5},{7,15},{8,0},{9,10},{10,... | collective-permute-start | bytes 196616 | tf_op jit(solution)/shard_map/ppermute | solution.py:464
  7.8 9.6 %collective-permute-start = (f32[8,2,8,128]{3,2,1,0:T(8,128)S(1)}, f32[8,2,8,128]{3,2,1,0:T(8,128)S(1)}, u32[]{:S(2)}, u32[]{:S(2)}) collective-permute-start(f32[8,2,8,128]{3,2,1,0:T(8,128)S(1)} %get-tuple-element.33), channel_id=1, source_target_pairs={{0,8},{8,16},{16,24},{24,0},{1,9},{9,17},{17,25},{25,1},{2,10},{10... | collective-permute-start | bytes 196616 | tf_op jit(solution)/shard_map/ppermute | solution.py:470
  16.8 4.4 %collective-permute-start.3 = (f32[128,128]{1,0:T(8,128)S(1)}, f32[128,128]{1,0:T(8,128)S(1)}, u32[]{:S(2)}, u32[]{:S(2)}) collective-permute-start(f32[128,128]{1,0:T(8,128)S(1)} %get-tuple-element.42.refs_7_), channel_id=1, source_target_pairs={{0,1},{1,0},{2,3},{3,2},{4,5},{5,4},{6,7},{7,6},{8,9},{9,8},{10,11... | collective-permute-start | bytes 196616 | tf_op jit(solution)/shard_map/ppermute | solution.py:464
  17.3 5.2 %collective-permute-start.4 = (f32[128,128]{1,0:T(8,128)S(1)}, f32[128,128]{1,0:T(8,128)S(1)}, u32[]{:S(2)}, u32[]{:S(2)}) collective-permute-start(f32[128,128]{1,0:T(8,128)S(1)} %get-tuple-element.43.refs_8_), channel_id=1, source_target_pairs={{0,8},{1,2},{2,1},{3,4},{4,3},{5,6},{6,5},{7,15},{8,0},{9,10},{10,... | collective-permute-start | bytes 196616 | tf_op jit(solution)/shard_map/ppermute | solution.py:464
  26.2 4.3 %collective-permute-start.5 = (f32[128,128]{1,0:T(8,128)S(1)}, f32[128,128]{1,0:T(8,128)S(1)}, u32[]{:S(2)}, u32[]{:S(2)}) collective-permute-start(f32[128,128]{1,0:T(8,128)S(1)} %get-tuple-element.46.ev_own), channel_id=1, source_target_pairs={{0,1},{1,0},{2,3},{3,2},{4,5},{5,4},{6,7},{7,6},{8,9},{9,8},{10,11... | collective-permute-start | bytes 196616 | tf_op jit(solution)/shard_map/ppermute | solution.py:464
  27.8 5.2 %collective-permute-start.6 = (f32[128,128]{1,0:T(8,128)S(1)}, f32[128,128]{1,0:T(8,128)S(1)}, u32[]{:S(2)}, u32[]{:S(2)}) collective-permute-start(f32[128,128]{1,0:T(8,128)S(1)} %get-tuple-element.47.od_own), channel_id=1, source_target_pairs={{0,8},{1,2},{2,1},{3,4},{4,3},{5,6},{6,5},{7,15},{8,0},{9,10},{10,... | collective-permute-start | bytes 196616 | tf_op jit(solution)/shard_map/ppermute | solution.py:464
  36.8 4.3 %collective-permute-start.7 = (f32[128,128]{1,0:T(8,128)S(1)}, f32[128,128]{1,0:T(8,128)S(1)}, u32[]{:S(2)}, u32[]{:S(2)}) collective-permute-start(f32[128,128]{1,0:T(8,128)S(1)} %get-tuple-element.48.ev_own), channel_id=1, source_target_pairs={{0,1},{1,0},{2,3},{3,2},{4,5},{5,4},{6,7},{7,6},{8,9},{9,8},{10,11... | collective-permute-start | bytes 196616 | tf_op jit(solution)/shard_map/ppermute | solution.py:464
  37.4 5.2 %collective-permute-start.8 = (f32[128,128]{1,0:T(8,128)S(1)}, f32[128,128]{1,0:T(8,128)S(1)}, u32[]{:S(2)}, u32[]{:S(2)}) collective-permute-start(f32[128,128]{1,0:T(8,128)S(1)} %get-tuple-element.49.od_own), channel_id=1, source_target_pairs={{0,8},{1,2},{2,1},{3,4},{4,3},{5,6},{6,5},{7,15},{8,0},{9,10},{10,... | collective-permute-start | bytes 196616 | tf_op jit(solution)/shard_map/ppermute | solution.py:464

commit v9 on v8

--- a/solution.py
+++ b/solution.py
@@ -21,7 +21,7 @@
 Q_E, P_O, Q_O, UP_O, DN_O, UP_E, DN_E = range(7)
 COIL_E, COIL_O, FACE_E, FACE_O = range(4)
 F32 = jnp.float32
-UNROLL = 4
+UNROLL = 8
 
 
 def tile_index(axis):

time: 43.6 us -> 43.4 us (level)
  no operation moved by 1% of the time
where the time goes in v9:
time: 43.4 us; the launch traced here: 43.3 us
  waiting for transfers between devices  19.5 us (45%)
  Pallas kernels  18.8 us (43%)
  starting transfers between devices  4.33 us (10%)
  between operations  0.67 us (2%)
    pallas_call x8, Pallas kernels, call(): pl.pallas_call(kernel, out_shape=shapes, in_specs=[pl.BlockSpec(memory_sp...  18.8 us
    ppermute x4, waiting for transfers between devices, swapped(): lax.ppermute(ev, 'space', even_faces)  11.9 us
    ppermute x4, waiting for transfers between devices, swapped(): lax.ppermute(od, ('tm', 'space'), odd_faces)  7.57 us
    ppermute x4, starting transfers between devices, swapped(): lax.ppermute(ev, 'space', even_faces)  4.31 us
  transfers between devices with their start and end apart: 9, of which 8 were waited for; matrix products, arithmetic and copies ran while one was open for 0% of the time, Pallas kernels for 11%

profile of v9, /device:TPU:8, one launch (start us, length us, event | category | flops | bytes accessed | tf_op | source)
XLA Modules:
  0.0 43.3 jit_solution(10000454845881883298)
XLA Ops:
  0.6 1.9 %first.1 = (f32[8,2,8,128]{3,2,1,0:T(8,128)S(1)}, f32[8,2,8,128]{3,2,1,0:T(8,128)S(1)}, f32[8,2,8,128]{3,2,1,0:T(8,128)S(1)}, f32[14,7,8,128]{3,2,1,0:T(8,128)S(...) custom-call(s32[16,1024]{1,0:T(8,128)} %labels_hbm.1, ...), custom_call_target="tpu_custom_call" | custom-call | tf_op jit(solution)/shard_map/first/pallas_call | solution.py:420
  2.6 3.5 %dir0.1 = (f32[8,2,8,128]{3,2,1,0:T(8,128)S(1)}, f32[128,128]{1,0:T(8,128)S(1)}, f32[128,128]{1,0:T(8,128)S(1)}) custom-call(f32[8,2,8,128]{3,2,1,0:T(8,128)S(1)} %get-tuple-element.26.refs_0_, f32[14,7,8,128]{3,2,1,0:T(8,128)S(1)} %get-tuple-element.27.refs_1_, f32[14,2,8,128]{3,2,1,0:T(8,128)S(1)} %get-tuple-element.28.refs_2_, ...), custom_call_target="tpu_custom_call" | custom-call | tf_op jit(solution)/shard_map/dir0/pallas_call | solution.py:420
  6.1 1.6 %collective-permute-start.1 = (f32[128,128]{1,0:T(8,128)S(1)}, f32[128,128]{1,0:T(8,128)S(1)}, u32[]{:S(2)}, u32[]{:S(2)}) collective-permute-start(f32[128,128]{1,0:T(8,128)S(1)} %get-tuple-element.40.ev_own), channel_id=1, source_target_pairs={{0,1},{1,0},{2,3},{3,2},{4,5},{5,4},{6,7},{7,6},{8,9},{9,8},{10,11... | collective-permute-start | bytes 196616 | tf_op jit(solution)/shard_map/ppermute | solution.py:464
  7.7 0.0 collective-permute-start.2
  7.7 0.0 collective-permute-start
  7.7 0.2 coef_neu.1
  7.9 2.5 %collective-permute-done.1.ev_got = f32[128,128]{1,0:T(8,128)S(1)} collective-permute-done((f32[128,128]{1,0:T(8,128)S(1)}, f32[128,128]{1,0:T(8,128)S(1)}, u32[]{:S(2)}, u32[]{:S(2)}) %collective-permute-start.1) | collective-permute-done | bytes 65568 | tf_op jit(solution)/shard_map/ppermute | solution.py:464
  10.4 2.4 %collective-permute-done.2.od_got = f32[128,128]{1,0:T(8,128)S(1)} collective-permute-done((f32[128,128]{1,0:T(8,128)S(1)}, f32[128,128]{1,0:T(8,128)S(1)}, u32[]{:S(2)}, u32[]{:S(2)}) %collective-permute-start.2) | collective-permute-done | bytes 65568 | tf_op jit(solution)/shard_map/ppermute | solution.py:464
  12.9 3.8 %neu.2 = (f32[128,128]{1,0:T(8,128)S(1)}, f32[128,128]{1,0:T(8,128)S(1)}) custom-call(f32[14,7,8,128]{3,2,1,0:T(8,128)S(1)} %get-tuple-element.36.c_ref, f32[14,2,8,128]{3,2,1,0:T(8,128)S(1)} %get-tuple-element.37.s_ref, f32[14,4,8,128]{3,2,1,0:T(8,128)S(1)} %get-tuple-element.38.r_ref, f32[4,8,128]{2,1,0:T(8,128)S(1)} %get-tuple-element.39.edge_ref, ...), custom_call_target="tpu_custom_call" | custom-call | tf_op jit(solution)/shard_map/neu/pallas_call | solution.py:420
  16.7 0.6 %collective-permute-start.3 = (f32[128,128]{1,0:T(8,128)S(1)}, f32[128,128]{1,0:T(8,128)S(1)}, u32[]{:S(2)}, u32[]{:S(2)}) collective-permute-start(f32[128,128]{1,0:T(8,128)S(1)} %get-tuple-element.42.refs_7_), channel_id=1, source_target_pairs={{0,1},{1,0},{2,3},{3,2},{4,5},{5,4},{6,7},{7,6},{8,9},{9,8},{10,11... | collective-permute-start | bytes 196616 | tf_op jit(solution)/shard_map/ppermute | solution.py:464
  17.2 0.0 collective-permute-start.4
  17.2 0.0 collective-permute-done.refs_0_
  17.2 3.8 %collective-permute-done.3.refs_9_ = f32[128,128]{1,0:T(8,128)S(1)} collective-permute-done((f32[128,128]{1,0:T(8,128)S(1)}, f32[128,128]{1,0:T(8,128)S(1)}, u32[]{:S(2)}, u32[]{:S(2)}) %collective-permute-start.3) | collective-permute-done | bytes 65568 | tf_op jit(solution)/shard_map/ppermute | solution.py:464
  21.1 1.3 %collective-permute-done.4.refs_10_ = f32[128,128]{1,0:T(8,128)S(1)} collective-permute-done((f32[128,128]{1,0:T(8,128)S(1)}, f32[128,128]{1,0:T(8,128)S(1)}, u32[]{:S(2)}, u32[]{:S(2)}) %collective-permute-start.4) | collective-permute-done | bytes 65568 | tf_op jit(solution)/shard_map/ppermute | solution.py:464
  22.4 3.7 %dir1.1 = (f32[8,2,8,128]{3,2,1,0:T(8,128)S(1)}, f32[128,128]{1,0:T(8,128)S(1)}, f32[128,128]{1,0:T(8,128)S(1)}, f32[128,128]{1,0:T(8,128)S(1)}) custom-call(f32[8,2,8,128]{3,2,1,0:T(8,128)S(1)} %collective-permute-done.refs_0_, f32[14,7,8,128]{3,2,1,0:T(8,128)S(1)} %get-tuple-element.27.refs_1_, f32[14,2,8,128]{3,2,1,0:T(8,128)S(1)} %get-tuple-element.28.refs_2_, ...), custom_call_target="tpu_custom_call" | custom-call | tf_op jit(solution)/shard_map/dir1/pallas_call | solution.py:420
  26.1 1.6 %collective-permute-start.5 = (f32[128,128]{1,0:T(8,128)S(1)}, f32[128,128]{1,0:T(8,128)S(1)}, u32[]{:S(2)}, u32[]{:S(2)}) collective-permute-start(f32[128,128]{1,0:T(8,128)S(1)} %get-tuple-element.46.ev_own), channel_id=1, source_target_pairs={{0,1},{1,0},{2,3},{3,2},{4,5},{5,4},{6,7},{7,6},{8,9},{9,8},{10,11... | collective-permute-start | bytes 196616 | tf_op jit(solution)/shard_map/ppermute | solution.py:464
  27.6 0.0 collective-permute-start.6
  27.6 2.7 %collective-permute-done.5.ev_got = f32[128,128]{1,0:T(8,128)S(1)} collective-permute-done((f32[128,128]{1,0:T(8,128)S(1)}, f32[128,128]{1,0:T(8,128)S(1)}, u32[]{:S(2)}, u32[]{:S(2)}) %collective-permute-start.5) | collective-permute-done | bytes 65568 | tf_op jit(solution)/shard_map/ppermute | solution.py:464
  30.4 2.4 %collective-permute-done.6.od_got = f32[128,128]{1,0:T(8,128)S(1)} collective-permute-done((f32[128,128]{1,0:T(8,128)S(1)}, f32[128,128]{1,0:T(8,128)S(1)}, u32[]{:S(2)}, u32[]{:S(2)}) %collective-permute-start.6) | collective-permute-done | bytes 65568 | tf_op jit(solution)/shard_map/ppermute | solution.py:464
  32.8 3.8 %neu.3 = (f32[128,128]{1,0:T(8,128)S(1)}, f32[128,128]{1,0:T(8,128)S(1)}) custom-call(f32[14,7,8,128]{3,2,1,0:T(8,128)S(1)} %get-tuple-element.36.c_ref, f32[14,2,8,128]{3,2,1,0:T(8,128)S(1)} %get-tuple-element.37.s_ref, f32[14,4,8,128]{3,2,1,0:T(8,128)S(1)} %get-tuple-element.38.r_ref, f32[4,8,128]{2,1,0:T(8,128)S(1)} %get-tuple-element.39.edge_ref, ...), custom_call_target="tpu_custom_call" | custom-call | tf_op jit(solution)/shard_map/neu/pallas_call | solution.py:420
  36.6 0.6 %collective-permute-start.7 = (f32[128,128]{1,0:T(8,128)S(1)}, f32[128,128]{1,0:T(8,128)S(1)}, u32[]{:S(2)}, u32[]{:S(2)}) collective-permute-start(f32[128,128]{1,0:T(8,128)S(1)} %get-tuple-element.48.ev_own), channel_id=1, source_target_pairs={{0,1},{1,0},{2,3},{3,2},{4,5},{5,4},{6,7},{7,6},{8,9},{9,8},{10,11... | collective-permute-start | bytes 196616 | tf_op jit(solution)/shard_map/ppermute | solution.py:464
  37.2 0.0 collective-permute-start.8
  37.2 0.9 %natural.1 = f32[1,16,1024]{2,1,0:T(8,128)} custom-call(f32[8,2,8,128]{3,2,1,0:T(8,128)S(1)} %get-tuple-element.44.ends_ref), custom_call_target="tpu_custom_call" | custom-call | tf_op jit(solution)/shard_map/natural/pallas_call | solution.py:420
  38.1 2.8 %collective-permute-done.7.ev_got = f32[128,128]{1,0:T(8,128)S(1)} collective-permute-done((f32[128,128]{1,0:T(8,128)S(1)}, f32[128,128]{1,0:T(8,128)S(1)}, u32[]{:S(2)}, u32[]{:S(2)}) %collective-permute-start.7) | collective-permute-done | bytes 65568 | tf_op jit(solution)/shard_map/ppermute | solution.py:464
  40.9 1.4 %collective-permute-done.8.od_got = f32[128,128]{1,0:T(8,128)S(1)} collective-permute-done((f32[128,128]{1,0:T(8,128)S(1)}, f32[128,128]{1,0:T(8,128)S(1)}, u32[]{:S(2)}, u32[]{:S(2)}) %collective-permute-start.8) | collective-permute-done | bytes 65568 | tf_op jit(solution)/shard_map/ppermute | solution.py:464
  42.3 1.0 %join.1 = f32[16,1024]{1,0:T(8,128)} custom-call(f32[128,128]{1,0:T(8,128)S(1)} %get-tuple-element.45.g_right, f32[128,128]{1,0:T(8,128)S(1)} %get-tuple-element.48.ev_own, f32[128,128]{1,0:T(8,128)S(1)} %get-tuple-element.49.od_own, f32[128,128]{1,0:T(8,128)S(1)} %collective-permute-done.7.ev_got, f32[128,128]{1,0:T(8,128)S(1)} %collective-permute-done.8.od_got), custom_call_target="tpu_custom_call" | custom-call | tf_op jit(solution)/shard_map/join/pallas_call | solution.py:420
Async XLA Ops:
  6.1 4.3 %collective-permute-start.1 = (f32[128,128]{1,0:T(8,128)S(1)}, f32[128,128]{1,0:T(8,128)S(1)}, u32[]{:S(2)}, u32[]{:S(2)}) collective-permute-start(f32[128,128]{1,0:T(8,128)S(1)} %get-tuple-element.40.ev_own), channel_id=1, source_target_pairs={{0,1},{1,0},{2,3},{3,2},{4,5},{5,4},{6,7},{7,6},{8,9},{9,8},{10,11... | collective-permute-start | bytes 196616 | tf_op jit(solution)/shard_map/ppermute | solution.py:464
  7.7 5.2 %collective-permute-start.2 = (f32[128,128]{1,0:T(8,128)S(1)}, f32[128,128]{1,0:T(8,128)S(1)}, u32[]{:S(2)}, u32[]{:S(2)}) collective-permute-start(f32[128,128]{1,0:T(8,128)S(1)} %get-tuple-element.41.od_own), channel_id=1, source_target_pairs={{0,8},{1,2},{2,1},{3,4},{4,3},{5,6},{6,5},{7,15},{8,0},{9,10},{10,... | collective-permute-start | bytes 196616 | tf_op jit(solution)/shard_map/ppermute | solution.py:464
  7.7 9.5 %collective-permute-start = (f32[8,2,8,128]{3,2,1,0:T(8,128)S(1)}, f32[8,2,8,128]{3,2,1,0:T(8,128)S(1)}, u32[]{:S(2)}, u32[]{:S(2)}) collective-permute-start(f32[8,2,8,128]{3,2,1,0:T(8,128)S(1)} %get-tuple-element.33), channel_id=1, source_target_pairs={{0,8},{8,16},{16,24},{24,0},{1,9},{9,17},{17,25},{25,1},{2,10},{10... | collective-permute-start | bytes 196616 | tf_op jit(solution)/shard_map/ppermute | solution.py:470
  16.7 4.4 %collective-permute-start.3 = (f32[128,128]{1,0:T(8,128)S(1)}, f32[128,128]{1,0:T(8,128)S(1)}, u32[]{:S(2)}, u32[]{:S(2)}) collective-permute-start(f32[128,128]{1,0:T(8,128)S(1)} %get-tuple-element.42.refs_7_), channel_id=1, source_target_pairs={{0,1},{1,0},{2,3},{3,2},{4,5},{5,4},{6,7},{7,6},{8,9},{9,8},{10,11... | collective-permute-start | bytes 196616 | tf_op jit(solution)/shard_map/ppermute | solution.py:464
  17.2 5.2 %collective-permute-start.4 = (f32[128,128]{1,0:T(8,128)S(1)}, f32[128,128]{1,0:T(8,128)S(1)}, u32[]{:S(2)}, u32[]{:S(2)}) collective-permute-start(f32[128,128]{1,0:T(8,128)S(1)} %get-tuple-element.43.refs_8_), channel_id=1, source_target_pairs={{0,8},{1,2},{2,1},{3,4},{4,3},{5,6},{6,5},{7,15},{8,0},{9,10},{10,... | collective-permute-start | bytes 196616 | tf_op jit(solution)/shard_map/ppermute | solution.py:464
  26.1 4.3 %collective-permute-start.5 = (f32[128,128]{1,0:T(8,128)S(1)}, f32[128,128]{1,0:T(8,128)S(1)}, u32[]{:S(2)}, u32[]{:S(2)}) collective-permute-start(f32[128,128]{1,0:T(8,128)S(1)} %get-tuple-element.46.ev_own), channel_id=1, source_target_pairs={{0,1},{1,0},{2,3},{3,2},{4,5},{5,4},{6,7},{7,6},{8,9},{9,8},{10,11... | collective-permute-start | bytes 196616 | tf_op jit(solution)/shard_map/ppermute | solution.py:464
  27.6 5.2 %collective-permute-start.6 = (f32[128,128]{1,0:T(8,128)S(1)}, f32[128,128]{1,0:T(8,128)S(1)}, u32[]{:S(2)}, u32[]{:S(2)}) collective-permute-start(f32[128,128]{1,0:T(8,128)S(1)} %get-tuple-element.47.od_own), channel_id=1, source_target_pairs={{0,8},{1,2},{2,1},{3,4},{4,3},{5,6},{6,5},{7,15},{8,0},{9,10},{10,... | collective-permute-start | bytes 196616 | tf_op jit(solution)/shard_map/ppermute | solution.py:464
  36.6 4.3 %collective-permute-start.7 = (f32[128,128]{1,0:T(8,128)S(1)}, f32[128,128]{1,0:T(8,128)S(1)}, u32[]{:S(2)}, u32[]{:S(2)}) collective-permute-start(f32[128,128]{1,0:T(8,128)S(1)} %get-tuple-element.48.ev_own), channel_id=1, source_target_pairs={{0,1},{1,0},{2,3},{3,2},{4,5},{5,4},{6,7},{7,6},{8,9},{9,8},{10,11... | collective-permute-start | bytes 196616 | tf_op jit(solution)/shard_map/ppermute | solution.py:464
  37.2 5.2 %collective-permute-start.8 = (f32[128,128]{1,0:T(8,128)S(1)}, f32[128,128]{1,0:T(8,128)S(1)}, u32[]{:S(2)}, u32[]{:S(2)}) collective-permute-start(f32[128,128]{1,0:T(8,128)S(1)} %get-tuple-element.49.od_own), channel_id=1, source_target_pairs={{0,8},{1,2},{2,1},{3,4},{4,3},{5,6},{6,5},{7,15},{8,0},{9,10},{10,... | collective-permute-start | bytes 196616 | tf_op jit(solution)/shard_map/ppermute | solution.py:464
